TPU v7x, 32 devices: a whole 2x2x4 slice. The times are simulated.
32 devices in a mesh: fsdp: 4 (over z), ctx: 4 (over x, core), tp: 2 (over y).
Axes of the slice: x: 2, y: 2, z: 4, core: 2. Of those that a mesh axis runs over, the one named last changes fastest.
Arguments:
- hidden_in: bfloat16 [4, 3072, 1536], P('fsdp', 'ctx'), may hold values from -6 to 6
- cotangent: bfloat16 [4, 3072, 1536], P('fsdp', 'ctx'), may hold values from -6 to 6
- doc_lengths: int32 [4, 8], P('fsdp'), may hold values from 1 to 1536, 3072 in all within a row
- stripe: int32 [4, 4], P('fsdp'), may hold values from 0 to 3, each once within a row
- query_key_value_weight: bfloat16 [1536, 3072], P('fsdp', 'tp'), may hold values from -0.15625 to 0.15625
- output_weight: bfloat16 [1536, 1536], P('fsdp', 'tp'), may hold values from -0.875 to 0.875
- feedforward_weight: bfloat16 [3, 1536, 4096], P(None, 'fsdp', 'tp'), may hold values from -0.15625 to 0.15625
- gains: bfloat16 [2, 1536], P(None, 'fsdp'), may hold values from 0.099609375 to 1.8984375
Outputs:
- hidden_out: bfloat16 [4, 3072, 1536], P('fsdp', 'ctx')
- grad_in: bfloat16 [4, 3072, 1536], P('fsdp', 'ctx')
- grad_qkv: float32 [1536, 3072], P(('fsdp', 'ctx'), 'tp')
- grad_out: float32 [1536, 1536], P(('fsdp', 'ctx'), 'tp')
- grad_ffn: float32 [3, 1536, 4096], P(None, ('fsdp', 'ctx'), 'tp')
- grad_gains: float32 [2, 1536], P(None, ('fsdp', 'ctx'))
Inputs may be any that keep to these rules, and one draw needn't show every extreme that they name: `stripe`: each row holds every index of ctx once. `doc_lengths`: the lengths of a sequence sum to 3072.
All inputs are finite; a program needn't handle non-finite values.
Results may differ from a plain program's by a relative error of at most 0.023.
Values may be sent and summed in bfloat16 or wider, within the bound.
No kernel may reach another device: no remote copies, remote signals or barrier semaphores. Data moves between devices by JAX's collectives and lax.ppermute only.
A program may use at most 256 MiB of HBM per device.

v0:
```python
import jax
import jax.numpy as jnp
from jax import lax
from jax.sharding import PartitionSpec as P

HEAD_SIZE = 96
QUERY_PER_KV = 2


norm_eps = 1e-05
rope_base = 100000.0
masked_score = -1e30


def shifted(shard, axis, by):
    length = lax.axis_size(axis)
    return lax.ppermute(shard, axis, [(i, (i + by) % length) for i in range(length)])


def slot_meta(first_row, row_count, rows_per_block, stripe_row, ends, lengths):
    rows_here = first_row + jnp.arange(row_count, dtype=jnp.int32)
    owners = rows_here // rows_per_block
    ctx_count = stripe_row.shape[0]
    picked = jnp.where(
        owners[:, None] == jnp.arange(ctx_count, dtype=jnp.int32)[None, :], stripe_row[None, :], 0
    )
    packed = rows_here % rows_per_block * ctx_count + jnp.sum(picked, axis=1)
    passed = (packed[:, None] >= ends[None, :]).astype(jnp.int32)
    return (packed, jnp.sum(passed, axis=1), packed - jnp.sum(passed * lengths[None, :], axis=1))


def rope_tables(position):
    half_width = HEAD_SIZE // 2
    frequency = rope_base ** (-(2.0 * jnp.arange(half_width, dtype=jnp.float32)) / HEAD_SIZE)
    angles = position.astype(jnp.float32)[..., None] * frequency
    return (jnp.cos(angles), jnp.sin(angles))


def rotate(vector, cos_table, sin_table):
    half_width = vector.shape[-1] // 2
    front_half = vector[..., :half_width]
    back_half = vector[..., half_width:]
    return jnp.concatenate(
        [
            front_half * cos_table - back_half * sin_table,
            back_half * cos_table + front_half * sin_table,
        ],
        axis=-1,
    )


def rotate_back(grad_vec, cos_table, sin_table):
    half_width = grad_vec.shape[-1] // 2
    front_half = grad_vec[..., :half_width]
    back_half = grad_vec[..., half_width:]
    return jnp.concatenate(
        [
            front_half * cos_table + back_half * sin_table,
            back_half * cos_table - front_half * sin_table,
        ],
        axis=-1,
    )


def rms_normed(values, gain):
    scale_row = lax.rsqrt(jnp.mean(values * values, axis=-1, keepdims=True) + norm_eps)
    return (values * scale_row * gain, scale_row)


def norm_back(grad_normed, values, scale_row, gain):
    unit_rows = values * scale_row
    weighted = grad_normed * gain
    grad_values = scale_row * (
        weighted - unit_rows * jnp.mean(weighted * unit_rows, axis=-1, keepdims=True)
    )
    return (grad_values, jnp.sum(grad_normed * unit_rows, axis=0))


def on_device(
    hidden_in,
    cotangent,
    doc_lengths,
    stripe,
    query_key_value_weight,
    output_weight,
    feedforward_weight,
    gains,
):
    ctx_count = lax.axis_size("ctx")
    ctx_index = lax.axis_index("ctx")
    tok_rows = hidden_in.shape[1]
    lengths = doc_lengths[0]
    ends = jnp.cumsum(lengths)
    stripe_row = stripe[0]
    query_idx, query_seg, query_pos = slot_meta(
        ctx_index * tok_rows, tok_rows, tok_rows, stripe_row, ends, lengths
    )
    cos_table, sin_table = rope_tables(query_pos)
    wq_full, wo_full, ffn_full, gain_full = (
        lax.all_gather(query_key_value_weight, "fsdp", axis=0, tiled=True),
        lax.all_gather(output_weight, "fsdp", axis=0, tiled=True),
        lax.all_gather(feedforward_weight, "fsdp", axis=1, tiled=True),
        lax.all_gather(gains, "fsdp", axis=1, tiled=True),
    )
    gain_rows = gain_full.astype(jnp.float32)
    layer_input = hidden_in[0].astype(jnp.float32)
    first_normed, scale_one = rms_normed(layer_input, gain_rows[0])
    first_normed = first_normed.astype(jnp.bfloat16)
    kv_heads = wq_full.shape[1] // ((QUERY_PER_KV + 2) * HEAD_SIZE)
    output_projected = jnp.dot(first_normed, wq_full, preferred_element_type=jnp.float32).reshape(
        tok_rows, kv_heads, QUERY_PER_KV + 2, HEAD_SIZE
    )
    queries = rotate(
        output_projected[:, :, :QUERY_PER_KV], cos_table[:, None, None], sin_table[:, None, None]
    ).astype(jnp.bfloat16)
    keys_own = rotate(
        output_projected[:, :, QUERY_PER_KV], cos_table[:, None], sin_table[:, None]
    ).astype(jnp.bfloat16)
    values_own = output_projected[:, :, QUERY_PER_KV + 1].astype(jnp.bfloat16)
    kv_block = jnp.stack(
        [
            keys_own.reshape(tok_rows, kv_heads * HEAD_SIZE),
            values_own.reshape(tok_rows, kv_heads * HEAD_SIZE),
        ],
        axis=1,
    )
    inv_scale = HEAD_SIZE ** (-0.5)

    def block_scores(kv_piece, first_row):
        piece_rows = kv_piece.shape[0]
        key_idx, key_seg, unused = slot_meta(
            first_row, piece_rows, tok_rows, stripe_row, ends, lengths
        )
        keys_piece = kv_piece[:, 0].reshape(piece_rows, kv_heads, HEAD_SIZE)
        values_piece = kv_piece[:, 1].reshape(piece_rows, kv_heads, HEAD_SIZE)
        scores = (
            jnp.einsum("qhgd,khd->hgqk", queries, keys_piece, preferred_element_type=jnp.float32)
            * inv_scale
        )
        allowed = (query_seg[:, None] == key_seg[None, :]) & (
            key_idx[None, :] <= query_idx[:, None]
        )
        return (scores, allowed, keys_piece, values_piece)

    def merge_block(stats, kv_piece, first_row):
        row_top, row_total, accum = stats
        scores, allowed, keys_piece, values_piece = block_scores(kv_piece, first_row)
        scores = jnp.where(allowed, scores, masked_score)
        new_top = jnp.maximum(row_top, jnp.max(scores, axis=-1))
        weights = jnp.where(allowed, jnp.exp(scores - new_top[..., None]), 0.0)
        fade = jnp.exp(row_top - new_top)
        product = jnp.einsum(
            "hgqk,khd->qhgd",
            weights.astype(jnp.bfloat16),
            values_piece,
            preferred_element_type=jnp.float32,
        )
        accum = accum * jnp.transpose(fade, (2, 0, 1))[..., None] + product
        row_total = row_total * fade + jnp.sum(weights, axis=-1)
        return (new_top, row_total, accum)

    start_stats = (
        jnp.full((kv_heads, QUERY_PER_KV, tok_rows), masked_score, jnp.float32),
        jnp.zeros((kv_heads, QUERY_PER_KV, tok_rows), jnp.float32),
        jnp.zeros((tok_rows, kv_heads, QUERY_PER_KV, HEAD_SIZE), jnp.float32),
    )

    def cycle_step(cycle_pos, carry):
        moving, stats = carry
        source = (ctx_index - cycle_pos) % ctx_count
        stats = merge_block(stats, moving, source * tok_rows)
        moving = shifted(moving, "ctx", 1)
        return (moving, stats)

    last_block, stats = lax.fori_loop(0, ctx_count - 1, cycle_step, (kv_block, start_stats))
    stats = merge_block(stats, last_block, (ctx_index + 1) % ctx_count * tok_rows)
    row_top, row_total, accum = stats
    attention_output = accum / jnp.transpose(row_total, (2, 0, 1))[..., None]
    log_total = row_top + jnp.log(row_total)
    attended_low = attention_output.reshape(tok_rows, kv_heads * QUERY_PER_KV * HEAD_SIZE).astype(
        jnp.bfloat16
    )
    attn_part = jnp.einsum("tc,dc->td", attended_low, wo_full, preferred_element_type=jnp.float32)
    residual_middle = layer_input + lax.psum(attn_part.astype(jnp.bfloat16), "tp").astype(
        jnp.float32
    )
    second_normed, scale_two = rms_normed(residual_middle, gain_rows[1])
    second_normed = second_normed.astype(jnp.bfloat16)
    gate_branch = jnp.dot(second_normed, ffn_full[0], preferred_element_type=jnp.float32)
    up_branch = jnp.dot(second_normed, ffn_full[1], preferred_element_type=jnp.float32)
    sigmoid_gate = jax.nn.sigmoid(gate_branch)
    silu_gate = gate_branch * sigmoid_gate
    silu_output = (silu_gate * up_branch).astype(jnp.bfloat16)
    down_part = jnp.einsum(
        "tf,df->td", silu_output, ffn_full[2], preferred_element_type=jnp.float32
    )
    hidden_out = (
        residual_middle + lax.psum(down_part.astype(jnp.bfloat16), "tp").astype(jnp.float32)
    ).astype(jnp.bfloat16)
    grad_low = cotangent[0]
    grad_top = grad_low.astype(jnp.float32)
    d_act = jnp.dot(grad_low, ffn_full[2], preferred_element_type=jnp.float32)
    grad_down = jnp.einsum("td,tf->df", grad_low, silu_output, preferred_element_type=jnp.float32)
    d_gate = (d_act * up_branch * sigmoid_gate * (1.0 + gate_branch * (1.0 - sigmoid_gate))).astype(
        jnp.bfloat16
    )
    d_up = (d_act * silu_gate).astype(jnp.bfloat16)
    grad_gate = jnp.einsum("td,tf->df", second_normed, d_gate, preferred_element_type=jnp.float32)
    grad_up = jnp.einsum("td,tf->df", second_normed, d_up, preferred_element_type=jnp.float32)
    d_two_part = jnp.einsum(
        "tf,df->td", d_gate, ffn_full[0], preferred_element_type=jnp.float32
    ) + jnp.einsum("tf,df->td", d_up, ffn_full[1], preferred_element_type=jnp.float32)
    d_two = lax.psum(d_two_part.astype(jnp.bfloat16), "tp").astype(jnp.float32)
    d_norm_two, grad_gain_two = norm_back(d_two, residual_middle, scale_two, gain_rows[1])
    d_mid = grad_top + d_norm_two
    d_branch = d_mid.astype(jnp.bfloat16)
    grad_wo = jnp.einsum("td,tc->dc", d_branch, attended_low, preferred_element_type=jnp.float32)
    d_att = (
        jnp.dot(d_branch, wo_full, preferred_element_type=jnp.float32)
        .astype(jnp.bfloat16)
        .reshape(tok_rows, kv_heads, QUERY_PER_KV, HEAD_SIZE)
    )
    delta = jnp.transpose(jnp.sum(d_att.astype(jnp.float32) * attention_output, axis=-1), (1, 2, 0))

    def block_grad(grad_query, kv_piece, first_row):
        piece_rows = kv_piece.shape[0]
        scores, allowed, keys_piece, values_piece = block_scores(kv_piece, first_row)
        probs = jnp.where(allowed, jnp.exp(scores - log_total[..., None]), 0.0)
        d_prob = jnp.einsum(
            "qhgd,khd->hgqk", d_att, values_piece, preferred_element_type=jnp.float32
        )
        d_score = (probs * (d_prob - delta[..., None])).astype(jnp.bfloat16)
        grad_query = (
            grad_query
            + jnp.einsum("hgqk,khd->qhgd", d_score, keys_piece, preferred_element_type=jnp.float32)
            * inv_scale
        )
        grad_key = (
            jnp.einsum("hgqk,qhgd->khd", d_score, queries, preferred_element_type=jnp.float32)
            * inv_scale
        )
        grad_value = jnp.einsum(
            "hgqk,qhgd->khd", probs.astype(jnp.bfloat16), d_att, preferred_element_type=jnp.float32
        )
        return (
            grad_query,
            jnp.stack(
                [
                    grad_key.reshape(piece_rows, kv_heads * HEAD_SIZE),
                    grad_value.reshape(piece_rows, kv_heads * HEAD_SIZE),
                ],
                axis=1,
            ),
        )

    zero_query = jnp.zeros((tok_rows, kv_heads, QUERY_PER_KV, HEAD_SIZE), jnp.float32)

    def pass_grads(grad_blk):
        return shifted(grad_blk.astype(jnp.bfloat16), "ctx", 1).astype(grad_blk.dtype)

    def back_step(cycle_pos, carry):
        moving, grad_blk, grad_query = carry
        source = (ctx_index - cycle_pos) % ctx_count
        grad_query, extra = block_grad(grad_query, moving, source * tok_rows)
        grad_blk = pass_grads(grad_blk + extra)
        moving = shifted(moving, "ctx", 1)
        return (moving, grad_blk, grad_query)

    zero_blk = jnp.zeros((tok_rows, 2, kv_heads * HEAD_SIZE), jnp.float32)
    last_block, grad_blk, grad_query = lax.fori_loop(
        0, ctx_count - 1, back_step, (kv_block, zero_blk, zero_query)
    )
    grad_query, extra = block_grad(grad_query, last_block, (ctx_index + 1) % ctx_count * tok_rows)
    grad_kv = pass_grads(grad_blk + extra)
    grad_key = grad_kv[:, 0].reshape(tok_rows, kv_heads, HEAD_SIZE)
    grad_value = grad_kv[:, 1].reshape(tok_rows, kv_heads, HEAD_SIZE)
    query_raw = rotate_back(grad_query, cos_table[:, None, None], sin_table[:, None, None])
    key_raw = rotate_back(grad_key, cos_table[:, None], sin_table[:, None])
    d_proj = (
        jnp.concatenate([query_raw, key_raw[:, :, None], grad_value[:, :, None]], axis=2)
        .reshape(tok_rows, kv_heads * (QUERY_PER_KV + 2) * HEAD_SIZE)
        .astype(jnp.bfloat16)
    )
    grad_wq = jnp.einsum("td,tc->dc", first_normed, d_proj, preferred_element_type=jnp.float32)
    d_one_part = jnp.einsum("tc,dc->td", d_proj, wq_full, preferred_element_type=jnp.float32)
    d_one = lax.psum(d_one_part.astype(jnp.bfloat16), "tp").astype(jnp.float32)
    d_norm_one, grad_gain_one = norm_back(d_one, layer_input, scale_one, gain_rows[0])
    grad_inputs = (d_mid + d_norm_one).astype(jnp.bfloat16)
    grad_ffn_full = jnp.stack([grad_gate, grad_up, grad_down], axis=0)
    grad_gain_full = jnp.stack([grad_gain_one, grad_gain_two], axis=0)
    grad_qkv, grad_out, grad_ffn, grad_gains = (
        lax.psum_scatter(grad_wq, ("fsdp", "ctx"), scatter_dimension=0, tiled=True),
        lax.psum_scatter(grad_wo, ("fsdp", "ctx"), scatter_dimension=0, tiled=True),
        lax.psum_scatter(grad_ffn_full, ("fsdp", "ctx"), scatter_dimension=1, tiled=True),
        lax.psum_scatter(grad_gain_full, ("fsdp", "ctx"), scatter_dimension=1, tiled=True),
    )
    return (hidden_out[None], grad_inputs[None], grad_qkv, grad_out, grad_ffn, grad_gains)


def solution(mesh):
    return jax.shard_map(
        on_device,
        mesh=mesh,
        in_specs=(
            P("fsdp", "ctx", None),
            P("fsdp", "ctx", None),
            P("fsdp", None),
            P("fsdp", None),
            P("fsdp", "tp"),
            P("fsdp", "tp"),
            P(None, "fsdp", "tp"),
            P(None, "fsdp"),
        ),
        out_specs=(
            P("fsdp", "ctx", None),
            P("fsdp", "ctx", None),
            P(("fsdp", "ctx"), "tp"),
            P(("fsdp", "ctx"), "tp"),
            P(None, ("fsdp", "ctx"), "tp"),
            P(None, ("fsdp", "ctx")),
        ),
        check_vma=False,
    )
```

profile of v0, /device:TPU:0, one launch (start us, length us, event | category | flops | bytes accessed | tf_op | source)
XLA Modules:
  0.0 1780.8 jit_solution(15485120004865932459)
XLA Ops:
  8.8 13.7 all_gather.12
  27.7 74.0 %all-gather.4.cloned.1.call-done = bf16[1536,1536]{1,0:T(8,128)(2,1)} async-done(((bf16[384,1536]{1,0:T(8,128)(2,1)}), bf16[1536,1536]{1,0:T(8,128)(2,1)}) %all-gather.4.cloned.1.call-update) | async-done | bytes 4718608 | tf_op jit(solution)/shard_map/all_gather | solution.py:100
  119.0 118.8 %while.44 = (s32[]{:T(128)}, bf16[768,2,384]{0,2,1:T(8,128)(2,1)}, f32[4,2,768]{2,1,0:T(2,128)}, f32[4,2,768]{2,1,0:T(2,128)}, f32[768,4,2,96]{0,3,2,1:T(8,128)}...) while((s32[]{:T(128)}, bf16[768,2,384]{0,2,1:T(8,128)(2,1)}, ...), condition=%wide.region_10.11_spmd.clone, body=%wide.region_5.10_spmd.clone.sunk | while | flops 1876896768 | bytes 76023200 | solution.py:175
  132.6 11.6 fusion.210
  147.0 11.1 bitcast_add_fusion.6
  172.6 11.5 fusion.210
  187.0 11.7 bitcast_add_fusion.6
  211.8 11.5 fusion.210
  226.1 11.7 bitcast_add_fusion.6
  239.2 9.8 fusion.44
  249.1 11.0 fusion.46
  260.7 12.2 fusion.134
  279.5 66.3 %all-reduce.5.cloned.1.call-done = bf16[768,1536]{1,0:T(8,128)(2,1)} async-done(((bf16[768,1536]{1,0:T(8,128)(2,1)}), bf16[768,1536]{1,0:T(8,128)(2,1)}) %all-reduce.5.cloned.1.call-update) | async-done | bytes 2359312 | tf_op jit(solution)/shard_map/psum | solution.py:184
  351.3 317.9 %all-gather.8.cloned.1.call-done = bf16[3,1536,2048]{2,1,0:T(8,128)(2,1)} async-done(((bf16[3,384,2048]{2,1,0:T(8,128)(2,1)}), bf16[3,1536,2048]{2,1,0:T(8,128)(2,1)}) %all-gather.8.cloned.1.call-update) | async-done | bytes 18874384 | tf_op jit(solution)/shard_map/all_gather | solution.py:102
  677.8 9.9 fusion.67
  687.7 12.6 multiply_convert_fusion
  718.4 66.8 %all-reduce.7.cloned.1.call-done = bf16[768,1536]{1,0:T(8,128)(2,1)} async-done(((bf16[768,1536]{1,0:T(8,128)(2,1)}), bf16[768,1536]{1,0:T(8,128)(2,1)}) %all-reduce.7.cloned.1.call-update) | async-done | bytes 2359312 | tf_op jit(solution)/shard_map/psum | solution.py:213
  797.0 171.2 %while.45 = (s32[]{:T(128)}, bf16[768,2,384]{0,2,1:T(8,128)(2,1)}, f32[768,2,384]{0,2,1:T(8,128)}, f32[768,4,2,96]{0,3,2,1:T(8,128)}, s32[768]{0:T(1024)S(1)}, /...) while((s32[]{:T(128)}, bf16[768,2,384]{0,2,1:T(8,128)(2,1)}, ...), condition=%wide.region_24.25_spmd.clone, body=%wide.region_21.24_spmd.clone.sunk | while | flops 4583857152 | bytes 246851200 | solution.py:270
  808.9 10.4 fusion.226
  843.2 9.8 collective-permute-done.1
  864.9 10.4 fusion.226
  900.8 9.8 collective-permute-done.1
  922.5 10.4 fusion.226
  958.4 9.8 collective-permute-done.1
  979.7 9.7 fusion.48
  989.4 10.3 fusion.41
  1004.6 9.7 fusion.83
  1026.6 119.1 %all-reduce.9.cloned.1.call-done = (bf16[768,1536]{1,0:T(8,128)(2,1)}, bf16[768,1536]{1,0:T(8,128)(2,1)}) async-done(((bf16[768,1536]{1,0:T(8,128)(2,1)}, bf16[768,1536]{1,0:T(8,128)(2,1)}), (bf16[768,1536]{1,0:T(8,128)(2,1)}, bf16[768,1536]{1,0:T(8,128)(2,1)})) %all-reduce.9.cloned.1.call-update) | async-done | bytes 4718608 | tf_op jit(solution)/shard_map/psum | solution.py:198
  1191.8 17.4 pad_maximum_fusion
  1218.9 66.9 %reduce-scatter.9.cloned.1.call-done = f32[96,768]{1,0:T(8,128)} async-done(((f32[1536,768]{1,0:T(8,128)}), f32[96,768]{1,0:T(8,128)}) %reduce-scatter.9.cloned.1.call-update) | async-done | bytes 294928 | tf_op jit(solution)/shard_map/reduce_scatter | solution.py:293
  1285.8 115.7 %reduce-scatter.7.cloned.1.call-done = f32[96,1536]{1,0:T(8,128)} async-done(((f32[1536,1536]{1,0:T(8,128)}), f32[96,1536]{1,0:T(8,128)}) %reduce-scatter.7.cloned.1.call-update) | async-done | bytes 589840 | tf_op jit(solution)/shard_map/reduce_scatter | solution.py:292
  1401.5 372.3 %reduce-scatter.11.cloned.1.call-done = f32[3,96,2048]{2,1,0:T(8,128)} async-done(((f32[3,1536,2048]{2,1,0:T(8,128)}), f32[3,96,2048]{2,1,0:T(8,128)}) %reduce-scatter.11.cloned.1.call-update) | async-done | bytes 2359312 | tf_op jit(solution)/shard_map/reduce_scatter | solution.py:294
  (330 shorter events, 319.6 us)
Async XLA Ops:
  7.2 18.2 %copy-start.54 = (s32[1,8]{1,0:T(1,128)S(1)}, s32[1,8]{1,0:T(1,128)}, u32[]{:S(2)}) copy-start(s32[1,8]{1,0:T(1,128)} %param.14) | copy-start | bytes 100
  7.2 18.4 %copy-start.41 = (s32[1,4]{1,0:T(1,128)S(1)}, s32[1,4]{1,0:T(1,128)}, u32[]{:S(2)}) copy-start(s32[1,4]{1,0:T(1,128)} %param.15) | copy-start | bytes 52
  7.2 94.5 %all-gather.4.cloned.1.call-start = ((), (), s32[]{:S(2)}) async-start(), calls=%async_computation.4 | async-start | bytes 5898240 | tf_op jit(solution)/shard_map/all_gather | solution.py:100
  7.9 265.0 %all-gather.6.cloned.1.call-start = ((), (), s32[]{:S(2)}) async-start(), calls=%async_computation.5 | async-start | bytes 2949120 | tf_op jit(solution)/shard_map/all_gather | solution.py:101
  8.7 337.1 %all-reduce.5.cloned.1.call-start = ((), (), s32[]{:S(2)}) async-start(), calls=%async_computation.6 | async-start | bytes 4718592 | tf_op jit(solution)/shard_map/psum | solution.py:184
  23.1 85.5 %copy-start.36 = (f32[1536]{0:T(1024)}, f32[1536]{0:T(1024)S(1)}, u32[]{:S(2)}) copy-start(f32[1536]{0:T(1024)S(1)} %get-tuple-element.757) | copy-start | bytes 18436
  25.3 83.3 %copy-start.45 = (f32[768]{0:T(1024)}, f32[768]{0:T(1024)S(1)}, u32[]{:S(2)}) copy-start(f32[768]{0:T(1024)S(1)} %add_rsqrt_fusion.1) | copy-start | bytes 9220
  26.4 88.7 %copy-start.15 = (f32[768,48]{0,1:T(8,128)}, f32[768,48]{0,1:T(8,128)S(1)}, u32[]{:S(2)}) copy-start(f32[768,48]{0,1:T(8,128)S(1)} %get-tuple-element.842) | copy-start | bytes 442372
  26.4 88.7 %copy-start.17 = (f32[768,48]{0,1:T(8,128)}, f32[768,48]{0,1:T(8,128)S(1)}, u32[]{:S(2)}) copy-start(f32[768,48]{0,1:T(8,128)S(1)} %get-tuple-element.843) | copy-start | bytes 442372
  120.9 37.2 %collective-permute-start = (bf16[768,2,384]{0,2,1:T(8,128)(2,1)S(1)}, bf16[768,2,384]{0,2,1:T(8,128)(2,1)}, u32[]{:S(2)}, u32[]{:S(2)}) collective-permute-start(bf16[768,2,384]{0,2,1:T(8,128)(2,1)S(1)} %copy.78), channel_id=1, source_target_pairs={{0,2},{2,4},{4,6},{6,0},{1,3},{3,5},{5,7},{7,1},{8,10},{10,12},{12... | collective-permute-start | bytes 3538952 | tf_op jit(solution)/shard_map/while/body/eval_jaxpr/ppermute | solution.py:17
  159.4 39.4 %collective-permute-start = (bf16[768,2,384]{0,2,1:T(8,128)(2,1)S(1)}, bf16[768,2,384]{0,2,1:T(8,128)(2,1)}, u32[]{:S(2)}, u32[]{:S(2)}) collective-permute-start(bf16[768,2,384]{0,2,1:T(8,128)(2,1)S(1)} %copy.78), channel_id=1, source_target_pairs={{0,2},{2,4},{4,6},{6,0},{1,3},{3,5},{5,7},{7,1},{8,10},{10,12},{12... | collective-permute-start | bytes 3538952 | tf_op jit(solution)/shard_map/while/body/eval_jaxpr/ppermute | solution.py:17
  200.0 37.9 %collective-permute-start = (bf16[768,2,384]{0,2,1:T(8,128)(2,1)S(1)}, bf16[768,2,384]{0,2,1:T(8,128)(2,1)}, u32[]{:S(2)}, u32[]{:S(2)}) collective-permute-start(bf16[768,2,384]{0,2,1:T(8,128)(2,1)S(1)} %copy.78), channel_id=1, source_target_pairs={{0,2},{2,4},{4,6},{6,0},{1,3},{3,5},{5,7},{7,1},{8,10},{10,12},{12... | collective-permute-start | bytes 3538952 | tf_op jit(solution)/shard_map/while/body/eval_jaxpr/ppermute | solution.py:17
  237.8 11.2 copy-start.43
  278.4 67.3 %copy-start.4 = (bf16[1,768,1536]{2,1,0:T(8,128)(2,1)S(1)}, bf16[1,768,1536]{2,1,0:T(8,128)(2,1)}, u32[]{:S(2)}) copy-start(bf16[1,768,1536]{2,1,0:T(8,128)(2,1)} %param.12) | copy-start | bytes 7077892
  278.4 390.8 %all-gather.8.cloned.1.call-start = ((), (), s32[]{:S(2)}) async-start(), calls=%async_computation.7 | async-start | bytes 23592960 | tf_op jit(solution)/shard_map/all_gather | solution.py:102
  279.0 70.0 %copy-start.34 = (f32[1536]{0:T(1024)S(1)}, f32[1536]{0:T(1024)}, u32[]{:S(2)}) copy-start(f32[1536]{0:T(1024)} %get-tuple-element.756) | copy-start | bytes 18436
  279.0 506.2 %all-reduce.7.cloned.1.call-start = ((), (), s32[]{:S(2)}) async-start(), calls=%async_computation.8 | async-start | bytes 4718592 | tf_op jit(solution)/shard_map/psum | solution.py:213
  718.2 427.4 %all-reduce.9.cloned.1.call-start = ((), (), s32[]{:S(2)}) async-start(), calls=%async_computation.13 | async-start | bytes 9437184 | tf_op jit(solution)/shard_map/psum | solution.py:198
  824.4 15.9 collective-permute-start.2
  824.4 28.6 %collective-permute-start.1 = (bf16[768,2,384]{0,2,1:T(8,128)(2,1)S(1)}, bf16[768,2,384]{0,2,1:T(8,128)(2,1)}, u32[]{:S(2)}, u32[]{:S(2)}) collective-permute-start(bf16[768,2,384]{0,2,1:T(8,128)(2,1)S(1)} %copy.94), channel_id=1, source_target_pairs={{0,2},{2,4},{4,6},{6,0},{1,3},{3,5},{5,7},{7,1},{8,10},{10,12},{12... | collective-permute-start | bytes 3538952 | tf_op jit(solution)/shard_map/while/body/eval_jaxpr/ppermute | solution.py:17
  882.0 15.9 collective-permute-start.2
  882.0 28.6 %collective-permute-start.1 = (bf16[768,2,384]{0,2,1:T(8,128)(2,1)S(1)}, bf16[768,2,384]{0,2,1:T(8,128)(2,1)}, u32[]{:S(2)}, u32[]{:S(2)}) collective-permute-start(bf16[768,2,384]{0,2,1:T(8,128)(2,1)S(1)} %copy.94), channel_id=1, source_target_pairs={{0,2},{2,4},{4,6},{6,0},{1,3},{3,5},{5,7},{7,1},{8,10},{10,12},{12... | collective-permute-start | bytes 3538952 | tf_op jit(solution)/shard_map/while/body/eval_jaxpr/ppermute | solution.py:17
  939.6 15.9 collective-permute-start.2
  939.6 28.6 %collective-permute-start.1 = (bf16[768,2,384]{0,2,1:T(8,128)(2,1)S(1)}, bf16[768,2,384]{0,2,1:T(8,128)(2,1)}, u32[]{:S(2)}, u32[]{:S(2)}) collective-permute-start(bf16[768,2,384]{0,2,1:T(8,128)(2,1)S(1)} %copy.94), channel_id=1, source_target_pairs={{0,2},{2,4},{4,6},{6,0},{1,3},{3,5},{5,7},{7,1},{8,10},{10,12},{12... | collective-permute-start | bytes 3538952 | tf_op jit(solution)/shard_map/while/body/eval_jaxpr/ppermute | solution.py:17
  1003.1 15.7 collective-permute-start.3
  1025.9 119.8 %copy-start.5 = (bf16[1,768,1536]{2,1,0:T(8,128)(2,1)S(1)}, bf16[1,768,1536]{2,1,0:T(8,128)(2,1)}, u32[]{:S(2)}) copy-start(bf16[1,768,1536]{2,1,0:T(8,128)(2,1)} %param.12) | copy-start | bytes 7077892
  1025.9 119.8 %copy-start.37 = (f32[1536]{0:T(1024)S(1)}, f32[1536]{0:T(1024)}, u32[]{:S(2)}) copy-start(f32[1536]{0:T(1024)} %copy-done.36) | copy-start | bytes 18436
  1025.9 119.8 %copy-start.46 = (f32[768]{0:T(1024)S(1)}, f32[768]{0:T(1024)}, u32[]{:S(2)}) copy-start(f32[768]{0:T(1024)} %copy-done.45) | copy-start | bytes 9220
  1025.9 191.5 %reduce-scatter.13.cloned.1.call-start = ((), (), s32[]{:S(2)}) async-start(), calls=%async_computation.12 | async-start | bytes 835584
  1150.1 135.7 %reduce-scatter.9.cloned.1.call-start = ((), (), s32[]{:S(2)}) async-start(), calls=%async_computation.10 | async-start | bytes 5013504 | tf_op jit(solution)/shard_map/reduce_scatter | solution.py:293
  1159.2 242.3 %reduce-scatter.7.cloned.1.call-start = ((), (), s32[]{:S(2)}) async-start(), calls=%async_computation.9 | async-start | bytes 10027008 | tf_op jit(solution)/shard_map/reduce_scatter | solution.py:292
  1168.0 605.8 %reduce-scatter.11.cloned.1.call-start = ((), (), s32[]{:S(2)}) async-start(), calls=%async_computation.11 | async-start | bytes 40108032 | tf_op jit(solution)/shard_map/reduce_scatter | solution.py:294
  (63 other events, 345.4 us)
Sparse Core Ops, SparseCore 0:
  9.6 92.0 all-gather.3
  103.3 48.9 all-gather.5
  278.5 67.1 all-reduce.4
  347.3 321.8 all-gather.7
  718.3 66.9 all-reduce.6
  1026.0 119.5 all-reduce.8
  1150.2 56.4 reduce-scatter.12
  1211.1 74.6 reduce-scatter.8
  1291.0 110.3 reduce-scatter.6
  1406.1 367.5 reduce-scatter.10
where the time goes:
time: 1790 us; the launch traced here: 1780 us
  waiting for transfers between devices  1250 us (70%)
  matrix products  329 us (18%)
  other arithmetic  120 us (7%)
  local copies, waits for them, and re-layouts  40.3 us (2%)
    reduce_scatter x1, waiting for transfers between devices, on_device(): lax.psum_scatter(grad_ffn_full, ('fsdp', 'ctx'), scatter_dimension=1, til...  372 us
    all_gather x1, waiting for transfers between devices, on_device(): lax.all_gather(feedforward_weight, 'fsdp', axis=1, tiled=True)  318 us
    psum x1, waiting for transfers between devices, on_device(): lax.psum(down_part.astype(jnp.bfloat16), 'tp').astype(jnp.float32)  119 us
    reduce_scatter x1, waiting for transfers between devices, on_device(): lax.psum_scatter(grad_wq, ('fsdp', 'ctx'), scatter_dimension=0, tiled=True)  116 us
    all_gather x1, waiting for transfers between devices, on_device(): lax.all_gather(query_key_value_weight, 'fsdp', axis=0, tiled=True)  74 us
    reduce_scatter x1, waiting for transfers between devices, on_device(): lax.psum_scatter(grad_wo, ('fsdp', 'ctx'), scatter_dimension=0, tiled=True)  66.9 us
    psum x1, waiting for transfers between devices, on_device(): d_two = lax.psum(d_two_part.astype(jnp.bfloat16), 'tp').astype(jnp.float32)  66.8 us
    psum x1, waiting for transfers between devices, on_device(): lax.psum(attn_part.astype(jnp.bfloat16), 'tp').astype(jnp.float32)  66.3 us
  transfers between devices with their start and end apart: 20, of which 15 were waited for; matrix products, arithmetic and copies ran while one was open for 16% of the time, Pallas kernels for 0%

commit v1 on v0

v1 whole, which is shorter than its diff:
```python
import functools
import math

import jax
import jax.numpy as jnp
from jax import lax
from jax.experimental import pallas as pl
from jax.experimental.pallas import tpu as pltpu
from jax.sharding import PartitionSpec as P

HEAD_SIZE = 96
QUERY_PER_KV = 2
HALF = HEAD_SIZE // 2
BLOCK = 128

norm_eps = 1e-05
rope_base = 100000.0
masked_score = -1e30
SCORE_SCALE = HEAD_SIZE ** (-0.5)
SCORE_SCALE_2 = SCORE_SCALE * math.log2(math.e)

bf16 = jnp.bfloat16
f32 = jnp.float32


def mm(a, b, contract=((1,), (0,))):
    return lax.dot_general(a, b, (contract, ((), ())), preferred_element_type=f32)


def fill_keys(count, blocks, kv_refs, kn_ref, kt_ref, vn_ref, vt_ref):
    for s in range(count):
        for b in range(blocks):
            columns = slice(b * BLOCK, (b + 1) * BLOCK)
            places = slice(s * BLOCK, (s + 1) * BLOCK)
            key = kv_refs[s][0, 0, :, columns]
            value = kv_refs[s][0, 1, :, columns]
            kn_ref[b, places, :] = key.T
            if kt_ref is not None:
                kt_ref[b, :, places] = key
            if vn_ref is not None:
                vn_ref[b, places, :] = value.T
            if vt_ref is not None:
                vt_ref[b, :, places] = value


def fill_places(count, stripes_ref, place_ref):
    step = lax.broadcasted_iota(jnp.int32, (BLOCK, QUERY_PER_KV * BLOCK), 0) * count
    for s in range(count):
        place_ref[s * BLOCK : (s + 1) * BLOCK, :] = step + stripes_ref[s]


def twice(row):
    return jnp.concatenate([row] * QUERY_PER_KV, axis=1)


def block_of(ref, i):
    columns = slice(i * BLOCK, (i + 1) * BLOCK)
    return jnp.concatenate([ref[0, g, :, columns] for g in range(QUERY_PER_KV)], axis=1)


def forward_kernel(count, blocks, starts_ref, stripes_ref, place_q_ref, start_q_ref, q_ref, *rest):
    kv_refs = rest[:count]
    o_ref, lse_ref, kn_ref, vt_ref, place_ref = rest[count:]
    fill_keys(count, blocks, kv_refs, kn_ref, None, None, vt_ref)
    fill_places(count, stripes_ref, place_ref)
    for i in range(blocks):
        columns = slice(i * BLOCK, (i + 1) * BLOCK)
        query = block_of(q_ref, i)
        place_q = twice(place_q_ref[:, columns])
        start_q = twice(start_q_ref[:, columns])

        def scores_of(b):
            scores = mm(kn_ref[b], query)
            offset = b * (BLOCK * count)
            place = place_ref[...]
            allowed = (place >= start_q - offset) & (place <= place_q - offset)
            return jnp.where(allowed, scores * SCORE_SCALE_2, masked_score)

        scores = scores_of(i)
        top = jnp.max(scores, axis=0, keepdims=True)
        weights = jnp.exp2(scores - top)
        total = jnp.sum(weights, axis=0, keepdims=True)
        accum = mm(vt_ref[i], weights.astype(bf16))

        def step(b, carry):
            top, total, accum = carry
            scores = scores_of(b)
            new_top = jnp.maximum(top, jnp.max(scores, axis=0, keepdims=True))
            fade = jnp.exp2(top - new_top)
            weights = jnp.exp2(scores - new_top)
            total = total * fade + jnp.sum(weights, axis=0, keepdims=True)
            accum = accum * fade + mm(vt_ref[b], weights.astype(bf16))
            return new_top, total, accum

        top, total, accum = lax.fori_loop(starts_ref[i], i, step, (top, total, accum))
        result = (accum / total).astype(bf16)
        lse = top + jnp.log2(total)
        for g in range(QUERY_PER_KV):
            part = slice(g * BLOCK, (g + 1) * BLOCK)
            o_ref[0, g, :, columns] = result[:, part]
            lse_ref[0, g : g + 1, columns] = lse[:, part]


def backward_kernel(
    count, blocks, starts_ref, stripes_ref, place_q_ref, start_q_ref, q_ref, do_ref, o_ref, lse_ref, *rest
):
    kv_refs = rest[:count]
    dq_ref = rest[count]
    dkv_refs = rest[count + 1 : 2 * count + 1]
    kn_ref, kt_ref, vn_ref, place_ref, dk_ref, dv_ref = rest[2 * count + 1 :]
    fill_keys(count, blocks, kv_refs, kn_ref, kt_ref, vn_ref, None)
    fill_places(count, stripes_ref, place_ref)
    dk_ref[...] = jnp.zeros_like(dk_ref)
    dv_ref[...] = jnp.zeros_like(dv_ref)
    for i in range(blocks):
        columns = slice(i * BLOCK, (i + 1) * BLOCK)
        query = block_of(q_ref, i)
        d_out = block_of(do_ref, i)
        out = block_of(o_ref, i)
        query_rows = query.T
        d_out_rows = d_out.T
        delta = jnp.sum(d_out.astype(f32) * out.astype(f32), axis=0, keepdims=True)
        lse = jnp.concatenate([lse_ref[0, g : g + 1, columns] for g in range(QUERY_PER_KV)], axis=1)
        place_q = twice(place_q_ref[:, columns])
        start_q = twice(start_q_ref[:, columns])

        def step(b, d_query):
            scores = mm(kn_ref[b], query)
            offset = b * (BLOCK * count)
            place = place_ref[...]
            allowed = (place >= start_q - offset) & (place <= place_q - offset)
            probs = jnp.exp2(jnp.where(allowed, scores * SCORE_SCALE_2, masked_score) - lse)
            d_prob = mm(vn_ref[b], d_out)
            d_score = (probs * (d_prob - delta)).astype(bf16)
            dv_ref[b] += mm(probs.astype(bf16), d_out_rows)
            dk_ref[b] += mm(d_score, query_rows)
            return d_query + mm(kt_ref[b], d_score)

        d_query = lax.fori_loop(
            starts_ref[i], i + 1, step, jnp.zeros((HEAD_SIZE, QUERY_PER_KV * BLOCK), f32)
        )
        for g in range(QUERY_PER_KV):
            dq_ref[0, g, :, columns] = d_query[:, g * BLOCK : (g + 1) * BLOCK] * SCORE_SCALE
    for s in range(count):
        places = slice(s * BLOCK, (s + 1) * BLOCK)
        for b in range(blocks):
            columns = slice(b * BLOCK, (b + 1) * BLOCK)
            dkv_refs[s][0, 0, :, columns] = (dk_ref[b, places, :] * SCORE_SCALE).T.astype(bf16)
            dkv_refs[s][0, 1, :, columns] = dv_ref[b, places, :].T.astype(bf16)


def head_spec(*dims):
    return pl.BlockSpec((1, *dims), lambda h, *_: (h,) + (0,) * len(dims))


def row_spec(tokens):
    return pl.BlockSpec((1, tokens), lambda h, *_: (0, 0))


def attention_forward(queries, pieces, starts, stripes, place, start):
    heads, _, _, tokens = queries.shape
    count, blocks = len(pieces), tokens // BLOCK
    keys = count * BLOCK
    per_query = head_spec(QUERY_PER_KV, HEAD_SIZE, tokens)
    per_kv = head_spec(2, HEAD_SIZE, tokens)
    return pl.pallas_call(
        functools.partial(forward_kernel, count, blocks),
        grid_spec=pltpu.PrefetchScalarGridSpec(
            num_scalar_prefetch=2,
            grid=(heads,),
            in_specs=[row_spec(tokens)] * 2 + [per_query] + [per_kv] * count,
            out_specs=[per_query, head_spec(QUERY_PER_KV, tokens)],
            scratch_shapes=[
                pltpu.VMEM((blocks, keys, HEAD_SIZE), bf16),
                pltpu.VMEM((blocks, HEAD_SIZE, keys), bf16),
                pltpu.VMEM((keys, QUERY_PER_KV * BLOCK), jnp.int32),
            ],
        ),
        out_shape=[
            jax.ShapeDtypeStruct(queries.shape, bf16),
            jax.ShapeDtypeStruct((heads, QUERY_PER_KV, tokens), f32),
        ],
        compiler_params=pltpu.CompilerParams(vmem_limit_bytes=40 << 20),
        cost_estimate=pl.CostEstimate(flops=3 << 30, bytes_accessed=8 << 20, transcendentals=8 << 20),
        name="attention_forward",
    )(starts, stripes, place, start, queries, *pieces)


def attention_backward(queries, d_att, attended, lse, pieces, starts, stripes, place, start):
    heads, _, _, tokens = queries.shape
    count, blocks = len(pieces), tokens // BLOCK
    keys = count * BLOCK
    per_query = head_spec(QUERY_PER_KV, HEAD_SIZE, tokens)
    per_kv = head_spec(2, HEAD_SIZE, tokens)
    return pl.pallas_call(
        functools.partial(backward_kernel, count, blocks),
        grid_spec=pltpu.PrefetchScalarGridSpec(
            num_scalar_prefetch=2,
            grid=(heads,),
            in_specs=[row_spec(tokens)] * 2
            + [per_query] * 3
            + [head_spec(QUERY_PER_KV, tokens)]
            + [per_kv] * count,
            out_specs=[per_query] + [per_kv] * count,
            scratch_shapes=[
                pltpu.VMEM((blocks, keys, HEAD_SIZE), bf16),
                pltpu.VMEM((blocks, HEAD_SIZE, keys), bf16),
                pltpu.VMEM((blocks, keys, HEAD_SIZE), bf16),
                pltpu.VMEM((keys, QUERY_PER_KV * BLOCK), jnp.int32),
                pltpu.VMEM((blocks, keys, HEAD_SIZE), f32),
                pltpu.VMEM((blocks, keys, HEAD_SIZE), f32),
            ],
        ),
        out_shape=[jax.ShapeDtypeStruct(queries.shape, f32)]
        + [jax.ShapeDtypeStruct(pieces[0].shape, bf16)] * count,
        compiler_params=pltpu.CompilerParams(vmem_limit_bytes=48 << 20),
        cost_estimate=pl.CostEstimate(flops=8 << 30, bytes_accessed=16 << 20, transcendentals=8 << 20),
        name="attention_backward",
    )(starts, stripes, place, start, queries, d_att, attended, lse, *pieces)


def core_swap(value):
    size = lax.axis_size("ctx")
    return lax.ppermute(value, "ctx", [(i, i ^ 1) for i in range(size)])


def chip_shift(value, by):
    size = lax.axis_size("ctx")
    return lax.ppermute(value, "ctx", [(i, (i + 2 * by) % size) for i in range(size)])


def group_shift(value, by):
    size = lax.axis_size("fsdp")
    return lax.ppermute(value, "fsdp", [(i, (i + by) % size) for i in range(size)])


def tp_sum(part):
    part = lax.optimization_barrier(part.astype(bf16))
    size = lax.axis_size("tp")
    if size != 2:
        return lax.psum(part, "tp").astype(f32)
    other = lax.ppermute(part, "tp", [(0, 1), (1, 0)])
    return part.astype(f32) + other.astype(f32)


def rows_for_core(activation, core):
    tokens, width = activation.shape
    groups, chips = lax.axis_size("fsdp"), lax.axis_size("ctx") // 2
    rows = width // (groups * chips * 2)
    turned = activation.T.reshape(groups, chips, 2, rows, tokens)
    return lax.dynamic_index_in_dim(turned, core, 2, keepdims=False)


def weight_gradient(left, right):
    chips = lax.axis_size("ctx") // 2
    groups = lax.axis_size("fsdp")
    chip, group = lax.axis_index("ctx") // 2, lax.axis_index("fsdp")
    _, _, rows, _ = left[0].shape
    columns = right[0].shape[1]

    def product(which):
        total = None
        for a, b in zip(left, right):
            picked = lax.dynamic_index_in_dim(a, which, 1, keepdims=False)
            term = mm(picked.reshape(groups * rows, -1), b)
            total = term if total is None else total + term
        return total

    arrived = [
        chip_shift(product((chip + by) % chips).astype(bf16), by) for by in range(1, chips)
    ]
    total = product(chip)
    for piece in arrived:
        total = total + piece.astype(f32)
    total = total.reshape(groups, rows, columns)
    low = total.astype(bf16)
    result = lax.dynamic_index_in_dim(total, group, 0, keepdims=False)
    for by in range(1, groups):
        sent = lax.dynamic_index_in_dim(low, (group + by) % groups, 0, keepdims=False)
        result = result + group_shift(sent, by).astype(f32)
    return result


def slot_meta(ctx_index, tokens, stripe_row, lengths):
    count = stripe_row.shape[0]
    ends = jnp.cumsum(lengths)
    residue = jnp.sum(jnp.where(jnp.arange(count) == ctx_index, stripe_row, 0))
    packed = jnp.arange(tokens, dtype=jnp.int32) * count + residue
    passed = (packed[:, None] >= ends[None, :]).astype(jnp.int32)
    start = jnp.sum(passed * lengths[None, :], axis=1)
    return packed, start


def rms_normed(values, gain):
    scale_row = lax.rsqrt(jnp.mean(values * values, axis=-1, keepdims=True) + norm_eps)
    return (values * scale_row * gain, scale_row)


def norm_back(grad_normed, values, scale_row, gain):
    unit_rows = values * scale_row
    weighted = grad_normed * gain
    return scale_row * (weighted - unit_rows * jnp.mean(weighted * unit_rows, axis=-1, keepdims=True))


def rotate(vector, cos_table, sin_table):
    front, back = vector[..., 0, :, :], vector[..., 1, :, :]
    return jnp.stack(
        [front * cos_table - back * sin_table, back * cos_table + front * sin_table], axis=-3
    )


def on_device(
    hidden_in,
    cotangent,
    doc_lengths,
    stripe,
    query_key_value_weight,
    output_weight,
    feedforward_weight,
    gains,
):
    ctx_count, ctx_index = lax.axis_size("ctx"), lax.axis_index("ctx")
    group_count, group = lax.axis_size("fsdp"), lax.axis_index("fsdp")
    core = ctx_index % 2
    tokens, width = hidden_in.shape[1:]
    qkv_columns = query_key_value_weight.shape[1]
    att_columns = output_weight.shape[1]
    units = feedforward_weight.shape[2]
    kv_heads = qkv_columns // ((QUERY_PER_KV + 2) * HEAD_SIZE)

    def share(weight):
        rows = weight.shape[0] // ctx_count
        return lax.dynamic_slice_in_dim(weight, ctx_index * rows, rows, 0)

    def gathered(weight):
        return lax.all_gather(weight, ("fsdp", "ctx"), axis=0, tiled=True)

    first = gathered(
        jnp.concatenate([share(query_key_value_weight), share(output_weight)], axis=1)
    )
    wq, wo = first[:, :qkv_columns], first[:, qkv_columns:]
    second = gathered(jnp.concatenate([share(feedforward_weight[i]) for i in range(3)], axis=1))
    w_gate, w_up, w_down = (second[:, i * units : (i + 1) * units] for i in range(3))

    gain_parts = [gains] + [group_shift(gains, by) for by in range(1, group_count)]
    gain_stack = jnp.stack(gain_parts, axis=0)
    gain_rows = jnp.concatenate(
        [
            lax.dynamic_index_in_dim(gain_stack, (group - i) % group_count, 0, keepdims=False)
            for i in range(group_count)
        ],
        axis=1,
    ).astype(f32)

    lengths, stripe_row = doc_lengths[0], stripe[0]
    packed, start = slot_meta(ctx_index, tokens, stripe_row, lengths)
    frequency = rope_base ** (-(2.0 * jnp.arange(HALF, dtype=f32)) / HEAD_SIZE)
    angles = frequency[:, None] * (packed - start).astype(f32)[None, :]
    cos_table, sin_table = jnp.cos(angles), jnp.sin(angles)
    block_starts = start[::BLOCK] // (ctx_count * BLOCK)
    sources = []
    for by in range(ctx_count // 2):
        source = (ctx_index - 2 * by) % ctx_count
        sources += [source, source ^ 1]
    stripes = jnp.stack(
        [lax.dynamic_index_in_dim(stripe_row, s, 0, keepdims=False) for s in sources]
    )
    meta = (block_starts, stripes, packed[None, :], start[None, :])

    layer_input = hidden_in[0].astype(f32)
    first_normed, scale_one = rms_normed(layer_input, gain_rows[0])
    first_normed = first_normed.astype(bf16)
    projected = mm(wq, first_normed, ((0,), (1,))).reshape(
        kv_heads, QUERY_PER_KV + 2, 2, HALF, tokens
    )
    turned = rotate(projected[:, : QUERY_PER_KV + 1], cos_table, sin_table).astype(bf16)
    queries = turned[:, :QUERY_PER_KV].reshape(kv_heads, QUERY_PER_KV, HEAD_SIZE, tokens)
    kv_own = jnp.stack(
        [
            turned[:, QUERY_PER_KV].reshape(kv_heads, HEAD_SIZE, tokens),
            projected[:, QUERY_PER_KV + 1].astype(bf16).reshape(kv_heads, HEAD_SIZE, tokens),
        ],
        axis=1,
    )
    pieces = []
    for by in range(ctx_count // 2):
        piece = chip_shift(kv_own, by) if by else kv_own
        pieces += [piece, core_swap(piece)]
    attended, lse = attention_forward(queries, pieces, *meta)
    attended_rows = attended.reshape(att_columns, tokens)
    attn_part = mm(attended_rows, wo, ((0,), (1,)))
    middle = layer_input + tp_sum(attn_part)

    second_normed, scale_two = rms_normed(middle, gain_rows[1])
    second_normed = second_normed.astype(bf16)
    grad_low = cotangent[0]
    gate = mm(second_normed, w_gate)
    up = mm(second_normed, w_up)
    d_act = mm(grad_low, w_down)
    sigmoid_gate = jax.nn.sigmoid(gate)
    silu_gate = gate * sigmoid_gate
    activated = (silu_gate * up).astype(bf16)
    d_gate = (d_act * up * sigmoid_gate * (1.0 + gate * (1.0 - sigmoid_gate))).astype(bf16)
    d_up = (d_act * silu_gate).astype(bf16)
    d_two = tp_sum(mm(d_gate, w_gate, ((1,), (1,))) + mm(d_up, w_up, ((1,), (1,))))
    hidden_out = (middle + tp_sum(mm(activated, w_down, ((1,), (1,))))).astype(bf16)

    def exchanged(activation):
        return rows_for_core(activation, core), core_swap(rows_for_core(activation, 1 - core))

    def both(value):
        return value, core_swap(value)

    rows_two = exchanged(second_normed)
    rows_dy = exchanged(grad_low)
    grad_gate = weight_gradient(rows_two, both(d_gate))
    grad_up = weight_gradient(rows_two, both(d_up))
    grad_down = weight_gradient(rows_dy, both(activated))

    d_mid = grad_low.astype(f32) + norm_back(d_two, middle, scale_two, gain_rows[1])
    gain_two = jnp.sum(d_two * (middle * scale_two), axis=0)
    d_branch = d_mid.astype(bf16)

    d_att = mm(wo, d_branch, ((0,), (1,))).astype(bf16).reshape(attended.shape)
    back = attention_backward(queries, d_att, attended, lse, pieces, *meta)
    d_query, d_pieces = back[0], back[1:]
    grad_out = weight_gradient(exchanged(d_branch), both(attended_rows.T))
    d_kv = None
    for by in reversed(range(ctx_count // 2)):
        mine, partners = d_pieces[2 * by], d_pieces[2 * by + 1]
        chip_sum = mine.astype(f32) + core_swap(partners).astype(f32)
        term = chip_shift(chip_sum.astype(bf16), -by).astype(f32) if by else chip_sum
        d_kv = term if d_kv is None else d_kv + term
    d_kv = d_kv.reshape(kv_heads, 2, 2, HALF, tokens)
    d_query = d_query.reshape(kv_heads, QUERY_PER_KV, 2, HALF, tokens)
    d_turned = rotate(
        jnp.concatenate([d_query, d_kv[:, :1]], axis=1), cos_table, -sin_table
    )
    d_proj = (
        jnp.concatenate([d_turned, d_kv[:, 1:]], axis=1).astype(bf16).reshape(qkv_columns, tokens)
    )
    d_one_part = mm(d_proj, wq, ((0,), (1,)))
    d_one = tp_sum(d_one_part)
    grad_qkv = weight_gradient(exchanged(first_normed), both(d_proj.T))
    grad_in = (d_mid + norm_back(d_one, layer_input, scale_one, gain_rows[0])).astype(bf16)
    gain_one = jnp.sum(d_one * (layer_input * scale_one), axis=0)

    grad_ffn = jnp.stack([grad_gate, grad_up, grad_down], axis=0)
    grad_gains = lax.psum_scatter(
        jnp.stack([gain_one, gain_two], axis=0), ("fsdp", "ctx"), scatter_dimension=1, tiled=True
    )
    return (hidden_out[None], grad_in[None], grad_qkv, grad_out, grad_ffn, grad_gains)


def solution(mesh):
    return jax.shard_map(
        on_device,
        mesh=mesh,
        in_specs=(
            P("fsdp", "ctx", None),
            P("fsdp", "ctx", None),
            P("fsdp", None),
            P("fsdp", None),
            P("fsdp", "tp"),
            P("fsdp", "tp"),
            P(None, "fsdp", "tp"),
            P(None, "fsdp"),
        ),
        out_specs=(
            P("fsdp", "ctx", None),
            P("fsdp", "ctx", None),
            P(("fsdp", "ctx"), "tp"),
            P(("fsdp", "ctx"), "tp"),
            P(None, ("fsdp", "ctx"), "tp"),
            P(None, ("fsdp", "ctx")),
        ),
        check_vma=False,
    )
```

time: 1790 us -> 807 us (0.45)
  waiting for transfers between devices: 1250 us -> 397 us
  matrix products: 329 us -> 156 us
  other arithmetic: 120 us -> 46.5 us
  Pallas kernels: 0 us -> 55.8 us
  starting transfers between devices: 7.45 us -> 62.7 us
  local copies, waits for them, and re-layouts: 40.3 us -> 68.1 us
    reduce_scatter x3 -> x0, waiting for transfers between devices: 555 us -> none  [the longest x1 372 us: on_device(): lax.psum_scatter(grad_ffn_full, ('fsdp', 'ctx'), scatter_dimension=1, til...]
    all_gather x3 -> x2, waiting for transfers between devices: 392 us -> 55.4 us  [gathered(): return lax.all_gather(weight, ('fsdp', 'ctx'), axis=0, tiled=True)]
    psum x3 -> x0, waiting for transfers between devices: 252 us -> none  [the longest x1 119 us: on_device(): lax.psum(down_part.astype(jnp.bfloat16), 'tp').astype(jnp.float32)]
    ppermute x10 -> x42, waiting for transfers between devices: 53.4 us -> 304 us  [the longest x7 143 us: chip_shift(): lax.ppermute(value, 'ctx', [(i, (i + 2 * by) % size) for i in range(size)])]
    dot_general x43 -> x30, matrix products: 329 us -> 156 us  [mm(): lax.dot_general(a, b, (contract, ((), ())), preferred_element_type=f32)]
    ppermute x10 -> x42, starting transfers between devices: 6.47 us -> 62.6 us  [the longest x18 49.7 us: group_shift(): lax.ppermute(value, 'fsdp', [(i, (i + by) % size) for i in range(size)])]
    pallas_call x0 -> x2, Pallas kernels: none -> 55.8 us  [the longest x1 30.5 us: attention_backward(): pl.pallas_call(functools.partial(backward_kernel, count, blocks), grid_sp...]
    reduce_sum x21 -> x4, other arithmetic: 55.9 us -> 6.69 us  [the longest x1 3.84 us: on_device(): gain_one = jnp.sum(d_one * (layer_input * scale_one), axis=0)]
  transfers between devices with their start and end apart: 20 -> 45, of which waited for: 15 -> 17; matrix products, arithmetic and copies ran while one was open for 16% -> 32% of each run, Pallas kernels for 0% -> 7%
where the time goes in v1:
time: 807 us; the launch traced here: 802 us
  waiting for transfers between devices  397 us (49%)
  matrix products  156 us (19%)
  local copies, waits for them, and re-layouts  68.1 us (8%)
  starting transfers between devices  62.7 us (8%)
  Pallas kernels  55.8 us (7%)
  other arithmetic  46.5 us (6%)
  between operations  15.1 us (2%)
    dot_general x30, matrix products, mm(): lax.dot_general(a, b, (contract, ((), ())), preferred_element_type=f32)  156 us
    ppermute x7, waiting for transfers between devices, chip_shift(): lax.ppermute(value, 'ctx', [(i, (i + 2 * by) % size) for i in range(size)])  143 us
    ppermute x4, waiting for transfers between devices, tp_sum(): other = lax.ppermute(part, 'tp', [(0, 1), (1, 0)])  109 us
    all_gather x2, waiting for transfers between devices, gathered(): return lax.all_gather(weight, ('fsdp', 'ctx'), axis=0, tiled=True)  55.4 us
    ppermute x18, waiting for transfers between devices, group_shift(): lax.ppermute(value, 'fsdp', [(i, (i + by) % size) for i in range(size)])  50.3 us
    ppermute x18, starting transfers between devices, group_shift(): lax.ppermute(value, 'fsdp', [(i, (i + by) % size) for i in range(size)])  49.7 us
    unnamed x4, waiting for transfers between devices  37.8 us
    pallas_call x1, Pallas kernels, attention_backward(): pl.pallas_call(functools.partial(backward_kernel, count, blocks), grid_sp...  30.5 us
  transfers between devices with their start and end apart: 45, of which 17 were waited for; matrix products, arithmetic and copies ran while one was open for 32% of the time, Pallas kernels for 7%

profile of v1, /device:TPU:0, one launch (start us, length us, event | category | flops | bytes accessed | tf_op | source)
XLA Modules:
  0.0 802.0 jit_solution(1776904411983247713)
XLA Ops:
  13.7 5.1 collective-permute-start.2
  24.9 55.4 %all-gather.3.cloned.1.call-done = bf16[1536,2304]{1,0:T(8,128)(2,1)} async-done(((bf16[96,2304]{1,0:T(8,128)(2,1)}), bf16[1536,2304]{1,0:T(8,128)(2,1)}) %all-gather.3.cloned.1.call-update) | async-done | bytes 7077904 | tf_op jit(solution)/shard_map/all_gather | solution.py:336
  85.1 6.9 copy.28
  92.0 5.9 fusion.50
  100.2 53.4 %collective-permute-done.4.rest_2_ = bf16[4,2,96,768]{3,2,1,0:T(8,128)(2,1)S(1)} collective-permute-done((bf16[4,2,96,768]{3,2,1,0:T(8,128)(2,1)S(1)}, bf16[4,2,96,768]{3,2,1,0:T(8,128)(2,1)S(1)}, u32[]{:S(2)}, u32[]{:S(2)}) %collective-permute-start.4) | collective-permute-done | bytes 1179680 | tf_op jit(solution)/shard_map/ppermute | solution.py:229
  162.6 25.3 %attention_forward.1 = (bf16[4,2,96,768]{3,2,1,0:T(8,128)(2,1)S(1)}, f32[4,2,768]{2,1,0:T(2,128)S(1)}) custom-call(s32[6]{0:T(128)S(1)} %and_select_fusion.starts_ref, s32[4]{0:T(128)S(1)} %pad_add_fusion.stripes_ref, s32[1,768]{1,0:T(1,128)S(1)} %multiply_add_fusion.3.place_q_ref, s32[1,768]{1,0:T(1,128)S(1)} %broadcast_in_dim.11.start_q_ref, ...), custom_call_target="tpu_custom_call" | custom-call | flops 3221225472 | bytes 8388608 | tf_op jit(solution)/shard_map/attention_forward/pallas_call | solution.py:166
  188.0 5.6 convolution_convert_fusion
  200.2 47.3 %collective-permute-done.6 = bf16[768,1536]{1,0:T(8,128)(2,1)} collective-permute-done((bf16[768,1536]{1,0:T(8,128)(2,1)}, bf16[768,1536]{1,0:T(8,128)(2,1)}, u32[]{:S(2)}, u32[]{:S(2)}) %collective-permute-start.6) | collective-permute-done | bytes 2359328 | tf_op jit(solution)/shard_map/ppermute | solution.py:242
  266.8 9.8 %fusion.12 = f32[2048,768]{0,1:T(8,128)} fusion(bf16[1536,6144]{1,0:T(8,128)(2,1)} %all-gather.5.cloned.1.call-done, bf16[1,768,1536]{2,1,0:T(8,128)(2,1)S(1)} %copy-done.27), kind=kOutput, calls=%fused_computation.18 | convolution fusion | flops 4831838208 | bytes 14942208 | tf_op jit(solution)/shard_map/dot_general | solution.py:27
  276.6 10.3 %fusion.22 = f32[768,2048]{1,0:T(8,128)} fusion(bf16[1536,6144]{1,0:T(8,128)(2,1)} %all-gather.5.cloned.1.call-done, f32[768,1536]{1,0:T(8,128)} %copy-done.14, f32[1536]{0:T(1024)S(1)} %copy-done.54, f32[768]{0:T(1024)S(1)} %copy-done.58), kind=kOutput, calls=%fused_computation.28 | convolution fusion | flops 4835377152 | bytes 17310720 | tf_op jit(solution)/shard_map/dot_general | solution.py:27
  286.9 14.0 %fusion.2 = (bf16[768,2048]{1,0:T(8,128)(2,1)}, bf16[768,2048]{1,0:T(8,128)(2,1)}, bf16[768,2048]{1,0:T(8,128)(2,1)}) fusion(f32[2048,768]{0,1:T(8,128)} %fusion.12, f32[768,2048]{1,0:T(8,128)} %fusion.22, bf16[1536,6144]{1,0:T(8,128)(2,1)} %all-gather.5.cloned.1.call-done, f32[768,1536]{1,0:T(8,128)S(1)} %bitcast.276, f32[1536]{0:T(1024)S(1)} %copy-done.54, ...), kind=kOutput, calls=%fused_computation.4 | convolution fusion | flops 4858970112 | bytes 33039360 | tf_op jit(solution)/shard_map/dot_general | solution.py:27
  301.1 8.2 %fusion.16 = f32[768,1536]{1,0:T(8,128)S(1)} fusion(bf16[768,2048]{1,0:T(8,128)(2,1)} %get-tuple-element.31, bf16[1536,6144]{1,0:T(8,128)(2,1)} %all-gather.5.cloned.1.call-done), kind=kOutput, calls=%fused_computation.22 | convolution fusion | flops 4831838208 | bytes 14155776 | tf_op jit(solution)/shard_map/dot_general | solution.py:27
  309.2 8.7 %add_convert_fusion = bf16[768,1536]{1,0:T(8,128)(2,1)S(1)} fusion(f32[768,1536]{1,0:T(8,128)S(1)} %fusion.16, bf16[768,2048]{1,0:T(8,128)(2,1)} %get-tuple-element.30, bf16[1536,6144]{1,0:T(8,128)(2,1)} %all-gather.5.cloned.1.call-done), kind=kOutput, calls=%fused_computation.46 | convolution fusion | flops 4834197504 | bytes 16515072 | tf_op jit(solution)/shard_map/dot_general | solution.py:27
  319.6 8.2 %fusion.43 = bf16[768,1536]{1,0:T(8,128)(2,1)S(1)} fusion(bf16[768,2048]{1,0:T(8,128)(2,1)} %get-tuple-element.32, bf16[1536,6144]{1,0:T(8,128)(2,1)} %all-gather.5.cloned.1.call-done), kind=kOutput, calls=%fused_computation.58 | convolution fusion | flops 4833017856 | bytes 11796480 | tf_op jit(solution)/shard_map/dot_general | solution.py:27
  358.3 13.8 %collective-permute-done.8 = bf16[768,1536]{1,0:T(8,128)(2,1)S(1)} collective-permute-done((bf16[768,1536]{1,0:T(8,128)(2,1)S(1)}, bf16[768,1536]{1,0:T(8,128)(2,1)S(1)}, u32[]{:S(2)}, u32[]{:S(2)}) %collective-permute-start.8) | collective-permute-done | bytes 2359328 | tf_op jit(solution)/shard_map/ppermute | solution.py:242
  374.2 47.9 %collective-permute-done.7 = bf16[768,1536]{1,0:T(8,128)(2,1)S(1)} collective-permute-done((bf16[768,1536]{1,0:T(8,128)(2,1)S(1)}, bf16[768,1536]{1,0:T(8,128)(2,1)S(1)}, u32[]{:S(2)}, u32[]{:S(2)}) %collective-permute-start.7) | collective-permute-done | bytes 2359328 | tf_op jit(solution)/shard_map/ppermute | solution.py:242
  427.0 6.4 fusion.61
  433.5 30.5 %attention_backward.1 = (f32[4,2,96,768]{3,2,1,0:T(8,128)}, bf16[4,2,96,768]{3,2,1,0:T(8,128)(2,1)S(1)}, bf16[4,2,96,768]{3,2,1,0:T(8,128)(2,1)}, bf16[4,2,96,76...) custom-call(s32[6]{0:T(128)S(1)} %and_select_fusion.starts_ref, s32[4]{0:T(128)S(1)} %pad_add_fusion.stripes_ref, ...), custom_call_target="tpu_custom_call" | custom-call | flops 8589934592 | bytes 16777216 | tf_op jit(solution)/shard_map/attention_backward/pallas_call | solution.py:195
  472.3 5.7 add_convert_fusion.3
  501.3 11.8 %collective-permute-done.21 = bf16[384,768]{1,0:T(8,128)(2,1)S(1)} collective-permute-done((bf16[384,768]{1,0:T(8,128)(2,1)S(1)}, bf16[384,768]{1,0:T(8,128)(2,1)S(1)}, u32[]{:S(2)}, u32[]{:S(2)}) %collective-permute-start.21) | collective-permute-done | bytes 589856 | tf_op jit(solution)/shard_map/ppermute | solution.py:229
  513.9 11.4 %collective-permute-start.24 = (bf16[96,768]{1,0:T(8,128)(2,1)S(1)}, bf16[96,768]{1,0:T(8,128)(2,1)S(1)}, u32[]{:S(2)}, u32[]{:S(2)}) collective-permute-start(bf16[96,768]{1,0:T(8,128)(2,1)S(1)} %get-tuple-element.71), channel_id=1, source_target_pairs={{0,24},{8,0},{16,8},{24,16},{1,25},{9,1},{17,9},{25,17},{2,26},{10... | collective-permute-start | bytes 442376 | tf_op jit(solution)/shard_map/ppermute | solution.py:234
  530.3 5.3 collective-permute-done.23
  544.2 6.2 fusion.40
  552.0 20.0 %collective-permute-done.38 = bf16[384,2048]{1,0:T(8,128)(2,1)S(1)} collective-permute-done((bf16[384,2048]{1,0:T(8,128)(2,1)}, bf16[384,2048]{1,0:T(8,128)(2,1)S(1)}, u32[]{:S(2)}, u32[]{:S(2)}) %collective-permute-start.38) | collective-permute-done | bytes 1572896 | tf_op jit(solution)/shard_map/ppermute | solution.py:229
  575.3 11.4 %collective-permute-start.41 = (bf16[96,2048]{1,0:T(8,128)(2,1)}, bf16[96,2048]{1,0:T(8,128)(2,1)}, u32[]{:S(2)}, u32[]{:S(2)}) collective-permute-start(bf16[96,2048]{1,0:T(8,128)(2,1)} %get-tuple-element.57), channel_id=1, source_target_pairs={{0,24},{8,0},{16,8},{24,16},{1,25},{9,1},{17,9},{25,17},{2,26},{10... | collective-permute-start | bytes 1179656 | tf_op jit(solution)/shard_map/ppermute | solution.py:234
  586.7 19.1 %collective-permute-done.32 = bf16[384,2048]{1,0:T(8,128)(2,1)S(1)} collective-permute-done((bf16[384,2048]{1,0:T(8,128)(2,1)}, bf16[384,2048]{1,0:T(8,128)(2,1)S(1)}, u32[]{:S(2)}, u32[]{:S(2)}) %collective-permute-start.32) | collective-permute-done | bytes 1572896 | tf_op jit(solution)/shard_map/ppermute | solution.py:229
  608.3 30.8 %collective-permute-done.27 = bf16[384,2048]{1,0:T(8,128)(2,1)S(1)} collective-permute-done((bf16[384,2048]{1,0:T(8,128)(2,1)}, bf16[384,2048]{1,0:T(8,128)(2,1)S(1)}, u32[]{:S(2)}, u32[]{:S(2)}) %collective-permute-start.27) | collective-permute-done | bytes 1572896 | tf_op jit(solution)/shard_map/ppermute | solution.py:229
  643.6 10.9 %collective-permute-start.35 = (bf16[96,2048]{1,0:T(8,128)(2,1)}, bf16[96,2048]{1,0:T(8,128)(2,1)}, u32[]{:S(2)}, u32[]{:S(2)}) collective-permute-start(bf16[96,2048]{1,0:T(8,128)(2,1)} %get-tuple-element.54), channel_id=1, source_target_pairs={{0,24},{8,0},{16,8},{24,16},{1,25},{9,1},{17,9},{25,17},{2,26},{10... | collective-permute-start | bytes 1179656 | tf_op jit(solution)/shard_map/ppermute | solution.py:234
  670.7 34.4 %collective-permute-done.34 = bf16[96,2048]{1,0:T(8,128)(2,1)S(1)} collective-permute-done((bf16[96,2048]{1,0:T(8,128)(2,1)S(1)}, bf16[96,2048]{1,0:T(8,128)(2,1)S(1)}, u32[]{:S(2)}, u32[]{:S(2)}) %collective-permute-start.34) | collective-permute-done | bytes 393248 | tf_op jit(solution)/shard_map/ppermute | solution.py:234
  716.1 9.9 %collective-permute-done.29 = bf16[96,2048]{1,0:T(8,128)(2,1)S(1)} collective-permute-done((bf16[96,2048]{1,0:T(8,128)(2,1)S(1)}, bf16[96,2048]{1,0:T(8,128)(2,1)S(1)}, u32[]{:S(2)}, u32[]{:S(2)}) %collective-permute-start.29) | collective-permute-done | bytes 393248 | tf_op jit(solution)/shard_map/ppermute | solution.py:234
  733.2 8.3 %collective-permute-done.15 = bf16[384,1536]{1,0:T(8,128)(2,1)} collective-permute-done((bf16[384,1536]{1,0:T(8,128)(2,1)}, bf16[384,1536]{1,0:T(8,128)(2,1)}, u32[]{:S(2)}, u32[]{:S(2)}) %collective-permute-start.15) | collective-permute-done | bytes 1179680 | tf_op jit(solution)/shard_map/ppermute | solution.py:229
  753.7 37.8 %reduce-scatter.4.cloned.1.call-done = f32[96,2]{1,0:T(8,128)} async-done(((f32[1536,2]{1,0:T(8,128)}), f32[96,2]{1,0:T(8,128)}) %reduce-scatter.4.cloned.1.call-update) | async-done | bytes 784
  (338 shorter events, 201.2 us)
Async XLA Ops:
  7.2 73.1 %all-gather.3.cloned.1.call-start = ((), (), s32[]{:S(2)}) async-start(), calls=%async_computation.1 | async-start | bytes 7520256 | tf_op jit(solution)/shard_map/all_gather | solution.py:336
  9.4 257.4 %all-gather.5.cloned.1.call-start = ((), (), s32[]{:S(2)}) async-start(), calls=%async_computation.2 | async-start | bytes 20054016 | tf_op jit(solution)/shard_map/all_gather | solution.py:336
  13.6 777.8 %reduce-scatter.4.cloned.1.call-start = ((), (), s32[]{:S(2)}) async-start(), calls=%async_computation.3 | async-start | bytes 835584
  99.7 53.9 %collective-permute-start.4 = (bf16[4,2,96,768]{3,2,1,0:T(8,128)(2,1)S(1)}, bf16[4,2,96,768]{3,2,1,0:T(8,128)(2,1)S(1)}, u32[]{:S(2)}, u32[]{:S(2)}) collective-permute-start(bf16[4,2,96,768]{3,2,1,0:T(8,128)(2,1)S(1)} %pad_maximum_fusion.2.rest_0_), channel_id=1, source_target_pairs={{0,4},{2,6},{4,0},{6,2},{1,5},{3,7},{5,1},{7,3},{8,12},{10,14},{12... | collective-permute-start | bytes 3538952 | tf_op jit(solution)/shard_map/ppermute | solution.py:229
  100.2 60.1 %collective-permute-start.3 = (bf16[4,2,96,768]{3,2,1,0:T(8,128)(2,1)S(1)}, bf16[4,2,96,768]{3,2,1,0:T(8,128)(2,1)S(1)}, u32[]{:S(2)}, u32[]{:S(2)}) collective-permute-start(bf16[4,2,96,768]{3,2,1,0:T(8,128)(2,1)S(1)} %pad_maximum_fusion.2.rest_0_), channel_id=1, source_target_pairs={{0,2},{2,0},{4,6},{6,4},{1,3},{3,1},{5,7},{7,5},{8,10},{10,8},{12,... | collective-permute-start | bytes 3538952 | tf_op jit(solution)/shard_map/ppermute | solution.py:224
  193.6 53.9 %collective-permute-start.6 = (bf16[768,1536]{1,0:T(8,128)(2,1)}, bf16[768,1536]{1,0:T(8,128)(2,1)}, u32[]{:S(2)}, u32[]{:S(2)}) collective-permute-start(bf16[768,1536]{1,0:T(8,128)(2,1)} %convolution_convert_fusion), channel_id=1, source_target_pairs={{0,1},{1,0},{2,3},{3,2},{4,5},{5,4},{6,7},{7,6},{8,9},{9,8},{10,11... | collective-permute-start | bytes 7077896 | tf_op jit(solution)/shard_map/ppermute | solution.py:242
  200.1 62.0 %collective-permute-start.36 = (bf16[4,2,96,768]{3,2,1,0:T(8,128)(2,1)}, bf16[4,2,96,768]{3,2,1,0:T(8,128)(2,1)}, u32[]{:S(2)}, u32[]{:S(2)}) collective-permute-start(bf16[4,2,96,768]{3,2,1,0:T(8,128)(2,1)} %dynamic-slice_bitcast_fusion), channel_id=1, source_target_pairs={{0,2},{2,0},{4,6},{6,4},{1,3},{3,1},{5,7},{7,5},{8,10},{10,8},{12,... | collective-permute-start | bytes 3538952 | tf_op jit(solution)/shard_map/ppermute | solution.py:224
  258.8 235.3 %collective-permute-start.20 = (bf16[768,768]{0,1:T(8,128)(2,1)S(1)}, bf16[768,768]{0,1:T(8,128)(2,1)}, u32[]{:S(2)}, u32[]{:S(2)}) collective-permute-start(bf16[768,768]{0,1:T(8,128)(2,1)S(1)} %bitcast.270), channel_id=1, source_target_pairs={{0,2},{2,0},{4,6},{6,4},{1,3},{3,1},{5,7},{7,5},{8,10},{10,8},{12,... | collective-permute-start | bytes 3538952 | tf_op jit(solution)/shard_map/ppermute | solution.py:224
  300.9 170.6 %collective-permute-start.31 = (bf16[768,2048]{1,0:T(8,128)(2,1)}, bf16[768,2048]{1,0:T(8,128)(2,1)}, u32[]{:S(2)}, u32[]{:S(2)}) collective-permute-start(bf16[768,2048]{1,0:T(8,128)(2,1)} %get-tuple-element.31), channel_id=1, source_target_pairs={{0,2},{2,0},{4,6},{6,4},{1,3},{3,1},{5,7},{7,5},{8,10},{10,8},{12,... | collective-permute-start | bytes 9437192 | tf_op jit(solution)/shard_map/ppermute | solution.py:224
  317.9 54.1 %collective-permute-start.8 = (bf16[768,1536]{1,0:T(8,128)(2,1)S(1)}, bf16[768,1536]{1,0:T(8,128)(2,1)S(1)}, u32[]{:S(2)}, u32[]{:S(2)}) collective-permute-start(bf16[768,1536]{1,0:T(8,128)(2,1)S(1)} %add_convert_fusion), channel_id=1, source_target_pairs={{0,1},{1,0},{2,3},{3,2},{4,5},{5,4},{6,7},{7,6},{8,9},{9,8},{10,11... | collective-permute-start | bytes 7077896 | tf_op jit(solution)/shard_map/ppermute | solution.py:242
  319.5 163.4 %collective-permute-start.37 = (bf16[768,2048]{1,0:T(8,128)(2,1)}, bf16[768,2048]{1,0:T(8,128)(2,1)}, u32[]{:S(2)}, u32[]{:S(2)}) collective-permute-start(bf16[768,2048]{1,0:T(8,128)(2,1)} %get-tuple-element.32), channel_id=1, source_target_pairs={{0,2},{2,0},{4,6},{6,4},{1,3},{3,1},{5,7},{7,5},{8,10},{10,8},{12,... | collective-permute-start | bytes 9437192 | tf_op jit(solution)/shard_map/ppermute | solution.py:224
  327.8 94.3 %collective-permute-start.7 = (bf16[768,1536]{1,0:T(8,128)(2,1)S(1)}, bf16[768,1536]{1,0:T(8,128)(2,1)S(1)}, u32[]{:S(2)}, u32[]{:S(2)}) collective-permute-start(bf16[768,1536]{1,0:T(8,128)(2,1)S(1)} %fusion.43), channel_id=1, source_target_pairs={{0,1},{1,0},{2,3},{3,2},{4,5},{5,4},{6,7},{7,6},{8,9},{9,8},{10,11... | collective-permute-start | bytes 7077896 | tf_op jit(solution)/shard_map/ppermute | solution.py:242
  372.1 105.9 %collective-permute-start.26 = (bf16[768,2048]{1,0:T(8,128)(2,1)}, bf16[768,2048]{1,0:T(8,128)(2,1)}, u32[]{:S(2)}, u32[]{:S(2)}) collective-permute-start(bf16[768,2048]{1,0:T(8,128)(2,1)} %get-tuple-element.30), channel_id=1, source_target_pairs={{0,2},{2,0},{4,6},{6,4},{1,3},{3,1},{5,7},{7,5},{8,10},{10,8},{12,... | collective-permute-start | bytes 9437192 | tf_op jit(solution)/shard_map/ppermute | solution.py:224
  465.1 73.4 %collective-permute-start.11 = (bf16[4,2,96,768]{3,2,1,0:T(8,128)(2,1)}, bf16[4,2,96,768]{3,2,1,0:T(8,128)(2,1)}, u32[]{:S(2)}, u32[]{:S(2)}) collective-permute-start(bf16[4,2,96,768]{3,2,1,0:T(8,128)(2,1)} %get-tuple-element.19), channel_id=1, source_target_pairs={{0,2},{2,0},{4,6},{6,4},{1,3},{3,1},{5,7},{7,5},{8,10},{10,8},{12,... | collective-permute-start | bytes 3538952 | tf_op jit(solution)/shard_map/ppermute | solution.py:224
  471.8 25.6 %collective-permute-start.9 = (bf16[4,2,96,768]{3,2,1,0:T(8,128)(2,1)S(1)}, bf16[4,2,96,768]{3,2,1,0:T(8,128)(2,1)S(1)}, u32[]{:S(2)}, u32[]{:S(2)}) collective-permute-start(bf16[4,2,96,768]{3,2,1,0:T(8,128)(2,1)S(1)} %copy-done.11), channel_id=1, source_target_pairs={{0,2},{2,0},{4,6},{6,4},{1,3},{3,1},{5,7},{7,5},{8,10},{10,8},{12,... | collective-permute-start | bytes 3538952 | tf_op jit(solution)/shard_map/ppermute | solution.py:224
  497.8 40.7 %collective-permute-start.10 = (bf16[4,2,96,768]{3,2,1,0:T(8,128)(2,1)S(1)}, bf16[4,2,96,768]{3,2,1,0:T(8,128)(2,1)S(1)}, u32[]{:S(2)}, u32[]{:S(2)}) collective-permute-start(bf16[4,2,96,768]{3,2,1,0:T(8,128)(2,1)S(1)} %add_convert_fusion.5), channel_id=1, source_target_pairs={{0,4},{2,6},{4,0},{6,2},{1,5},{3,7},{5,1},{7,3},{8,12},{10,14},{12... | collective-permute-start | bytes 3538952 | tf_op jit(solution)/shard_map/ppermute | solution.py:229
  529.6 42.4 %collective-permute-start.38 = (bf16[384,2048]{1,0:T(8,128)(2,1)}, bf16[384,2048]{1,0:T(8,128)(2,1)S(1)}, u32[]{:S(2)}, u32[]{:S(2)}) collective-permute-start(bf16[384,2048]{1,0:T(8,128)(2,1)} %add_convert_fusion.2), channel_id=1, source_target_pairs={{0,4},{2,6},{4,0},{6,2},{1,5},{3,7},{5,1},{7,3},{8,12},{10,14},{12... | collective-permute-start | bytes 4718600 | tf_op jit(solution)/shard_map/ppermute | solution.py:229
  535.6 70.2 %collective-permute-start.32 = (bf16[384,2048]{1,0:T(8,128)(2,1)}, bf16[384,2048]{1,0:T(8,128)(2,1)S(1)}, u32[]{:S(2)}, u32[]{:S(2)}) collective-permute-start(bf16[384,2048]{1,0:T(8,128)(2,1)} %add_convert_fusion.3), channel_id=1, source_target_pairs={{0,4},{2,6},{4,0},{6,2},{1,5},{3,7},{5,1},{7,3},{8,12},{10,14},{12... | collective-permute-start | bytes 4718600 | tf_op jit(solution)/shard_map/ppermute | solution.py:229
  536.3 102.7 %collective-permute-start.27 = (bf16[384,2048]{1,0:T(8,128)(2,1)}, bf16[384,2048]{1,0:T(8,128)(2,1)S(1)}, u32[]{:S(2)}, u32[]{:S(2)}) collective-permute-start(bf16[384,2048]{1,0:T(8,128)(2,1)} %add_convert_fusion.4), channel_id=1, source_target_pairs={{0,4},{2,6},{4,0},{6,2},{1,5},{3,7},{5,1},{7,3},{8,12},{10,14},{12... | collective-permute-start | bytes 4718600 | tf_op jit(solution)/shard_map/ppermute | solution.py:229
  550.4 93.2 %collective-permute-start.12 = (bf16[768,1536]{1,0:T(8,128)(2,1)S(1)}, bf16[768,1536]{1,0:T(8,128)(2,1)S(1)}, u32[]{:S(2)}, u32[]{:S(2)}) collective-permute-start(bf16[768,1536]{1,0:T(8,128)(2,1)S(1)} %fusion.40), channel_id=1, source_target_pairs={{0,1},{1,0},{2,3},{3,2},{4,5},{5,4},{6,7},{7,6},{8,9},{9,8},{10,11... | collective-permute-start | bytes 7077896 | tf_op jit(solution)/shard_map/ppermute | solution.py:242
  552.0 159.5 %collective-permute-start.14 = (bf16[768,1536]{0,1:T(8,128)(2,1)}, bf16[768,1536]{0,1:T(8,128)(2,1)}, u32[]{:S(2)}, u32[]{:S(2)}) collective-permute-start(bf16[768,1536]{0,1:T(8,128)(2,1)} %bitcast.42), channel_id=1, source_target_pairs={{0,2},{2,0},{4,6},{6,4},{1,3},{3,1},{5,7},{7,5},{8,10},{10,8},{12,... | collective-permute-start | bytes 7077896 | tf_op jit(solution)/shard_map/ppermute | solution.py:224
  575.3 88.9 %collective-permute-start.41 = (bf16[96,2048]{1,0:T(8,128)(2,1)}, bf16[96,2048]{1,0:T(8,128)(2,1)}, u32[]{:S(2)}, u32[]{:S(2)}) collective-permute-start(bf16[96,2048]{1,0:T(8,128)(2,1)} %get-tuple-element.57), channel_id=1, source_target_pairs={{0,24},{8,0},{16,8},{24,16},{1,25},{9,1},{17,9},{25,17},{2,26},{10... | collective-permute-start | bytes 1179656 | tf_op jit(solution)/shard_map/ppermute | solution.py:234
  605.8 59.1 %collective-permute-start.40 = (bf16[96,2048]{1,0:T(8,128)(2,1)S(1)}, bf16[96,2048]{1,0:T(8,128)(2,1)}, u32[]{:S(2)}, u32[]{:S(2)}) collective-permute-start(bf16[96,2048]{1,0:T(8,128)(2,1)S(1)} %get-tuple-element.58), channel_id=1, source_target_pairs={{0,16},{8,24},{16,0},{24,8},{1,17},{9,25},{17,1},{25,9},{2,18},{10... | collective-permute-start | bytes 1179656 | tf_op jit(solution)/shard_map/ppermute | solution.py:234
  639.0 27.8 %collective-permute-start.39 = (bf16[96,2048]{1,0:T(8,128)(2,1)S(1)}, bf16[96,2048]{1,0:T(8,128)(2,1)}, u32[]{:S(2)}, u32[]{:S(2)}) collective-permute-start(bf16[96,2048]{1,0:T(8,128)(2,1)S(1)} %get-tuple-element.56), channel_id=1, source_target_pairs={{0,8},{8,16},{16,24},{24,0},{1,9},{9,17},{17,25},{25,1},{2,10},{10... | collective-permute-start | bytes 1179656 | tf_op jit(solution)/shard_map/ppermute | solution.py:234
  664.2 40.9 %collective-permute-start.34 = (bf16[96,2048]{1,0:T(8,128)(2,1)S(1)}, bf16[96,2048]{1,0:T(8,128)(2,1)S(1)}, u32[]{:S(2)}, u32[]{:S(2)}) collective-permute-start(bf16[96,2048]{1,0:T(8,128)(2,1)S(1)} %copy-done.52), channel_id=1, source_target_pairs={{0,16},{8,24},{16,0},{24,8},{1,17},{9,25},{17,1},{25,9},{2,18},{10... | collective-permute-start | bytes 1179656 | tf_op jit(solution)/shard_map/ppermute | solution.py:234
  664.9 40.2 %collective-permute-start.33 = (bf16[96,2048]{1,0:T(8,128)(2,1)}, bf16[96,2048]{1,0:T(8,128)(2,1)S(1)}, u32[]{:S(2)}, u32[]{:S(2)}) collective-permute-start(bf16[96,2048]{1,0:T(8,128)(2,1)} %get-tuple-element.53), channel_id=1, source_target_pairs={{0,8},{8,16},{16,24},{24,0},{1,9},{9,17},{17,25},{25,1},{2,10},{10... | collective-permute-start | bytes 1179656 | tf_op jit(solution)/shard_map/ppermute | solution.py:234
  666.9 43.7 %collective-permute-start.13 = (bf16[4,2,96,768]{3,2,1,0:T(8,128)(2,1)S(1)}, bf16[4,2,96,768]{3,2,1,0:T(8,128)(2,1)S(1)}, u32[]{:S(2)}, u32[]{:S(2)}) collective-permute-start(bf16[4,2,96,768]{3,2,1,0:T(8,128)(2,1)S(1)} %dynamic-slice_bitcast_fusion.3), channel_id=1, source_target_pairs={{0,2},{2,0},{4,6},{6,4},{1,3},{3,1},{5,7},{7,5},{8,10},{10,8},{12,... | collective-permute-start | bytes 3538952 | tf_op jit(solution)/shard_map/ppermute | solution.py:224
  668.6 47.5 %collective-permute-start.30 = (bf16[96,2048]{1,0:T(8,128)(2,1)S(1)}, bf16[96,2048]{1,0:T(8,128)(2,1)S(1)}, u32[]{:S(2)}, u32[]{:S(2)}) collective-permute-start(bf16[96,2048]{1,0:T(8,128)(2,1)S(1)} %copy-done.51), channel_id=1, source_target_pairs={{0,24},{8,0},{16,8},{24,16},{1,25},{9,1},{17,9},{25,17},{2,26},{10... | collective-permute-start | bytes 1179656 | tf_op jit(solution)/shard_map/ppermute | solution.py:234
  715.3 26.2 %collective-permute-start.15 = (bf16[384,1536]{1,0:T(8,128)(2,1)}, bf16[384,1536]{1,0:T(8,128)(2,1)}, u32[]{:S(2)}, u32[]{:S(2)}) collective-permute-start(bf16[384,1536]{1,0:T(8,128)(2,1)} %fusion.47), channel_id=1, source_target_pairs={{0,4},{2,6},{4,0},{6,2},{1,5},{3,7},{5,1},{7,3},{8,12},{10,14},{12... | collective-permute-start | bytes 3538952 | tf_op jit(solution)/shard_map/ppermute | solution.py:229
  746.5 46.4 %collective-permute-start.18 = (bf16[96,1536]{1,0:T(8,128)(2,1)}, bf16[96,1536]{1,0:T(8,128)(2,1)}, u32[]{:S(2)}, u32[]{:S(2)}) collective-permute-start(bf16[96,1536]{1,0:T(8,128)(2,1)} %get-tuple-element.66), channel_id=1, source_target_pairs={{0,24},{8,0},{16,8},{24,16},{1,25},{9,1},{17,9},{25,17},{2,26},{10... | collective-permute-start | bytes 884744 | tf_op jit(solution)/shard_map/ppermute | solution.py:234
  746.5 46.4 %collective-permute-start.17 = (bf16[96,1536]{1,0:T(8,128)(2,1)}, bf16[96,1536]{1,0:T(8,128)(2,1)}, u32[]{:S(2)}, u32[]{:S(2)}) collective-permute-start(bf16[96,1536]{1,0:T(8,128)(2,1)} %get-tuple-element.67), channel_id=1, source_target_pairs={{0,16},{8,24},{16,0},{24,8},{1,17},{9,25},{17,1},{25,9},{2,18},{10... | collective-permute-start | bytes 884744 | tf_op jit(solution)/shard_map/ppermute | solution.py:234
  750.4 42.5 %collective-permute-start.16 = (bf16[96,1536]{1,0:T(8,128)(2,1)}, bf16[96,1536]{1,0:T(8,128)(2,1)}, u32[]{:S(2)}, u32[]{:S(2)}) collective-permute-start(bf16[96,1536]{1,0:T(8,128)(2,1)} %get-tuple-element.65), channel_id=1, source_target_pairs={{0,8},{8,16},{16,24},{24,0},{1,9},{9,17},{17,25},{25,1},{2,10},{10... | collective-permute-start | bytes 884744 | tf_op jit(solution)/shard_map/ppermute | solution.py:234
  (91 other events, 1465.3 us)
Sparse Core Ops, SparseCore 0:
  10.9 69.3 all-gather.2
  82.4 122.4 all-gather.4
  730.3 61.0 reduce-scatter.3

commit v2 on v1

--- a/solution.py
+++ b/solution.py
@@ -12,12 +12,15 @@
 QUERY_PER_KV = 2
 HALF = HEAD_SIZE // 2
 BLOCK = 128
+CHUNKS = 2
 
 norm_eps = 1e-05
 rope_base = 100000.0
 masked_score = -1e30
 SCORE_SCALE = HEAD_SIZE ** (-0.5)
 SCORE_SCALE_2 = SCORE_SCALE * math.log2(math.e)
+
+SMALL_COST = pl.CostEstimate(flops=1, bytes_accessed=1, transcendentals=0)
 
 bf16 = jnp.bfloat16
 f32 = jnp.float32
@@ -181,7 +184,7 @@
             jax.ShapeDtypeStruct((heads, QUERY_PER_KV, tokens), f32),
         ],
         compiler_params=pltpu.CompilerParams(vmem_limit_bytes=40 << 20),
-        cost_estimate=pl.CostEstimate(flops=3 << 30, bytes_accessed=8 << 20, transcendentals=8 << 20),
+        cost_estimate=SMALL_COST,
         name="attention_forward",
     )(starts, stripes, place, start, queries, *pieces)
 
@@ -214,9 +217,407 @@
         out_shape=[jax.ShapeDtypeStruct(queries.shape, f32)]
         + [jax.ShapeDtypeStruct(pieces[0].shape, bf16)] * count,
         compiler_params=pltpu.CompilerParams(vmem_limit_bytes=48 << 20),
-        cost_estimate=pl.CostEstimate(flops=8 << 30, bytes_accessed=16 << 20, transcendentals=8 << 20),
+        cost_estimate=SMALL_COST,
         name="attention_backward",
     )(starts, stripes, place, start, queries, d_att, attended, lse, *pieces)
+
+
+def pack_kernel(_, ffn_ref, out_ref, other_ref, packed_ref):
+    units, columns = ffn_ref.shape[2], out_ref.shape[1]
+    for i in range(3):
+        packed_ref[:, i * units : (i + 1) * units] = ffn_ref[i]
+    packed_ref[:, 3 * units : 3 * units + columns] = out_ref[...]
+    packed_ref[:, 3 * units + columns :] = other_ref[...]
+
+
+def packed_share(feedforward_weight, out_share, out_other, index, share_of):
+    rows, columns = out_share.shape
+    units = feedforward_weight.shape[2]
+    if rows % 16:
+        parts = [share_of(feedforward_weight[i]) for i in range(3)]
+        return jnp.concatenate([*parts, out_share, out_other], axis=1)
+    whole = pl.BlockSpec((rows, columns), lambda n, _: (0, 0))
+    width = 3 * units + 2 * columns
+    return pl.pallas_call(
+        pack_kernel,
+        grid_spec=pltpu.PrefetchScalarGridSpec(
+            num_scalar_prefetch=1,
+            grid=(1,),
+            in_specs=[
+                pl.BlockSpec((3, rows, units), lambda n, place: (0, place[0], 0)),
+                whole,
+                whole,
+            ],
+            out_specs=pl.BlockSpec((rows, width), lambda n, _: (0, 0)),
+        ),
+        out_shape=jax.ShapeDtypeStruct((rows, width), bf16),
+        compiler_params=pltpu.CompilerParams(vmem_limit_bytes=32 << 20),
+        cost_estimate=SMALL_COST,
+        name="pack",
+    )(index[None], feedforward_weight, out_share, out_other)
+
+
+def input_gradient_kernel(mine_ref, other_ref, x_ref, d_mid_ref, gain_ref, out_ref):
+    x = x_ref[...].astype(f32)
+    scale = lax.rsqrt(jnp.mean(x * x, axis=-1, keepdims=True) + norm_eps)
+    unit = x * scale
+    weighted = (mine_ref[...].astype(f32) + other_ref[...].astype(f32)) * gain_ref[...]
+    out_ref[...] = (
+        d_mid_ref[...]
+        + scale * (weighted - unit * jnp.mean(weighted * unit, axis=-1, keepdims=True))
+    ).astype(bf16)
+
+
+def input_gradient(sent, x, d_mid, gain):
+    tokens, width = x.shape
+    block = 256
+    here = pl.BlockSpec((block, width), lambda n: (n, 0))
+    return pl.pallas_call(
+        input_gradient_kernel,
+        grid=(tokens // block,),
+        in_specs=[here] * 4 + [pl.BlockSpec((1, width), lambda n: (0, 0))],
+        out_specs=here,
+        out_shape=jax.ShapeDtypeStruct((tokens, width), bf16),
+        compiler_params=pltpu.CompilerParams(vmem_limit_bytes=32 << 20),
+        cost_estimate=SMALL_COST,
+        name="input_gradient",
+    )(*sent, x, d_mid, gain)
+
+
+def project_kernel(x_ref, w_ref, cos_ref, sin_ref, q_ref, kv_ref):
+    projected = mm(x_ref[...], w_ref[...]).T
+    cos_table, sin_table = cos_ref[...], sin_ref[...]
+    for j in range(QUERY_PER_KV + 1):
+        first = j * HEAD_SIZE
+        front = projected[first : first + HALF]
+        back = projected[first + HALF : first + HEAD_SIZE]
+        target = q_ref.at[0, j] if j < QUERY_PER_KV else kv_ref.at[0, 0]
+        target[:HALF, :] = (front * cos_table - back * sin_table).astype(bf16)
+        target[HALF:, :] = (back * cos_table + front * sin_table).astype(bf16)
+    kv_ref[0, 1] = projected[(QUERY_PER_KV + 1) * HEAD_SIZE :].astype(bf16)
+
+
+def project(normed, weight, cos_table, sin_table, first, heads):
+    tokens, width = normed.shape
+    columns = (QUERY_PER_KV + 2) * HEAD_SIZE
+    whole = lambda shape: pl.BlockSpec(shape, lambda h: (0, 0))
+    return pl.pallas_call(
+        project_kernel,
+        grid=(heads,),
+        in_specs=[
+            whole((tokens, width)),
+            pl.BlockSpec((width, columns), lambda h: (0, first + h)),
+            whole((HALF, tokens)),
+            whole((HALF, tokens)),
+        ],
+        out_specs=[
+            pl.BlockSpec((1, QUERY_PER_KV, HEAD_SIZE, tokens), lambda h: (h, 0, 0, 0)),
+            pl.BlockSpec((1, 2, HEAD_SIZE, tokens), lambda h: (h, 0, 0, 0)),
+        ],
+        out_shape=[
+            jax.ShapeDtypeStruct((heads, QUERY_PER_KV, HEAD_SIZE, tokens), bf16),
+            jax.ShapeDtypeStruct((heads, 2, HEAD_SIZE, tokens), bf16),
+        ],
+        compiler_params=pltpu.CompilerParams(vmem_limit_bytes=40 << 20),
+        cost_estimate=SMALL_COST,
+        name="project",
+    )(normed, weight, cos_table, sin_table)
+
+
+def middle_kernel(count, tp_ref, x_ref, gain_ref, *refs):
+    mine, others = refs[:count], refs[count : 2 * count]
+    w_first, w_second, middle_ref, normed_ref, first_ref, second_ref = refs[2 * count :]
+
+    def fill(first, second):
+        first_ref[...] = jnp.concatenate([r[...] for r in first], axis=0).T
+        second_ref[...] = jnp.concatenate([r[...] for r in second], axis=0).T
+
+    @pl.when(tp_ref[0] == 0)
+    def _():
+        fill(mine, others)
+
+    @pl.when(tp_ref[0] == 1)
+    def _():
+        fill(others, mine)
+
+    branch = mm(first_ref[...], w_first[...], ((1,), (1,))) + mm(
+        second_ref[...], w_second[...], ((1,), (1,))
+    )
+    middle = x_ref[...].astype(f32) + branch
+    middle_ref[...] = middle
+    scale = lax.rsqrt(jnp.mean(middle * middle, axis=-1, keepdims=True) + norm_eps)
+    normed_ref[...] = (middle * scale * gain_ref[...]).astype(bf16)
+
+
+def middle_of(mine, others, tp_index, x, gain, weight, first):
+    tokens, width = x.shape
+    features = sum(p.shape[0] for p in mine)
+    block = 256
+    half = first // features
+    token_spec = pl.BlockSpec((block, width), lambda n, _: (n, 0))
+    return pl.pallas_call(
+        functools.partial(middle_kernel, len(mine)),
+        grid_spec=pltpu.PrefetchScalarGridSpec(
+            num_scalar_prefetch=1,
+            grid=(tokens // block,),
+            in_specs=[token_spec, pl.BlockSpec((1, width), lambda n, _: (0, 0))]
+            + [pl.BlockSpec((p.shape[0], block), lambda n, _: (0, n)) for p in (*mine, *others)]
+            + [
+                pl.BlockSpec((width, features), lambda n, tp: (0, half + tp[0])),
+                pl.BlockSpec((width, features), lambda n, tp: (0, half + 1 - tp[0])),
+            ],
+            out_specs=[token_spec] * 2,
+            scratch_shapes=[pltpu.VMEM((block, features), bf16)] * 2,
+        ),
+        out_shape=[
+            jax.ShapeDtypeStruct((tokens, width), f32),
+            jax.ShapeDtypeStruct((tokens, width), bf16),
+        ],
+        compiler_params=pltpu.CompilerParams(vmem_limit_bytes=40 << 20),
+        cost_estimate=SMALL_COST,
+        name="middle",
+    )(tp_index[None], x, gain, *mine, *others, weight, weight)
+
+
+def down_kernel(a_ref, w_ref, out_ref):
+    out_ref[...] = mm(a_ref[...], w_ref[...], ((1,), (1,))).astype(bf16)
+
+
+def down_project(activated, weight, first):
+    tokens, units = activated.shape
+    width, block = weight.shape[0], 512
+    return pl.pallas_call(
+        down_kernel,
+        grid=(width // block,),
+        in_specs=[
+            pl.BlockSpec((tokens, units), lambda n: (0, 0)),
+            pl.BlockSpec((block, units), lambda n: (n, first // units)),
+        ],
+        out_specs=pl.BlockSpec((tokens, block), lambda n: (0, n)),
+        out_shape=jax.ShapeDtypeStruct((tokens, width), bf16),
+        compiler_params=pltpu.CompilerParams(vmem_limit_bytes=40 << 20),
+        cost_estimate=SMALL_COST,
+        name="down_project",
+    )(activated, weight)
+
+
+def d_middle_kernel(
+    mine_ref, other_ref, middle_ref, dy_ref, gain_ref, w_ref, d_mid_ref, branch_ref, d_att_ref
+):
+    middle = middle_ref[...]
+    scale = lax.rsqrt(jnp.mean(middle * middle, axis=-1, keepdims=True) + norm_eps)
+    unit = middle * scale
+    weighted = (mine_ref[...].astype(f32) + other_ref[...].astype(f32)) * gain_ref[...]
+    d_mid = dy_ref[...].astype(f32) + scale * (
+        weighted - unit * jnp.mean(weighted * unit, axis=-1, keepdims=True)
+    )
+    d_mid_ref[...] = d_mid
+    branch = d_mid.astype(bf16)
+    branch_ref[...] = branch
+    d_att_ref[...] = mm(branch, w_ref[...]).astype(bf16).T
+
+
+def d_middle_of(sent, middle, d_out, gain, weight, first, features):
+    mine, other = sent
+    tokens, width = middle.shape
+    block = 256
+    here = pl.BlockSpec((block, width), lambda n: (n, 0))
+    row = pl.BlockSpec((1, width), lambda n: (0, 0))
+    return pl.pallas_call(
+        d_middle_kernel,
+        grid=(tokens // block,),
+        in_specs=[here, here, here, here, row]
+        + [pl.BlockSpec((width, features), lambda n: (0, first // features))],
+        out_specs=[here, here, pl.BlockSpec((features, block), lambda n: (0, n))],
+        out_shape=[
+            jax.ShapeDtypeStruct((tokens, width), f32),
+            jax.ShapeDtypeStruct((tokens, width), bf16),
+            jax.ShapeDtypeStruct((features, tokens), bf16),
+        ],
+        compiler_params=pltpu.CompilerParams(vmem_limit_bytes=48 << 20),
+        cost_estimate=SMALL_COST,
+        name="d_middle",
+    )(mine, other, middle, d_out, gain, weight)
+
+
+def turn_back_kernel(cos_ref, sin_ref, dq_ref, *refs):
+    kv_refs, out_ref = refs[:-1], refs[-1]
+    cos_table, sin_table = cos_ref[...], sin_ref[...]
+    total = kv_refs[0][0].astype(f32)
+    for ref in kv_refs[1:]:
+        total = total + ref[0].astype(f32)
+    for j in range(QUERY_PER_KV + 1):
+        vector = dq_ref[0, j] if j < QUERY_PER_KV else total[0]
+        front, back = vector[:HALF], vector[HALF:]
+        first = j * HEAD_SIZE
+        out_ref[first : first + HALF, :] = (front * cos_table + back * sin_table).astype(bf16)
+        out_ref[first + HALF : first + HEAD_SIZE, :] = (
+            back * cos_table - front * sin_table
+        ).astype(bf16)
+    out_ref[(QUERY_PER_KV + 1) * HEAD_SIZE :, :] = total[1].astype(bf16)
+
+
+def turned_back(d_query, d_kv_terms, cos_table, sin_table):
+    heads, _, _, tokens = d_query.shape
+    columns = (QUERY_PER_KV + 2) * HEAD_SIZE
+    whole = pl.BlockSpec((HALF, tokens), lambda h: (0, 0))
+    head = lambda n: pl.BlockSpec((1, n, HEAD_SIZE, tokens), lambda h: (h, 0, 0, 0))
+    return pl.pallas_call(
+        turn_back_kernel,
+        grid=(heads,),
+        in_specs=[whole, whole, head(QUERY_PER_KV)] + [head(2)] * len(d_kv_terms),
+        out_specs=pl.BlockSpec((columns, tokens), lambda h: (h, 0)),
+        out_shape=jax.ShapeDtypeStruct((heads * columns, tokens), bf16),
+        compiler_params=pltpu.CompilerParams(vmem_limit_bytes=32 << 20),
+        cost_estimate=SMALL_COST,
+        name="turn_back",
+    )(cos_table, sin_table, d_query, *d_kv_terms)
+
+
+def d_one_kernel(count, *refs):
+    parts, w_ref, out_ref, rows_ref = refs[:count], refs[count], refs[count + 1], refs[count + 2]
+
+    @pl.when(pl.program_id(0) == 0)
+    def _():
+        first = 0
+        for part in parts:
+            columns = part.shape[0]
+            rows_ref[:, first : first + columns] = part[...].T
+            first += columns
+
+    out_ref[...] = mm(rows_ref[...], w_ref[...], ((1,), (1,))).astype(bf16)
+
+
+def d_one_of(parts, weight):
+    width, columns = weight.shape
+    tokens, block = parts[0].shape[1], 512
+    return pl.pallas_call(
+        functools.partial(d_one_kernel, len(parts)),
+        grid=(width // block,),
+        in_specs=[pl.BlockSpec(p.shape, lambda n: (0, 0)) for p in parts]
+        + [pl.BlockSpec((block, columns), lambda n: (n, 0))],
+        out_specs=pl.BlockSpec((tokens, block), lambda n: (0, n)),
+        out_shape=jax.ShapeDtypeStruct((tokens, width), bf16),
+        scratch_shapes=[pltpu.VMEM((tokens, columns), bf16)],
+        compiler_params=pltpu.CompilerParams(vmem_limit_bytes=40 << 20),
+        cost_estimate=SMALL_COST,
+        name="d_one",
+    )(*parts, weight)
+
+
+def ffn_kernel(
+    h_ref, dy_ref, wg_ref, wu_ref, wd_ref, act_ref, dg_ref, du_ref, out_ref, acc_ref
+):
+    step = pl.program_id(0)
+    w_gate, w_up = wg_ref[...], wu_ref[...]
+    gate = mm(h_ref[...], w_gate)
+    up = mm(h_ref[...], w_up)
+    d_act = mm(dy_ref[...], wd_ref[...])
+    sigmoid_gate = jax.nn.sigmoid(gate)
+    silu_gate = gate * sigmoid_gate
+    act_ref[...] = (silu_gate * up).astype(bf16)
+    d_gate = (d_act * up * sigmoid_gate * (1.0 + gate * (1.0 - sigmoid_gate))).astype(bf16)
+    d_up = (d_act * silu_gate).astype(bf16)
+    dg_ref[...] = d_gate
+    du_ref[...] = d_up
+    term = mm(d_gate, w_gate, ((1,), (1,))) + mm(d_up, w_up, ((1,), (1,)))
+
+    @pl.when(step == 0)
+    def _():
+        acc_ref[...] = term
+
+    @pl.when(step > 0)
+    def _():
+        acc_ref[...] += term
+
+    @pl.when(step == pl.num_programs(0) - 1)
+    def _():
+        out_ref[...] = acc_ref[...].astype(bf16)
+
+
+FFN_BLOCK = 512
+
+
+def feed_forward(normed, d_out, weights, units):
+    tokens, width = normed.shape
+    weight_spec = lambda i: pl.BlockSpec(
+        (width, FFN_BLOCK), lambda n: (0, i * units // FFN_BLOCK + n)
+    )
+    column_spec = pl.BlockSpec((tokens, FFN_BLOCK), lambda n: (0, n))
+    whole = pl.BlockSpec((tokens, width), lambda n: (0, 0))
+    return pl.pallas_call(
+        ffn_kernel,
+        grid=(units // FFN_BLOCK,),
+        in_specs=[whole, whole] + [weight_spec(i) for i in range(3)],
+        out_specs=[column_spec] * 3 + [whole],
+        out_shape=[jax.ShapeDtypeStruct((tokens, units), bf16)] * 3
+        + [jax.ShapeDtypeStruct((tokens, width), bf16)],
+        scratch_shapes=[pltpu.VMEM((tokens, width), f32)],
+        compiler_params=pltpu.CompilerParams(vmem_limit_bytes=56 << 20),
+        cost_estimate=SMALL_COST,
+        name="feed_forward",
+    )(normed, d_out, weights, weights, weights)
+
+
+def turn_kernel(chips, rows, core_ref, x_ref, mine_ref, other_ref, turned_ref):
+    turned_ref[...] = x_ref[...].T
+    core = core_ref[0]
+    for chip in range(chips):
+        for ref, which in ((mine_ref, core), (other_ref, 1 - core)):
+            first = pl.multiple_of((chip * 2 + which) * rows, 16)
+            ref[0, chip] = turned_ref[pl.ds(first, rows), :]
+
+
+def rows_for_cores(activation, core):
+    tokens, width = activation.shape
+    groups, chips = lax.axis_size("fsdp"), lax.axis_size("ctx") // 2
+    rows = width // (groups * chips * 2)
+    shape = (groups, chips, rows, tokens)
+    if rows % 16 or (width // groups) % 128:
+        turned = activation.T.reshape(groups, chips, 2, rows, tokens)
+        return tuple(
+            lax.dynamic_index_in_dim(turned, c, 2, keepdims=False) for c in (core, 1 - core)
+        )
+    spec = pl.BlockSpec((1, chips, rows, tokens), lambda g, _: (g, 0, 0, 0))
+    return pl.pallas_call(
+        functools.partial(turn_kernel, chips, rows),
+        grid_spec=pltpu.PrefetchScalarGridSpec(
+            num_scalar_prefetch=1,
+            grid=(groups,),
+            in_specs=[pl.BlockSpec((tokens, width // groups), lambda g, _: (0, g))],
+            out_specs=[spec, spec],
+            scratch_shapes=[pltpu.VMEM((width // groups, tokens), bf16)],
+        ),
+        out_shape=[jax.ShapeDtypeStruct(shape, bf16)] * 2,
+        compiler_params=pltpu.CompilerParams(vmem_limit_bytes=32 << 20),
+        cost_estimate=SMALL_COST,
+        name="turn_rows",
+    )(core[None], activation)
+
+
+class Order:
+    def __init__(self, always=None):
+        self.last = ()
+        self.always = always
+
+    def __call__(self, function, *args):
+        leaves, tree = jax.tree.flatten(args)
+        held = lax.optimization_barrier((*leaves, *self.last))
+        result = function(*jax.tree.unflatten(tree, held[: len(leaves)]))
+        self.last = (jax.tree.leaves(result)[0],)
+        return result
+
+    def apart(self, function, *args):
+        def guarded(*args):
+            shapes = jax.eval_shape(function, *args)
+            nothing = lambda *_: jax.tree.map(lambda s: jnp.zeros(s.shape, s.dtype), shapes)
+            return lax.cond(self.always, function, nothing, *args)
+
+        return self(guarded, *args)
+
+
+def swapped_of(*values):
+    return [core_swap(v) for v in values]
 
 
 def core_swap(value):
@@ -234,51 +635,174 @@
     return lax.ppermute(value, "fsdp", [(i, (i + by) % size) for i in range(size)])
 
 
-def tp_sum(part):
-    part = lax.optimization_barrier(part.astype(bf16))
-    size = lax.axis_size("tp")
-    if size != 2:
-        return lax.psum(part, "tp").astype(f32)
-    other = lax.ppermute(part, "tp", [(0, 1), (1, 0)])
-    return part.astype(f32) + other.astype(f32)
-
-
-def rows_for_core(activation, core):
-    tokens, width = activation.shape
-    groups, chips = lax.axis_size("fsdp"), lax.axis_size("ctx") // 2
-    rows = width // (groups * chips * 2)
-    turned = activation.T.reshape(groups, chips, 2, rows, tokens)
-    return lax.dynamic_index_in_dim(turned, core, 2, keepdims=False)
-
-
-def weight_gradient(left, right):
-    chips = lax.axis_size("ctx") // 2
-    groups = lax.axis_size("fsdp")
-    chip, group = lax.axis_index("ctx") // 2, lax.axis_index("fsdp")
-    _, _, rows, _ = left[0].shape
-    columns = right[0].shape[1]
-
-    def product(which):
+def tp_swap(value):
+    return lax.ppermute(value, "tp", [(0, 1), (1, 0)])
+
+
+def tp_send(part):
+    part = lax.optimization_barrier(part)
+    return part, tp_swap(part)
+
+
+def tp_add(sent):
+    mine, other = sent
+    return mine.astype(f32) + other.astype(f32)
+
+
+def both_cores(value):
+    return value, core_swap(value)
+
+
+def gathered_rows(weight, gains, hold):
+    groups, count = lax.axis_size("fsdp"), lax.axis_size("ctx")
+    group, index = lax.axis_index("fsdp"), lax.axis_index("ctx")
+    rows, columns = weight.shape
+    share = rows // count
+    mine = lax.dynamic_slice_in_dim(weight, index * share, share, 0)
+    extra = jnp.pad(gains, ((0, 16 - gains.shape[0]), (0, columns - gains.shape[1])))
+    mine = jnp.concatenate([mine, extra], axis=0)
+    fetched = [group_shift(mine, by) for by in range(1, groups)]
+    stack = jnp.stack([gains] + [p[share : share + 2, : gains.shape[1]] for p in fetched], axis=0)
+    all_gains = jnp.concatenate(
+        [
+            lax.dynamic_index_in_dim(stack, (group - i) % groups, 0, keepdims=False)
+            for i in range(groups)
+        ],
+        axis=1,
+    ).astype(f32)
+    weight, _ = lax.optimization_barrier((weight, hold))
+    whole = jnp.zeros((groups * rows, columns), weight.dtype)
+    whole = lax.dynamic_update_slice_in_dim(whole, weight, group * rows, 0)
+    pieces = jnp.stack([p[:share] for p in fetched], axis=0)
+
+    def placed(whole, pieces, source):
+        for by in range(1, groups):
+            first = (group - by) % groups * rows + source * share
+            whole = lax.dynamic_update_slice_in_dim(whole, pieces[by - 1], first, 0)
+        return whole
+
+    passed = [pieces] + [chip_shift(pieces, by) for by in range(1, count // 2)]
+    for by, moved in enumerate(passed):
+        source = (index - 2 * by) % count
+        whole = placed(whole, moved, source)
+        whole = placed(whole, core_swap(moved), source ^ 1)
+    return whole, all_gains
+
+
+def gradient_kernel(pairs, turned, pieces, place_ref, *refs):
+    total = None
+    for i in range(pairs):
+        left, right = refs[2 * i], refs[2 * i + 1]
+        groups, _, rows, tokens = left.shape
+        term = mm(
+            left[...].reshape(groups * rows, tokens), right[...], ((1,), (1 if turned else 0,))
+        )
+        total = term if total is None else total + term
+    total = total.reshape(groups, rows, total.shape[-1])
+    refs = refs[2 * pairs :]
+    arrived = refs[: -1 if not pieces else -1 - groups]
+    for piece in arrived:
+        total = total + piece[...].astype(f32)
+    if not pieces:
+        refs[-1][...] = total.astype(bf16)
+        return
+    outs, sum_ref = refs[-1 - groups : -1], refs[-1]
+    sum_ref[...] = total
+    group = place_ref[1]
+    for by, out in enumerate(outs):
+        out[...] = sum_ref[lax.rem(group + by, groups)].astype(out.dtype)
+
+
+def gradient_call(left, right, which, turned, arrived, pieces):
+    groups, chips, rows, tokens = left[0].shape
+    group = lax.axis_index("fsdp")
+    columns = right[0].shape[0 if turned else 1]
+    block = next((b for b in (512, 384) if columns % b == 0), columns)
+    if rows % 16 or columns % block:
         total = None
         for a, b in zip(left, right):
             picked = lax.dynamic_index_in_dim(a, which, 1, keepdims=False)
-            term = mm(picked.reshape(groups * rows, -1), b)
+            term = mm(picked.reshape(groups * rows, -1), b, ((1,), (1 if turned else 0,)))
             total = term if total is None else total + term
-        return total
-
-    arrived = [
-        chip_shift(product((chip + by) % chips).astype(bf16), by) for by in range(1, chips)
+        total = sum((piece.astype(f32) for piece in arrived), total.reshape(groups, rows, -1))
+        if not pieces:
+            return total.astype(bf16)
+        parts = [
+            lax.dynamic_index_in_dim(total, (group + by) % groups, 0, keepdims=False)
+            for by in range(groups)
+        ]
+        return [parts[0]] + [p.astype(bf16) for p in parts[1:]]
+    left_spec = pl.BlockSpec((groups, 1, rows, tokens), lambda n, place: (0, place[0], 0, 0))
+    if turned:
+        right_spec = pl.BlockSpec((block, tokens), lambda n, _: (n, 0))
+    else:
+        right_spec = pl.BlockSpec((tokens, block), lambda n, _: (0, n))
+    sum_spec = pl.BlockSpec((groups, rows, block), lambda n, _: (0, 0, n))
+    operands = [v for pair in zip(left, right) for v in pair] + list(arrived)
+    if pieces:
+        out_specs = [pl.BlockSpec((rows, block), lambda n, _: (0, n))] * groups
+        out_shape = [
+            jax.ShapeDtypeStruct((rows, columns), bf16 if by else f32) for by in range(groups)
+        ]
+        scratch = [pltpu.VMEM((groups, rows, block), f32)]
+    else:
+        out_specs, scratch = sum_spec, []
+        out_shape = jax.ShapeDtypeStruct((groups, rows, columns), bf16)
+    return pl.pallas_call(
+        functools.partial(gradient_kernel, len(left), turned, pieces),
+        grid_spec=pltpu.PrefetchScalarGridSpec(
+            num_scalar_prefetch=1,
+            grid=(columns // block,),
+            in_specs=[left_spec, right_spec] * len(left) + [sum_spec] * len(arrived),
+            out_specs=out_specs,
+            scratch_shapes=scratch,
+        ),
+        out_shape=out_shape,
+        compiler_params=pltpu.CompilerParams(vmem_limit_bytes=40 << 20),
+        cost_estimate=SMALL_COST,
+        name="gradient_chip" if arrived else "gradient_send",
+    )(jnp.stack([which, group]), *operands)
+
+
+def gradient_products(left, right, turned=False):
+    chips, chip = lax.axis_size("ctx") // 2, lax.axis_index("ctx") // 2
+    return [
+        gradient_call(left, right, (chip + by) % chips, turned, (), False)
+        for by in range(1, chips)
     ]
-    total = product(chip)
-    for piece in arrived:
-        total = total + piece.astype(f32)
-    total = total.reshape(groups, rows, columns)
-    low = total.astype(bf16)
-    result = lax.dynamic_index_in_dim(total, group, 0, keepdims=False)
-    for by in range(1, groups):
-        sent = lax.dynamic_index_in_dim(low, (group + by) % groups, 0, keepdims=False)
-        result = result + group_shift(sent, by).astype(f32)
-    return result
+
+
+def gradient_send(products):
+    return [chip_shift(p, by) for by, p in enumerate(products, 1)]
+
+
+def gradient_chip(left, right, arrived, turned=False, pieces=False):
+    return gradient_call(left, right, lax.axis_index("ctx") // 2, turned, arrived, pieces)
+
+
+def gradient_groups(pieces):
+    return [group_shift(piece, by) if by else piece for by, piece in enumerate(pieces)]
+
+
+def gradient_scatter(total):
+    groups, rows, columns = total.shape
+    return lax.psum_scatter(
+        total.reshape(groups * rows, columns), "fsdp", scatter_dimension=0, tiled=True
+    )
+
+
+def gradient_sum(terms):
+    total = terms[0].astype(f32)
+    for term in terms[1:]:
+        total = total + term.astype(f32)
+    return total
+
+
+def gain_gradient(weights, gradients, gain):
+    total = 0.0
+    for weight, gradient in zip(weights, gradients):
+        total = total + jnp.sum(weight.astype(f32) * gradient.astype(f32), axis=1)
+    return total / gain
 
 
 def slot_meta(ctx_index, tokens, stripe_row, lengths):
@@ -300,13 +824,6 @@
     unit_rows = values * scale_row
     weighted = grad_normed * gain
     return scale_row * (weighted - unit_rows * jnp.mean(weighted * unit_rows, axis=-1, keepdims=True))
-
-
-def rotate(vector, cos_table, sin_table):
-    front, back = vector[..., 0, :, :], vector[..., 1, :, :]
-    return jnp.stack(
-        [front * cos_table - back * sin_table, back * cos_table + front * sin_table], axis=-3
-    )
 
 
 def on_device(
@@ -332,25 +849,12 @@
         rows = weight.shape[0] // ctx_count
         return lax.dynamic_slice_in_dim(weight, ctx_index * rows, rows, 0)
 
-    def gathered(weight):
-        return lax.all_gather(weight, ("fsdp", "ctx"), axis=0, tiled=True)
-
-    first = gathered(
-        jnp.concatenate([share(query_key_value_weight), share(output_weight)], axis=1)
-    )
-    wq, wo = first[:, :qkv_columns], first[:, qkv_columns:]
-    second = gathered(jnp.concatenate([share(feedforward_weight[i]) for i in range(3)], axis=1))
-    w_gate, w_up, w_down = (second[:, i * units : (i + 1) * units] for i in range(3))
-
-    gain_parts = [gains] + [group_shift(gains, by) for by in range(1, group_count)]
-    gain_stack = jnp.stack(gain_parts, axis=0)
-    gain_rows = jnp.concatenate(
-        [
-            lax.dynamic_index_in_dim(gain_stack, (group - i) % group_count, 0, keepdims=False)
-            for i in range(group_count)
-        ],
-        axis=1,
-    ).astype(f32)
+    tp_index = lax.axis_index("tp")
+    out_share = share(output_weight)
+    out_other = tp_swap(out_share)
+    payload = packed_share(feedforward_weight, out_share, out_other, ctx_index, share)
+    others = lax.all_gather(payload, ("fsdp", "ctx"), axis=0, tiled=True)
+    wq, gain_rows = gathered_rows(query_key_value_weight, gains, payload)
 
     lengths, stripe_row = doc_lengths[0], stripe[0]
     packed, start = slot_meta(ctx_index, tokens, stripe_row, lengths)
@@ -367,88 +871,198 @@
     )
     meta = (block_starts, stripes, packed[None, :], start[None, :])
 
-    layer_input = hidden_in[0].astype(f32)
-    first_normed, scale_one = rms_normed(layer_input, gain_rows[0])
-    first_normed = first_normed.astype(bf16)
-    projected = mm(wq, first_normed, ((0,), (1,))).reshape(
-        kv_heads, QUERY_PER_KV + 2, 2, HALF, tokens
-    )
-    turned = rotate(projected[:, : QUERY_PER_KV + 1], cos_table, sin_table).astype(bf16)
-    queries = turned[:, :QUERY_PER_KV].reshape(kv_heads, QUERY_PER_KV, HEAD_SIZE, tokens)
-    kv_own = jnp.stack(
-        [
-            turned[:, QUERY_PER_KV].reshape(kv_heads, HEAD_SIZE, tokens),
-            projected[:, QUERY_PER_KV + 1].astype(bf16).reshape(kv_heads, HEAD_SIZE, tokens),
-        ],
-        axis=1,
-    )
-    pieces = []
-    for by in range(ctx_count // 2):
-        piece = chip_shift(kv_own, by) if by else kv_own
-        pieces += [piece, core_swap(piece)]
-    attended, lse = attention_forward(queries, pieces, *meta)
-    attended_rows = attended.reshape(att_columns, tokens)
-    attn_part = mm(attended_rows, wo, ((0,), (1,)))
-    middle = layer_input + tp_sum(attn_part)
-
-    second_normed, scale_two = rms_normed(middle, gain_rows[1])
-    second_normed = second_normed.astype(bf16)
-    grad_low = cotangent[0]
-    gate = mm(second_normed, w_gate)
-    up = mm(second_normed, w_up)
-    d_act = mm(grad_low, w_down)
-    sigmoid_gate = jax.nn.sigmoid(gate)
-    silu_gate = gate * sigmoid_gate
-    activated = (silu_gate * up).astype(bf16)
-    d_gate = (d_act * up * sigmoid_gate * (1.0 + gate * (1.0 - sigmoid_gate))).astype(bf16)
-    d_up = (d_act * silu_gate).astype(bf16)
-    d_two = tp_sum(mm(d_gate, w_gate, ((1,), (1,))) + mm(d_up, w_up, ((1,), (1,))))
-    hidden_out = (middle + tp_sum(mm(activated, w_down, ((1,), (1,))))).astype(bf16)
-
-    def exchanged(activation):
-        return rows_for_core(activation, core), core_swap(rows_for_core(activation, 1 - core))
-
-    def both(value):
-        return value, core_swap(value)
-
-    rows_two = exchanged(second_normed)
-    rows_dy = exchanged(grad_low)
-    grad_gate = weight_gradient(rows_two, both(d_gate))
-    grad_up = weight_gradient(rows_two, both(d_up))
-    grad_down = weight_gradient(rows_dy, both(activated))
-
-    d_mid = grad_low.astype(f32) + norm_back(d_two, middle, scale_two, gain_rows[1])
-    gain_two = jnp.sum(d_two * (middle * scale_two), axis=0)
-    d_branch = d_mid.astype(bf16)
-
-    d_att = mm(wo, d_branch, ((0,), (1,))).astype(bf16).reshape(attended.shape)
-    back = attention_backward(queries, d_att, attended, lse, pieces, *meta)
-    d_query, d_pieces = back[0], back[1:]
-    grad_out = weight_gradient(exchanged(d_branch), both(attended_rows.T))
-    d_kv = None
-    for by in reversed(range(ctx_count // 2)):
-        mine, partners = d_pieces[2 * by], d_pieces[2 * by + 1]
-        chip_sum = mine.astype(f32) + core_swap(partners).astype(f32)
-        term = chip_shift(chip_sum.astype(bf16), -by).astype(f32) if by else chip_sum
-        d_kv = term if d_kv is None else d_kv + term
-    d_kv = d_kv.reshape(kv_heads, 2, 2, HALF, tokens)
-    d_query = d_query.reshape(kv_heads, QUERY_PER_KV, 2, HALF, tokens)
-    d_turned = rotate(
-        jnp.concatenate([d_query, d_kv[:, :1]], axis=1), cos_table, -sin_table
-    )
-    d_proj = (
-        jnp.concatenate([d_turned, d_kv[:, 1:]], axis=1).astype(bf16).reshape(qkv_columns, tokens)
-    )
-    d_one_part = mm(d_proj, wq, ((0,), (1,)))
-    d_one = tp_sum(d_one_part)
-    grad_qkv = weight_gradient(exchanged(first_normed), both(d_proj.T))
-    grad_in = (d_mid + norm_back(d_one, layer_input, scale_one, gain_rows[0])).astype(bf16)
-    gain_one = jnp.sum(d_one * (layer_input * scale_one), axis=0)
-
-    grad_ffn = jnp.stack([grad_gate, grad_up, grad_down], axis=0)
-    grad_gains = lax.psum_scatter(
-        jnp.stack([gain_one, gain_two], axis=0), ("fsdp", "ctx"), scatter_dimension=1, tiled=True
-    )
+    order = Order(lengths[0] > 0)
+    touch = lambda *v: v
+    x, grad_low = hidden_in[0], cotangent[0]
+    rows_dy = order(rows_for_cores, grad_low, core)
+
+    def first_norm(x, gain):
+        values = x.astype(f32)
+        scale = lax.rsqrt(jnp.mean(values * values, axis=-1, keepdims=True) + norm_eps)
+        return (values * scale * gain).astype(bf16), scale
+
+    first_normed, scale_one = order(first_norm, x, gain_rows[0])
+    rows_one = order(rows_for_cores, first_normed, core)
+    first_normed, tables, *meta = lax.optimization_barrier(
+        (first_normed, (cos_table, sin_table), *meta)
+    )
+    chunk = kv_heads // CHUNKS
+    queries, own, moving, pieces, attended, lse = [], [], [], [], [], []
+    for c in range(CHUNKS):
+        query, kv_own = order(
+            functools.partial(project, first=c * chunk, heads=chunk), first_normed, wq, *tables
+        )
+        queries.append(query)
+        own.append(kv_own)
+        moving.append([chip_shift(kv_own, by) for by in range(1, ctx_count // 2)])
+    own_swapped = order.apart(swapped_of, *own)
+    other_dy, other_one = order.apart(swapped_of, rows_dy[1], rows_one[1])
+    left_dy, left_one = (rows_dy[0], other_dy), (rows_one[0], other_one)
+
+    def attend(query, mine, partners, arrived, *meta):
+        pieces = [mine, partners]
+        for piece in arrived:
+            pieces += [piece, core_swap(piece)]
+        return attention_forward(query, pieces, *meta), pieces[3::2]
+
+    attended_others = []
+    for c in range(CHUNKS):
+        (att, lse_c), swapped = order.apart(
+            attend, queries[c], own[c], own_swapped[c], moving[c], *meta
+        )
+        both = [v for pair in zip(moving[c], swapped) for v in pair]
+        pieces.append([own[c], own_swapped[c], *both])
+        attended.append(att)
+        lse.append(lse_c)
+        attended_others.append(tp_swap(att.reshape(-1, tokens)))
+    attended_rows = [a.reshape(-1, tokens) for a in attended]
+    attended_others[0] = order(lambda v: v, attended_others[0])
+    all_attended, other_attended = order.apart(
+        lambda *parts: (jnp.concatenate(parts, axis=0), core_swap(jnp.concatenate(parts, axis=0))),
+        *attended_rows,
+    )
+    right_att = (all_attended, other_attended)
+    middle, second_normed = order(
+        functools.partial(middle_of, first=3 * units),
+        attended_rows,
+        attended_others,
+        tp_index,
+        x,
+        gain_rows[1:],
+        others,
+    )
+
+    turned_products = functools.partial(gradient_products, turned=True)
+    activated, d_gate, d_up, d_two_part = order(
+        functools.partial(feed_forward, units=units), second_normed, grad_low, others
+    )
+    d_two_sent = tp_send(d_two_part)
+
+    def down_part(activated, normed, left_dy, core):
+        inner = Order()
+        other = core_swap(activated)
+        rows = inner(rows_for_cores, normed, core)
+        rows_other = core_swap(rows[1])
+        return inner(gradient_products, left_dy, (activated, other)), other, (rows[0], rows_other)
+
+    down_products, other_act, left_two = order.apart(
+        down_part, activated, second_normed, left_dy, core
+    )
+    right_act = (activated, other_act)
+    down_arrived = gradient_send(down_products)
+
+    def gate_part(activated, d_gate, d_up, left_two, others):
+        inner = Order()
+        other_gate = core_swap(d_gate)
+        down_sum = inner(functools.partial(down_project, first=2 * units), activated, others)
+        gate_products = inner(gradient_products, left_two, (d_gate, other_gate))
+        other_up = core_swap(lax.optimization_barrier((d_up, down_sum))[0])
+        up_products = inner(gradient_products, left_two, (d_up, other_up))
+        return gate_products, up_products, down_sum, other_gate, other_up
+
+    gate_products, up_products, down_sum, other_gate, other_up = order.apart(
+        gate_part, activated, d_gate, d_up, left_two, others
+    )
+    right_gate, right_up = (d_gate, other_gate), (d_up, other_up)
+    down_arrived, gate_products, down_sum, d_two_sent = order(
+        touch, down_arrived, gate_products, down_sum, d_two_sent
+    )
+    gate_arrived = gradient_send(gate_products)
+    down_sent = tp_send(down_sum)
+    d_mid, d_branch, d_att = order(
+        functools.partial(d_middle_of, first=3 * units, features=att_columns),
+        d_two_sent,
+        middle,
+        grad_low,
+        gain_rows[1:],
+        others,
+    )
+    down_scattered = gradient_scatter(order(gradient_chip, left_dy, right_act, down_arrived))
+    d_att = d_att.reshape(CHUNKS, chunk, QUERY_PER_KV, HEAD_SIZE, tokens)
+
+    def attend_back(query, d_att, attended, lse, pieces, *meta):
+        d_query, *d_pieces = attention_backward(query, d_att, attended, lse, pieces, *meta)
+        sums = [
+            (mine.astype(f32) + core_swap(partners).astype(f32)).astype(bf16)
+            for mine, partners in zip(d_pieces[::2], d_pieces[1::2])
+        ]
+        return d_query, sums
+
+    def attention_step(c):
+        d_query, sums = order.apart(
+            attend_back, queries[c], d_att[c], attended[c], lse[c], pieces[c], *meta
+        )
+        return d_query, [chip_shift(s, -by) if by else s for by, s in enumerate(sums)]
+
+    d_query_0, d_kv_0 = attention_step(0)
+    gate_arrived, up_products = order(touch, gate_arrived, up_products)
+    up_arrived = gradient_send(up_products)
+    gate_scattered = gradient_scatter(order(gradient_chip, left_two, right_gate, gate_arrived))
+    d_query_1, d_kv_1 = attention_step(1)
+
+    def branch_part(d_branch, core, right_att):
+        inner = Order()
+        rows = inner(rows_for_cores, d_branch, core)
+        left = (rows[0], core_swap(rows[1]))
+        return inner(turned_products, left, right_att), left
+
+    out_products, left_branch = order.apart(branch_part, d_branch, core, right_att)
+    out_arrived = gradient_send(out_products)
+    d_kv_0, d_kv_1, down_sent = order(touch, d_kv_0, d_kv_1, down_sent)
+
+    def project_back(d_query, d_kv, wq, *tables):
+        inner = Order()
+        parts = [inner(turned_back, q, kv, *tables) for q, kv in zip(d_query, d_kv)]
+        others = [core_swap(p) for p in parts]
+        return inner(d_one_of, parts, wq), parts, others
+
+    d_one_part, d_proj, other_proj = order.apart(
+        project_back, [d_query_0, d_query_1], [d_kv_0, d_kv_1], wq, *tables
+    )
+    d_one_sent = tp_send(d_one_part)
+    up_scattered = gradient_scatter(order(gradient_chip, left_two, right_up, up_arrived))
+    right_proj = list(zip(d_proj, other_proj))
+    qkv_arrived = [
+        gradient_send(order(turned_products, left_one, right_proj[c])) for c in range(CHUNKS)
+    ]
+    finish = functools.partial(gradient_chip, turned=True, pieces=True)
+    out_terms = gradient_groups(order(finish, left_branch, right_att, out_arrived))
+    hidden_out = order(lambda m, s: (m + tp_add(s)).astype(bf16), middle, down_sent)
+    qkv_terms = [
+        gradient_groups(order(finish, left_one, right_proj[c], qkv_arrived[c]))
+        for c in range(CHUNKS)
+    ]
+    grad_out = order(gradient_sum, out_terms)
+    grad_qkv = order(
+        lambda *terms: jnp.concatenate([gradient_sum(t) for t in terms], axis=1), *qkv_terms
+    )
+    own_gains = lax.dynamic_slice_in_dim(
+        gains, ctx_index * out_share.shape[0], out_share.shape[0], 1
+    ).astype(f32)
+
+    def gain_parts(grad_qkv, grad_gate, grad_up):
+        return jnp.stack(
+            [
+                gain_gradient([share(query_key_value_weight)], [grad_qkv], own_gains[0]),
+                gain_gradient(
+                    [share(feedforward_weight[i]) for i in range(2)],
+                    [grad_gate, grad_up],
+                    own_gains[1],
+                ),
+            ],
+            axis=0,
+        )
+
+    grad_gains = order(gain_parts, grad_qkv, gate_scattered, up_scattered)
+    gains_other = tp_swap(grad_gains)
+    grad_ffn = order(
+        lambda *parts: jnp.stack(parts, axis=0).astype(f32),
+        gate_scattered,
+        up_scattered,
+        down_scattered,
+    )
+    grad_gains = order(lambda a, b: a + b, grad_gains, gains_other)
+    grad_in = order(input_gradient, d_one_sent, x, d_mid, gain_rows[:1])
     return (hidden_out[None], grad_in[None], grad_qkv, grad_out, grad_ffn, grad_gains)
 
 

time: 807 us -> 562 us (0.70)
  waiting for transfers between devices: 397 us -> 191 us
  Pallas kernels: 55.8 us -> 226 us
  matrix products: 156 us -> 0 us
  local copies, waits for them, and re-layouts: 68.1 us -> 32.8 us
  other arithmetic: 46.5 us -> 24.5 us
    pallas_call x0 -> x27, Pallas kernels: none -> 164 us  [the longest x12 65.3 us: gradient_call(): pl.pallas_call(functools.partial(gradient_kernel, len(left), turned, piec...]
    dot_general x30 -> x0, matrix products: 156 us -> none  [mm(): lax.dot_general(a, b, (contract, ((), ())), preferred_element_type=f32)]
    ppermute x4 -> x7, waiting for transfers between devices: 109 us -> 13.9 us  [tp_swap(): return lax.ppermute(value, 'tp', [(0, 1), (1, 0)])]
    all_gather x2 -> x1, waiting for transfers between devices: 55.4 us -> 0.01 us  [on_device(): others = lax.all_gather(payload, ('fsdp', 'ctx'), axis=0, tiled=True)]
    ppermute x7 -> x11, waiting for transfers between devices: 143 us -> 95 us  [chip_shift(): lax.ppermute(value, 'ctx', [(i, (i + 2 * by) % size) for i in range(size)])]
    unnamed x4, waiting for transfers between devices: 37.8 us -> 0.07 us
    ppermute x13 -> x20, waiting for transfers between devices: 1.63 us -> 25.8 us  [core_swap(): return lax.ppermute(value, 'ctx', [(i, i ^ 1) for i in range(size)])]
    ppermute x18 -> x12, starting transfers between devices: 49.7 us -> 34.9 us  [group_shift(): lax.ppermute(value, 'fsdp', [(i, (i + by) % size) for i in range(size)])]
  transfers between devices with their start and end apart: 45 -> 54, of which waited for: 17 -> 28; matrix products, arithmetic and copies ran while one was open for 32% -> 7% of each run, Pallas kernels for 7% -> 31%
where the time goes in v2:
time: 562 us; the launch traced here: 552 us
  Pallas kernels  226 us (40%)
  waiting for transfers between devices  191 us (34%)
  starting transfers between devices  61 us (11%)
  local copies, waits for them, and re-layouts  32.8 us (6%)
  other arithmetic  24.5 us (4%)
  between operations  14.8 us (3%)
    ppermute x11, waiting for transfers between devices, chip_shift(): lax.ppermute(value, 'ctx', [(i, (i + 2 * by) % size) for i in range(size)])  95 us
    pallas_call x12, Pallas kernels, gradient_call(): pl.pallas_call(functools.partial(gradient_kernel, len(left), turned, piec...  65.3 us
    ppermute x12, waiting for transfers between devices, group_shift(): lax.ppermute(value, 'fsdp', [(i, (i + by) % size) for i in range(size)])  52.7 us
    ppermute x12, starting transfers between devices, group_shift(): lax.ppermute(value, 'fsdp', [(i, (i + by) % size) for i in range(size)])  34.9 us
    pallas_call x1, Pallas kernels, feed_forward(): pl.pallas_call(ffn_kernel, grid=(units // FFN_BLOCK,), in_specs=[whole, w...  34.2 us
    pallas_call x2, Pallas kernels, attention_backward(): pl.pallas_call(functools.partial(backward_kernel, count, blocks), grid_sp...  33.5 us
    pallas_call x2, Pallas kernels, attention_forward(): pl.pallas_call(functools.partial(forward_kernel, count, blocks), grid_spe...  29.1 us
    ppermute x20, waiting for transfers between devices, core_swap(): return lax.ppermute(value, 'ctx', [(i, i ^ 1) for i in range(size)])  25.8 us
  transfers between devices with their start and end apart: 54, of which 28 were waited for; matrix products, arithmetic and copies ran while one was open for 7% of the time, Pallas kernels for 31%

profile of v2, /device:TPU:0, one launch (start us, length us, event | category | flops | bytes accessed | tf_op | source)
XLA Modules:
  0.0 551.5 jit_solution(1993283754339116900)
XLA Ops:
  38.9 14.5 %collective-permute-done.19 = bf16[112,1536]{1,0:T(8,128)(2,1)} collective-permute-done((bf16[112,1536]{1,0:T(8,128)(2,1)S(1)}, bf16[112,1536]{1,0:T(8,128)(2,1)}, u32[]{:S(2)}, u32[]{:S(2)}) %collective-permute-start.19) | collective-permute-done | bytes 344096 | tf_op jit(solution)/shard_map/ppermute | solution.py:635
  54.4 6.9 %collective-permute-done.20 = bf16[112,1536]{1,0:T(8,128)(2,1)} collective-permute-done((bf16[112,1536]{1,0:T(8,128)(2,1)S(1)}, bf16[112,1536]{1,0:T(8,128)(2,1)}, u32[]{:S(2)}, u32[]{:S(2)}) %collective-permute-start.20) | collective-permute-done | bytes 344096 | tf_op jit(solution)/shard_map/ppermute | solution.py:635
  69.5 34.1 %collective-permute-done.23 = bf16[3,96,1536]{2,1,0:T(8,128)(2,1)S(1)} collective-permute-done((bf16[3,96,1536]{2,1,0:T(8,128)(2,1)S(1)}, bf16[3,96,1536]{2,1,0:T(8,128)(2,1)S(1)}, u32[]{:S(2)}, u32[]{:S(2)}) %collective-permute-start.23) | collective-permute-done | bytes 884768 | tf_op jit(solution)/shard_map/ppermute | solution.py:630
  124.7 14.6 %collective-permute-done.25 = bf16[2,2,96,768]{3,2,1,0:T(8,128)(2,1)} collective-permute-done((bf16[2,2,96,768]{3,2,1,0:T(8,128)(2,1)}, bf16[2,2,96,768]{3,2,1,0:T(8,128)(2,1)}, u32[]{:S(2)}, u32[]{:S(2)}) %collective-permute-start.25) | collective-permute-done | bytes 589856 | tf_op jit(solution)/shard_map/ppermute | solution.py:630
  139.4 19.5 %conditional.13 = (bf16[2,2,96,768]{3,2,1,0:T(8,128)(2,1)}, f32[2,2,768]{2,1,0:T(2,128)}, bf16[2,2,96,768]{3,2,1,0:T(8,128)(2,1)}, bf16[384,768]{1,0:T(8,128)(2,1)}) conditional(s32[]{:T(128)} %bitcast.10, () %tuple.152, (bf16[2,2,96,768]{3,2,1,0:T(8,128)(2,1)}, s32[6]{0:T(128)}, s32[4]{0:T(128)}, s32[1,768]{1,0:T(1,128)}, s32[1,768]{1,0:T(1,128)}, ...), branch_computations={%region_8.9_spmd, %region_9.10_spmd} | conditional | flops 1 | bytes 3539017 | solution.py:614
  142.3 14.6 %attention_forward.2 = (bf16[2,2,96,768]{3,2,1,0:T(8,128)(2,1)}, f32[2,2,768]{2,1,0:T(2,128)}) custom-call(s32[6]{0:T(128)} %get-tuple-element.145.starts_ref, s32[4]{0:T(128)} %get-tuple-element.146.stripes_ref, s32[1,768]{1,0:T(1,128)} %get-tuple-element.147.place_q_ref, s32[1,768]{1,0:T(1,128)} %get-tuple-element.148.start_q_ref, ...), custom_call_target="tpu_custom_call" | custom-call | flops 1 | bytes 1 | tf_op jit(solution)/shard_map/cond/branch_1_fun/attention_forward/pallas_call | solution.py:169
  165.5 17.7 %conditional.14 = (bf16[2,2,96,768]{3,2,1,0:T(8,128)(2,1)}, f32[2,2,768]{2,1,0:T(2,128)}, bf16[2,2,96,768]{3,2,1,0:T(8,128)(2,1)}, bf16[384,768]{1,0:T(8,128)(2,1)S(1)}) conditional(s32[]{:T(128)} %bitcast.10, () %tuple.168, (bf16[2,2,96,768]{3,2,1,0:T(8,128)(2,1)S(1)}, s32[6]{0:T(128)}, s32[4]{0:T(128)}, s32[1,768]{1,0:T(1,128)}, ...), branch_computations={%region_10.11_spmd, %region_11.12_spmd} | conditional | flops 1 | bytes 3539017 | solution.py:614
  167.6 14.5 %attention_forward.3 = (bf16[2,2,96,768]{3,2,1,0:T(8,128)(2,1)}, f32[2,2,768]{2,1,0:T(2,128)}) custom-call(s32[6]{0:T(128)} %get-tuple-element.155.starts_ref, s32[4]{0:T(128)} %get-tuple-element.156.stripes_ref, s32[1,768]{1,0:T(1,128)} %get-tuple-element.157.place_q_ref, s32[1,768]{1,0:T(1,128)} %get-tuple-element.158.start_q_ref, ...), custom_call_target="tpu_custom_call" | custom-call | flops 1 | bytes 1 | tf_op jit(solution)/shard_map/cond/branch_1_fun/attention_forward/pallas_call | solution.py:169
  191.2 8.4 %collective-permute-done.28.refs_3_ = bf16[384,768]{1,0:T(8,128)(2,1)S(1)} collective-permute-done((bf16[384,768]{1,0:T(8,128)(2,1)}, bf16[384,768]{1,0:T(8,128)(2,1)S(1)}, u32[]{:S(2)}, u32[]{:S(2)}) %collective-permute-start.28) | collective-permute-done | bytes 589856 | tf_op jit(solution)/shard_map/ppermute | solution.py:639
  199.6 8.3 %middle.1 = (f32[768,1536]{1,0:T(8,128)S(1)}, bf16[768,1536]{1,0:T(8,128)(2,1)S(1)}) custom-call(s32[1]{0:T(128)} %bitcast.44.tp_ref, bf16[768,1536]{1,0:T(8,128)(2,1)S(1)} %bitcast.109, f32[1,1536]{1,0:T(1,128)S(1)} %get-tuple-element.625.gain_ref, bf16[384,768]{1,0:T(8,128)(2,1)} %get-tuple-element.588.refs_0_, bf16[384,768]{1,0:T(8,128)(2,1)} %copy-done.21, ...), custom_call_target="tpu_custom_call" | custom-call | flops 1 | bytes 1 | tf_op jit(solution)/shard_map/middle/pallas_call | solution.py:358
  210.0 34.2 %feed_forward.1 = (bf16[768,2048]{1,0:T(8,128)(2,1)}, bf16[768,2048]{1,0:T(8,128)(2,1)}, bf16[768,2048]{1,0:T(8,128)(2,1)}, bf16[768,1536]{1,0:T(8,128)(2,1)}) custom-call(bf16[768,1536]{1,0:T(8,128)(2,1)S(1)} %get-tuple-element.600.h_ref, bf16[768,1536]{1,0:T(8,128)(2,1)} %bitcast.111, ...), custom_call_target="tpu_custom_call" | custom-call | flops 1 | bytes 1 | tf_op jit(solution)/shard_map/feed_forward/pallas_call | solution.py:548
  245.6 13.1 %conditional.16 = (bf16[4,96,2048]{2,1,0:T(8,128)(2,1)}, bf16[768,2048]{1,0:T(8,128)(2,1)}, bf16[4,2,96,768]{3,2,1,0:T(8,128)(2,1)}, bf16[4,2,96,768]{3,2,1,0:T(8,128)(2,1)}) conditional(s32[]{:T(128)} %bitcast.10, () %tuple.177, (bf16[768,2048]{1,0:T(8,128)(2,1)}, bf16[768,1536]{1,0:T(8,128)(2,1)S(1)}, s32[]{:T(128)}, ...), branch_computations={%region_14.15_spmd, %region_15.16_spmd} | conditional | flops 37 | bytes 17301968 | solution.py:614
  251.6 7.1 %gradient_send.6 = bf16[4,96,2048]{2,1,0:T(8,128)(2,1)} custom-call(s32[2]{0:T(128)S(1)} %pad_add_fusion.place_ref, bf16[4,2,96,768]{3,2,1,0:T(8,128)(2,1)} %get-tuple-element.175.refs_0_, bf16[768,2048]{1,0:T(8,128)(2,1)} %get-tuple-element.176.refs_1_, bf16[4,2,96,768]{3,2,1,0:T(8,128)(2,1)} %get-tuple-element.177.refs_2_, ...), custom_call_target="tpu_custom_call" | custom-call | flops 1 | bytes 1 | tf_op jit(solution)/shard_map/cond/branch_1_fun/gradient_send/pallas_call | solution.py:751
  260.0 24.1 %conditional.17 = (bf16[4,96,2048]{2,1,0:T(8,128)(2,1)}, bf16[4,96,2048]{2,1,0:T(8,128)(2,1)}, bf16[768,1536]{1,0:T(8,128)(2,1)}, bf16[768,2048]{1,0:T(8,128)(2,1)}, bf16[768,2048]{1,0:T(8,128)(2,1)}) conditional(s32[]{:T(128)} %bitcast.10, () %tuple.181, (bf16[768,2048]{1,0:T(8,128)(2,1)}, bf16[768,2048]{1,0:T(8,128)(2,1)}, ...), branch_computations={%region_16.17_spmd, %region_17.18_spmd} | conditional | flops 38 | bytes 25166296 | solution.py:614
  260.0 8.9 %down_project.1 = bf16[768,1536]{1,0:T(8,128)(2,1)} custom-call(bf16[768,2048]{1,0:T(8,128)(2,1)} %get-tuple-element.185.a_ref, bf16[1536,7680]{1,0:T(8,128)(2,1)} %get-tuple-element.186.w_ref), custom_call_target="tpu_custom_call" | custom-call | flops 1 | bytes 1 | tf_op jit(solution)/shard_map/cond/branch_1_fun/down_project/pallas_call | solution.py:389
  269.5 7.1 %gradient_send.7 = bf16[4,96,2048]{2,1,0:T(8,128)(2,1)} custom-call(s32[2]{0:T(128)S(1)} %pad_add_fusion.1.place_ref, bf16[4,2,96,768]{3,2,1,0:T(8,128)(2,1)} %get-tuple-element.193.refs_0_, bf16[768,2048]{1,0:T(8,128)(2,1)} %get-tuple-element.188.refs_1_, bf16[4,2,96,768]{3,2,1,0:T(8,128)(2,1)} %get-tuple-element.195.refs_2_, ...), custom_call_target="tpu_custom_call" | custom-call | flops 1 | bytes 1 | tf_op jit(solution)/shard_map/cond/branch_1_fun/gradient_send/pallas_call | solution.py:751
  276.6 7.1 %gradient_send.8 = bf16[4,96,2048]{2,1,0:T(8,128)(2,1)} custom-call(s32[2]{0:T(128)S(1)} %pad_add_fusion.1.place_ref, bf16[4,2,96,768]{3,2,1,0:T(8,128)(2,1)} %get-tuple-element.193.refs_0_, bf16[768,2048]{1,0:T(8,128)(2,1)} %get-tuple-element.194.refs_1_, bf16[4,2,96,768]{3,2,1,0:T(8,128)(2,1)} %get-tuple-element.195.refs_2_, ...), custom_call_target="tpu_custom_call" | custom-call | flops 1 | bytes 1 | tf_op jit(solution)/shard_map/cond/branch_1_fun/gradient_send/pallas_call | solution.py:751
  284.1 11.3 %collective-permute-done.29.refs_4_ = bf16[4,96,2048]{2,1,0:T(8,128)(2,1)} collective-permute-done((bf16[4,96,2048]{2,1,0:T(8,128)(2,1)}, bf16[4,96,2048]{2,1,0:T(8,128)(2,1)}, u32[]{:S(2)}, u32[]{:S(2)}) %collective-permute-start.29) | collective-permute-done | bytes 1572896 | tf_op jit(solution)/shard_map/ppermute | solution.py:630
  300.6 9.5 %d_middle.1 = (f32[768,1536]{1,0:T(8,128)}, bf16[768,1536]{1,0:T(8,128)(2,1)}, bf16[768,768]{1,0:T(8,128)(2,1)S(1)}) custom-call(bf16[768,1536]{1,0:T(8,128)(2,1)S(1)} %copy-done.14, bf16[768,1536]{1,0:T(8,128)(2,1)} %collective-permute-done.30.other_ref, f32[768,1536]{1,0:T(8,128)} %copy-done.4, bf16[768,1536]{1,0:T(8,128)(2,1)} %bitcast.112, ...), custom_call_target="tpu_custom_call" | custom-call | flops 1 | bytes 1 | tf_op jit(solution)/shard_map/d_middle/pallas_call | solution.py:426
  318.0 19.6 %conditional.18 = (f32[2,2,96,768]{3,2,1,0:T(8,128)}, bf16[2,2,96,768]{3,2,1,0:T(8,128)(2,1)S(1)}, bf16[2,2,96,768]{3,2,1,0:T(8,128)(2,1)}) conditional(s32[]{:T(128)} %bitcast.10, () %tuple.176, (s32[6]{0:T(128)S(1)}, s32[4]{0:T(128)S(1)}, s32[1,768]{1,0:T(1,128)S(1)}, s32[1,768]{1,0:T(1,128)S(1)}, bf16[2,2,96,768]{3,2,1,0:T(8,128)(2,1)S(1)}, ...), branch_computations={%region_18.19_spmd, %region_19.20_spmd} | conditional | flops 2359297 | bytes 8257641 | solution.py:614
  318.0 16.5 %attention_backward.2 = (f32[2,2,96,768]{3,2,1,0:T(8,128)}, bf16[2,2,96,768]{3,2,1,0:T(8,128)(2,1)S(1)}, bf16[2,2,96,768]{3,2,1,0:T(8,128)(2,1)S(1)}, bf16[2,2,9...) custom-call(s32[6]{0:T(128)S(1)} %get-tuple-element.197.starts_ref, s32[4]{0:T(128)S(1)} %get-tuple-element.198.stripes_ref, ...), custom_call_target="tpu_custom_call" | custom-call | flops 1 | bytes 1 | tf_op jit(solution)/shard_map/cond/branch_1_fun/attention_backward/pallas_call | solution.py:198
  348.3 20.1 %conditional.19 = (f32[2,2,96,768]{3,2,1,0:T(8,128)}, bf16[2,2,96,768]{3,2,1,0:T(8,128)(2,1)S(1)}, bf16[2,2,96,768]{3,2,1,0:T(8,128)(2,1)}) conditional(s32[]{:T(128)} %bitcast.10, () %tuple.189, (s32[6]{0:T(128)}, s32[4]{0:T(128)}, s32[1,768]{1,0:T(1,128)}, s32[1,768]{1,0:T(1,128)S(1)}, bf16[2,2,96,768]{3,2,1,0:T(8,128)(2,1)}, ...), branch_computations={%region_20.21_spmd, %region_21.22_spmd} | conditional | flops 2359297 | bytes 8257641 | solution.py:614
  348.3 17.0 %attention_backward.3 = (f32[2,2,96,768]{3,2,1,0:T(8,128)}, bf16[2,2,96,768]{3,2,1,0:T(8,128)(2,1)S(1)}, bf16[2,2,96,768]{3,2,1,0:T(8,128)(2,1)S(1)}, bf16[2,2,9...) custom-call(s32[6]{0:T(128)} %get-tuple-element.214.starts_ref, s32[4]{0:T(128)} %get-tuple-element.215.stripes_ref, ...), custom_call_target="tpu_custom_call" | custom-call | flops 1 | bytes 1 | tf_op jit(solution)/shard_map/cond/branch_1_fun/attention_backward/pallas_call | solution.py:198
  369.7 12.3 %conditional.20 = (bf16[4,96,768]{2,1,0:T(8,128)(2,1)}, bf16[4,2,96,768]{3,2,1,0:T(8,128)(2,1)}, bf16[4,2,96,768]{3,2,1,0:T(8,128)(2,1)}) conditional(s32[]{:T(128)} %bitcast.10, () %tuple.194, (bf16[768,1536]{1,0:T(8,128)(2,1)}, s32[]{:T(128)}, bf16[768,768]{1,0:T(8,128)(2,1)}, bf16[768,768]{1,0:T(8,128)(2,1)}) %tuple.196), branch_computations={%region_22.23_spmd, %region_23.24_spmd} | conditional | flops 37 | bytes 4719009 | solution.py:614
  382.1 14.5 %collective-permute-done.31 = bf16[2,2,96,768]{3,2,1,0:T(8,128)(2,1)} collective-permute-done((bf16[2,2,96,768]{3,2,1,0:T(8,128)(2,1)}, bf16[2,2,96,768]{3,2,1,0:T(8,128)(2,1)}, u32[]{:S(2)}, u32[]{:S(2)}) %collective-permute-start.31) | collective-permute-done | bytes 589856 | tf_op jit(solution)/shard_map/ppermute | solution.py:630
  396.5 11.5 %collective-permute-done.33 = bf16[2,2,96,768]{3,2,1,0:T(8,128)(2,1)} collective-permute-done((bf16[2,2,96,768]{3,2,1,0:T(8,128)(2,1)}, bf16[2,2,96,768]{3,2,1,0:T(8,128)(2,1)}, u32[]{:S(2)}, u32[]{:S(2)}) %collective-permute-start.33) | collective-permute-done | bytes 589856 | tf_op jit(solution)/shard_map/ppermute | solution.py:630
  408.0 12.4 %conditional.21 = (bf16[768,1536]{1,0:T(8,128)(2,1)S(1)}, bf16[768,768]{1,0:T(8,128)(2,1)}, bf16[768,768]{1,0:T(8,128)(2,1)}, bf16[768,768]{1,0:T(8,128)(2,1)}, bf16[768,768]{1,0:T(8,128)(2,1)}) conditional(s32[]{:T(128)} %bitcast.10, () %tuple.198, (f32[2,2,96,768]{3,2,1,0:T(8,128)}, bf16[2,2,96,768]{3,2,1,0:T(8,128)(2,1)S(1)}, ...), branch_computations={%region_24.25_spmd, %region_25.26_spmd} | conditional | flops 3 | bytes 28311704 | solution.py:614
  420.5 6.7 %gradient_chip.8 = bf16[4,96,2048]{2,1,0:T(8,128)(2,1)S(1)} custom-call(s32[2]{0:T(128)S(1)} %pad_add_fusion.4.place_ref, bf16[4,2,96,768]{3,2,1,0:T(8,128)(2,1)} %get-tuple-element.711.refs_0_, bf16[768,2048]{1,0:T(8,128)(2,1)} %get-tuple-element.712.refs_1_, bf16[4,2,96,768]{3,2,1,0:T(8,128)(2,1)} %get-tuple-element.713.refs_2_, ...), custom_call_target="tpu_custom_call" | custom-call | flops 1 | bytes 1 | tf_op jit(solution)/shard_map/gradient_chip/pallas_call | solution.py:751
  449.4 13.0 %collective-permute-start.47 = (bf16[96,768]{1,0:T(8,128)(2,1)S(1)}, bf16[96,768]{1,0:T(8,128)(2,1)S(1)}, u32[]{:S(2)}, u32[]{:S(2)}) collective-permute-start(bf16[96,768]{1,0:T(8,128)(2,1)S(1)} %get-tuple-element.752), channel_id=1, source_target_pairs={{0,16},{8,24},{16,0},{24,8},{1,17},{9,25},{17,1},{25,9},{2,18},{10... | collective-permute-start | bytes 442376 | tf_op jit(solution)/shard_map/ppermute | solution.py:635
  478.0 8.3 %collective-permute-start.44 = (bf16[96,768]{1,0:T(8,128)(2,1)S(1)}, bf16[96,768]{1,0:T(8,128)(2,1)S(1)}, u32[]{:S(2)}, u32[]{:S(2)}) collective-permute-start(bf16[96,768]{1,0:T(8,128)(2,1)S(1)} %get-tuple-element.749), channel_id=1, source_target_pairs={{0,16},{8,24},{16,0},{24,8},{1,17},{9,25},{17,1},{25,9},{2,18},{10... | collective-permute-start | bytes 442376 | tf_op jit(solution)/shard_map/ppermute | solution.py:635
  491.2 10.9 %collective-permute-done.44 = bf16[96,768]{1,0:T(8,128)(2,1)S(1)} collective-permute-done((bf16[96,768]{1,0:T(8,128)(2,1)S(1)}, bf16[96,768]{1,0:T(8,128)(2,1)S(1)}, u32[]{:S(2)}, u32[]{:S(2)}) %collective-permute-start.44) | collective-permute-done | bytes 147488 | tf_op jit(solution)/shard_map/ppermute | solution.py:635
  506.7 19.4 %collective-permute-done.40 = bf16[96,768]{1,0:T(8,128)(2,1)S(1)} collective-permute-done((bf16[96,768]{1,0:T(8,128)(2,1)S(1)}, bf16[96,768]{1,0:T(8,128)(2,1)S(1)}, u32[]{:S(2)}, u32[]{:S(2)}) %collective-permute-start.40) | collective-permute-done | bytes 147488 | tf_op jit(solution)/shard_map/ppermute | solution.py:635
  (294 shorter events, 230.9 us)
Async XLA Ops:
  7.2 192.5 %all-gather.2.cloned.1.call-start = ((), (), s32[]{:S(2)}) async-start(), calls=%async_computation.3 | async-start | bytes 25067520 | tf_op jit(solution)/shard_map/all_gather | solution.py:856
  18.7 507.7 %reduce-scatter.4.cloned.1.call-start = ((), (), s32[]{:S(2)}) async-start(), calls=%async_computation.4 | async-start | bytes 1966080 | tf_op jit(solution)/shard_map/reduce_scatter | solution.py:789
  20.0 18.9 %collective-permute-start.18 = (bf16[112,1536]{1,0:T(8,128)(2,1)S(1)}, bf16[112,1536]{1,0:T(8,128)(2,1)S(1)}, u32[]{:S(2)}, u32[]{:S(2)}) collective-permute-start(bf16[112,1536]{1,0:T(8,128)(2,1)S(1)} %fusion.6), channel_id=1, source_target_pairs={{0,8},{8,16},{16,24},{24,0},{1,9},{9,17},{17,25},{25,1},{2,10},{10... | collective-permute-start | bytes 1032200 | tf_op jit(solution)/shard_map/ppermute | solution.py:635
  21.8 31.6 %collective-permute-start.19 = (bf16[112,1536]{1,0:T(8,128)(2,1)S(1)}, bf16[112,1536]{1,0:T(8,128)(2,1)}, u32[]{:S(2)}, u32[]{:S(2)}) collective-permute-start(bf16[112,1536]{1,0:T(8,128)(2,1)S(1)} %fusion.6), channel_id=1, source_target_pairs={{0,16},{8,24},{16,0},{24,8},{1,17},{9,25},{17,1},{25,9},{2,18},{10... | collective-permute-start | bytes 1032200 | tf_op jit(solution)/shard_map/ppermute | solution.py:635
  24.4 36.9 %collective-permute-start.20 = (bf16[112,1536]{1,0:T(8,128)(2,1)S(1)}, bf16[112,1536]{1,0:T(8,128)(2,1)}, u32[]{:S(2)}, u32[]{:S(2)}) collective-permute-start(bf16[112,1536]{1,0:T(8,128)(2,1)S(1)} %fusion.6), channel_id=1, source_target_pairs={{0,24},{8,0},{16,8},{24,16},{1,25},{9,1},{17,9},{25,17},{2,26},{10... | collective-permute-start | bytes 1032200 | tf_op jit(solution)/shard_map/ppermute | solution.py:635
  62.4 41.2 %collective-permute-start.22 = (bf16[3,96,1536]{2,1,0:T(8,128)(2,1)S(1)}, bf16[3,96,1536]{2,1,0:T(8,128)(2,1)S(1)}, u32[]{:S(2)}, u32[]{:S(2)}) collective-permute-start(bf16[3,96,1536]{2,1,0:T(8,128)(2,1)S(1)} %pad_maximum_fusion), channel_id=1, source_target_pairs={{0,2},{2,0},{4,6},{6,4},{1,3},{3,1},{5,7},{7,5},{8,10},{10,8},{12,... | collective-permute-start | bytes 2654216 | tf_op jit(solution)/shard_map/ppermute | solution.py:625
  62.5 41.1 %collective-permute-start.23 = (bf16[3,96,1536]{2,1,0:T(8,128)(2,1)S(1)}, bf16[3,96,1536]{2,1,0:T(8,128)(2,1)S(1)}, u32[]{:S(2)}, u32[]{:S(2)}) collective-permute-start(bf16[3,96,1536]{2,1,0:T(8,128)(2,1)S(1)} %pad_maximum_fusion), channel_id=1, source_target_pairs={{0,4},{2,6},{4,0},{6,2},{1,5},{3,7},{5,1},{7,3},{8,12},{10,14},{12... | collective-permute-start | bytes 2654216 | tf_op jit(solution)/shard_map/ppermute | solution.py:630
  110.3 29.1 %collective-permute-start.25 = (bf16[2,2,96,768]{3,2,1,0:T(8,128)(2,1)}, bf16[2,2,96,768]{3,2,1,0:T(8,128)(2,1)}, u32[]{:S(2)}, u32[]{:S(2)}) collective-permute-start(bf16[2,2,96,768]{3,2,1,0:T(8,128)(2,1)} %get-tuple-element.645), channel_id=1, source_target_pairs={{0,4},{2,6},{4,0},{6,2},{1,5},{3,7},{5,1},{7,3},{8,12},{10,14},{12... | collective-permute-start | bytes 1769480 | tf_op jit(solution)/shard_map/ppermute | solution.py:630
  115.9 48.3 %collective-permute-start.26 = (bf16[2,2,96,768]{3,2,1,0:T(8,128)(2,1)}, bf16[2,2,96,768]{3,2,1,0:T(8,128)(2,1)S(1)}, u32[]{:S(2)}, u32[]{:S(2)}) collective-permute-start(bf16[2,2,96,768]{3,2,1,0:T(8,128)(2,1)} %get-tuple-element.671), channel_id=1, source_target_pairs={{0,4},{2,6},{4,0},{6,2},{1,5},{3,7},{5,1},{7,3},{8,12},{10,14},{12... | collective-permute-start | bytes 1769480 | tf_op jit(solution)/shard_map/ppermute | solution.py:630
  164.3 20.7 %collective-permute-start.27 = (bf16[384,768]{1,0:T(8,128)(2,1)}, bf16[384,768]{1,0:T(8,128)(2,1)S(1)}, u32[]{:S(2)}, u32[]{:S(2)}) collective-permute-start(bf16[384,768]{1,0:T(8,128)(2,1)} %get-tuple-element.588.refs_0_), channel_id=1, source_target_pairs={{0,1},{1,0},{2,3},{3,2},{4,5},{5,4},{6,7},{7,6},{8,9},{9,8},{10,11... | collective-permute-start | bytes 1769480 | tf_op jit(solution)/shard_map/ppermute | solution.py:639
  184.0 15.6 %collective-permute-start.28 = (bf16[384,768]{1,0:T(8,128)(2,1)}, bf16[384,768]{1,0:T(8,128)(2,1)S(1)}, u32[]{:S(2)}, u32[]{:S(2)}) collective-permute-start(bf16[384,768]{1,0:T(8,128)(2,1)} %copy-done.21), channel_id=1, source_target_pairs={{0,1},{1,0},{2,3},{3,2},{4,5},{5,4},{6,7},{7,6},{8,9},{9,8},{10,11... | collective-permute-start | bytes 1769480 | tf_op jit(solution)/shard_map/ppermute | solution.py:639
  244.2 52.8 %collective-permute-start.30 = (bf16[768,1536]{1,0:T(8,128)(2,1)}, bf16[768,1536]{1,0:T(8,128)(2,1)}, u32[]{:S(2)}, u32[]{:S(2)}) collective-permute-start(bf16[768,1536]{1,0:T(8,128)(2,1)} %get-tuple-element.621.mine_ref), channel_id=1, source_target_pairs={{0,1},{1,0},{2,3},{3,2},{4,5},{5,4},{6,7},{7,6},{8,9},{9,8},{10,11... | collective-permute-start | bytes 7077896 | tf_op jit(solution)/shard_map/ppermute | solution.py:639
  258.6 36.8 %collective-permute-start.29 = (bf16[4,96,2048]{2,1,0:T(8,128)(2,1)}, bf16[4,96,2048]{2,1,0:T(8,128)(2,1)}, u32[]{:S(2)}, u32[]{:S(2)}) collective-permute-start(bf16[4,96,2048]{2,1,0:T(8,128)(2,1)} %get-tuple-element.604), channel_id=1, source_target_pairs={{0,4},{2,6},{4,0},{6,2},{1,5},{3,7},{5,1},{7,3},{8,12},{10,14},{12... | collective-permute-start | bytes 4718600 | tf_op jit(solution)/shard_map/ppermute | solution.py:630
  297.1 40.5 %collective-permute-start.32 = (bf16[4,96,2048]{2,1,0:T(8,128)(2,1)}, bf16[4,96,2048]{2,1,0:T(8,128)(2,1)}, u32[]{:S(2)}, u32[]{:S(2)}) collective-permute-start(bf16[4,96,2048]{2,1,0:T(8,128)(2,1)} %get-tuple-element.654), channel_id=1, source_target_pairs={{0,4},{2,6},{4,0},{6,2},{1,5},{3,7},{5,1},{7,3},{8,12},{10,14},{12... | collective-permute-start | bytes 4718600 | tf_op jit(solution)/shard_map/ppermute | solution.py:630
  345.4 181.0 %reduce-scatter.6.cloned.1.call-start = ((), (), s32[]{:S(2)}) async-start(), calls=%async_computation.5 | async-start | bytes 1966080 | tf_op jit(solution)/shard_map/reduce_scatter | solution.py:789
  345.4 62.6 %collective-permute-start.34 = (bf16[768,1536]{1,0:T(8,128)(2,1)}, bf16[768,1536]{1,0:T(8,128)(2,1)}, u32[]{:S(2)}, u32[]{:S(2)}) collective-permute-start(bf16[768,1536]{1,0:T(8,128)(2,1)} %get-tuple-element.731), channel_id=1, source_target_pairs={{0,1},{1,0},{2,3},{3,2},{4,5},{5,4},{6,7},{7,6},{8,9},{9,8},{10,11... | collective-permute-start | bytes 7077896 | tf_op jit(solution)/shard_map/ppermute | solution.py:639
  346.3 74.2 %collective-permute-start.36 = (bf16[4,96,2048]{2,1,0:T(8,128)(2,1)}, bf16[4,96,2048]{2,1,0:T(8,128)(2,1)}, u32[]{:S(2)}, u32[]{:S(2)}) collective-permute-start(bf16[4,96,2048]{2,1,0:T(8,128)(2,1)} %get-tuple-element.709), channel_id=1, source_target_pairs={{0,4},{2,6},{4,0},{6,2},{1,5},{3,7},{5,1},{7,3},{8,12},{10,14},{12... | collective-permute-start | bytes 4718600 | tf_op jit(solution)/shard_map/ppermute | solution.py:630
  347.5 49.0 %collective-permute-start.31 = (bf16[2,2,96,768]{3,2,1,0:T(8,128)(2,1)}, bf16[2,2,96,768]{3,2,1,0:T(8,128)(2,1)}, u32[]{:S(2)}, u32[]{:S(2)}) collective-permute-start(bf16[2,2,96,768]{3,2,1,0:T(8,128)(2,1)} %get-tuple-element.650), channel_id=1, source_target_pairs={{0,4},{2,6},{4,0},{6,2},{1,5},{3,7},{5,1},{7,3},{8,12},{10,14},{12... | collective-permute-start | bytes 1769480 | tf_op jit(solution)/shard_map/ppermute | solution.py:630
  368.4 39.6 %collective-permute-start.33 = (bf16[2,2,96,768]{3,2,1,0:T(8,128)(2,1)}, bf16[2,2,96,768]{3,2,1,0:T(8,128)(2,1)}, u32[]{:S(2)}, u32[]{:S(2)}) collective-permute-start(bf16[2,2,96,768]{3,2,1,0:T(8,128)(2,1)} %get-tuple-element.676), channel_id=1, source_target_pairs={{0,4},{2,6},{4,0},{6,2},{1,5},{3,7},{5,1},{7,3},{8,12},{10,14},{12... | collective-permute-start | bytes 1769480 | tf_op jit(solution)/shard_map/ppermute | solution.py:630
  428.4 105.4 %reduce-scatter.8.cloned.1.call-start = ((), (), s32[]{:S(2)}) async-start(), calls=%async_computation.6 | async-start | bytes 1966080 | tf_op jit(solution)/shard_map/reduce_scatter | solution.py:789
  428.5 16.5 %collective-permute-start.35 = (bf16[4,96,768]{2,1,0:T(8,128)(2,1)}, bf16[4,96,768]{2,1,0:T(8,128)(2,1)S(1)}, u32[]{:S(2)}, u32[]{:S(2)}) collective-permute-start(bf16[4,96,768]{2,1,0:T(8,128)(2,1)} %get-tuple-element.685), channel_id=1, source_target_pairs={{0,4},{2,6},{4,0},{6,2},{1,5},{3,7},{5,1},{7,3},{8,12},{10,14},{12... | collective-permute-start | bytes 1769480 | tf_op jit(solution)/shard_map/ppermute | solution.py:630
  429.8 107.5 %collective-permute-start.37 = (bf16[768,1536]{1,0:T(8,128)(2,1)}, bf16[768,1536]{1,0:T(8,128)(2,1)}, u32[]{:S(2)}, u32[]{:S(2)}) collective-permute-start(bf16[768,1536]{1,0:T(8,128)(2,1)} %copy-done.19), channel_id=1, source_target_pairs={{0,1},{1,0},{2,3},{3,2},{4,5},{5,4},{6,7},{7,6},{8,9},{9,8},{10,11... | collective-permute-start | bytes 7077896 | tf_op jit(solution)/shard_map/ppermute | solution.py:639
  435.5 31.6 %collective-permute-start.38 = (bf16[4,96,768]{2,1,0:T(8,128)(2,1)S(1)}, bf16[4,96,768]{2,1,0:T(8,128)(2,1)S(1)}, u32[]{:S(2)}, u32[]{:S(2)}) collective-permute-start(bf16[4,96,768]{2,1,0:T(8,128)(2,1)S(1)} %gradient_send.10), channel_id=1, source_target_pairs={{0,4},{2,6},{4,0},{6,2},{1,5},{3,7},{5,1},{7,3},{8,12},{10,14},{12... | collective-permute-start | bytes 1769480 | tf_op jit(solution)/shard_map/ppermute | solution.py:630
  440.9 33.1 %collective-permute-start.42 = (bf16[4,96,768]{2,1,0:T(8,128)(2,1)S(1)}, bf16[4,96,768]{2,1,0:T(8,128)(2,1)S(1)}, u32[]{:S(2)}, u32[]{:S(2)}) collective-permute-start(bf16[4,96,768]{2,1,0:T(8,128)(2,1)S(1)} %gradient_send.11), channel_id=1, source_target_pairs={{0,4},{2,6},{4,0},{6,2},{1,5},{3,7},{5,1},{7,3},{8,12},{10,14},{12... | collective-permute-start | bytes 1769480 | tf_op jit(solution)/shard_map/ppermute | solution.py:630
  449.3 28.7 %collective-permute-start.46 = (bf16[96,768]{1,0:T(8,128)(2,1)S(1)}, bf16[96,768]{1,0:T(8,128)(2,1)S(1)}, u32[]{:S(2)}, u32[]{:S(2)}) collective-permute-start(bf16[96,768]{1,0:T(8,128)(2,1)S(1)} %get-tuple-element.751), channel_id=1, source_target_pairs={{0,8},{8,16},{16,24},{24,0},{1,9},{9,17},{17,25},{25,1},{2,10},{10... | collective-permute-start | bytes 442376 | tf_op jit(solution)/shard_map/ppermute | solution.py:635
  449.4 39.7 %collective-permute-start.47 = (bf16[96,768]{1,0:T(8,128)(2,1)S(1)}, bf16[96,768]{1,0:T(8,128)(2,1)S(1)}, u32[]{:S(2)}, u32[]{:S(2)}) collective-permute-start(bf16[96,768]{1,0:T(8,128)(2,1)S(1)} %get-tuple-element.752), channel_id=1, source_target_pairs={{0,16},{8,24},{16,0},{24,8},{1,17},{9,25},{17,1},{25,9},{2,18},{10... | collective-permute-start | bytes 442376 | tf_op jit(solution)/shard_map/ppermute | solution.py:635
  467.2 22.0 %collective-permute-start.48 = (bf16[96,768]{1,0:T(8,128)(2,1)S(1)}, bf16[96,768]{1,0:T(8,128)(2,1)S(1)}, u32[]{:S(2)}, u32[]{:S(2)}) collective-permute-start(bf16[96,768]{1,0:T(8,128)(2,1)S(1)} %get-tuple-element.753), channel_id=1, source_target_pairs={{0,24},{8,0},{16,8},{24,16},{1,25},{9,1},{17,9},{25,17},{2,26},{10... | collective-permute-start | bytes 442376 | tf_op jit(solution)/shard_map/ppermute | solution.py:635
  478.0 24.1 %collective-permute-start.44 = (bf16[96,768]{1,0:T(8,128)(2,1)S(1)}, bf16[96,768]{1,0:T(8,128)(2,1)S(1)}, u32[]{:S(2)}, u32[]{:S(2)}) collective-permute-start(bf16[96,768]{1,0:T(8,128)(2,1)S(1)} %get-tuple-element.749), channel_id=1, source_target_pairs={{0,16},{8,24},{16,0},{24,8},{1,17},{9,25},{17,1},{25,9},{2,18},{10... | collective-permute-start | bytes 442376 | tf_op jit(solution)/shard_map/ppermute | solution.py:635
  489.2 17.6 %collective-permute-start.45 = (bf16[96,768]{1,0:T(8,128)(2,1)S(1)}, bf16[96,768]{1,0:T(8,128)(2,1)S(1)}, u32[]{:S(2)}, u32[]{:S(2)}) collective-permute-start(bf16[96,768]{1,0:T(8,128)(2,1)S(1)} %get-tuple-element.750), channel_id=1, source_target_pairs={{0,24},{8,0},{16,8},{24,16},{1,25},{9,1},{17,9},{25,17},{2,26},{10... | collective-permute-start | bytes 442376 | tf_op jit(solution)/shard_map/ppermute | solution.py:635
  489.2 17.6 %collective-permute-start.39 = (bf16[96,768]{1,0:T(8,128)(2,1)S(1)}, bf16[96,768]{1,0:T(8,128)(2,1)S(1)}, u32[]{:S(2)}, u32[]{:S(2)}) collective-permute-start(bf16[96,768]{1,0:T(8,128)(2,1)S(1)} %get-tuple-element.739), channel_id=1, source_target_pairs={{0,8},{8,16},{16,24},{24,0},{1,9},{9,17},{17,25},{25,1},{2,10},{10... | collective-permute-start | bytes 442376 | tf_op jit(solution)/shard_map/ppermute | solution.py:635
  491.2 34.9 %collective-permute-start.40 = (bf16[96,768]{1,0:T(8,128)(2,1)S(1)}, bf16[96,768]{1,0:T(8,128)(2,1)S(1)}, u32[]{:S(2)}, u32[]{:S(2)}) collective-permute-start(bf16[96,768]{1,0:T(8,128)(2,1)S(1)} %get-tuple-element.740), channel_id=1, source_target_pairs={{0,16},{8,24},{16,0},{24,8},{1,17},{9,25},{17,1},{25,9},{2,18},{10... | collective-permute-start | bytes 442376 | tf_op jit(solution)/shard_map/ppermute | solution.py:635
  502.1 24.0 %collective-permute-start.41 = (bf16[96,768]{1,0:T(8,128)(2,1)S(1)}, bf16[96,768]{1,0:T(8,128)(2,1)S(1)}, u32[]{:S(2)}, u32[]{:S(2)}) collective-permute-start(bf16[96,768]{1,0:T(8,128)(2,1)S(1)} %get-tuple-element.741), channel_id=1, source_target_pairs={{0,24},{8,0},{16,8},{24,16},{1,25},{9,1},{17,9},{25,17},{2,26},{10... | collective-permute-start | bytes 442376 | tf_op jit(solution)/shard_map/ppermute | solution.py:635
  (73 other events, 877.2 us)
Sparse Core Ops, SparseCore 0:
  18.8 174.5 all-gather.1
  345.5 43.7 reduce-scatter.3
  428.5 53.2 reduce-scatter.5
  484.0 49.8 reduce-scatter.7

commit v3 on v2

--- a/solution.py
+++ b/solution.py
@@ -30,20 +30,21 @@
     return lax.dot_general(a, b, (contract, ((), ())), preferred_element_type=f32)
 
 
-def fill_keys(count, blocks, kv_refs, kn_ref, kt_ref, vn_ref, vt_ref):
-    for s in range(count):
-        for b in range(blocks):
-            columns = slice(b * BLOCK, (b + 1) * BLOCK)
-            places = slice(s * BLOCK, (s + 1) * BLOCK)
-            key = kv_refs[s][0, 0, :, columns]
-            value = kv_refs[s][0, 1, :, columns]
-            kn_ref[b, places, :] = key.T
-            if kt_ref is not None:
-                kt_ref[b, :, places] = key
-            if vn_ref is not None:
-                vn_ref[b, places, :] = value.T
-            if vt_ref is not None:
-                vt_ref[b, :, places] = value
+def fill_keys(heads, count, blocks, kv_refs, kn_ref, kt_ref, vn_ref, vt_ref):
+    for h in range(heads):
+        for s in range(count):
+            for b in range(blocks):
+                columns = slice(b * BLOCK, (b + 1) * BLOCK)
+                places = slice(s * BLOCK, (s + 1) * BLOCK)
+                key = kv_refs[s][h, 0, :, columns]
+                value = kv_refs[s][h, 1, :, columns]
+                kn_ref[h, b, places, :] = key.T
+                if kt_ref is not None:
+                    kt_ref[h, b, :, places] = key
+                if vn_ref is not None:
+                    vn_ref[h, b, places, :] = value.T
+                if vt_ref is not None:
+                    vt_ref[h, b, :, places] = value
 
 
 def fill_places(count, stripes_ref, place_ref):
@@ -56,126 +57,145 @@
     return jnp.concatenate([row] * QUERY_PER_KV, axis=1)
 
 
-def block_of(ref, i):
+def block_of(ref, h, i):
     columns = slice(i * BLOCK, (i + 1) * BLOCK)
-    return jnp.concatenate([ref[0, g, :, columns] for g in range(QUERY_PER_KV)], axis=1)
-
-
-def forward_kernel(count, blocks, starts_ref, stripes_ref, place_q_ref, start_q_ref, q_ref, *rest):
+    return jnp.concatenate([ref[h, g, :, columns] for g in range(QUERY_PER_KV)], axis=1)
+
+
+def allowed_keys(place_ref, count, b, place_q, start_q):
+    place, offset = place_ref[...], b * (BLOCK * count)
+    allowed = place >= start_q - offset
+    return allowed if place_q is None else allowed & (place <= place_q - offset)
+
+
+def forward_kernel(heads, count, blocks, starts_ref, stripes_ref, place_q_ref, start_q_ref, q_ref, *rest):
     kv_refs = rest[:count]
     o_ref, lse_ref, kn_ref, vt_ref, place_ref = rest[count:]
-    fill_keys(count, blocks, kv_refs, kn_ref, None, None, vt_ref)
+    fill_keys(heads, count, blocks, kv_refs, kn_ref, None, None, vt_ref)
     fill_places(count, stripes_ref, place_ref)
     for i in range(blocks):
         columns = slice(i * BLOCK, (i + 1) * BLOCK)
-        query = block_of(q_ref, i)
+        queries = [block_of(q_ref, h, i) for h in range(heads)]
         place_q = twice(place_q_ref[:, columns])
         start_q = twice(start_q_ref[:, columns])
 
-        def scores_of(b):
-            scores = mm(kn_ref[b], query)
-            offset = b * (BLOCK * count)
-            place = place_ref[...]
-            allowed = (place >= start_q - offset) & (place <= place_q - offset)
-            return jnp.where(allowed, scores * SCORE_SCALE_2, masked_score)
-
-        scores = scores_of(i)
-        top = jnp.max(scores, axis=0, keepdims=True)
-        weights = jnp.exp2(scores - top)
-        total = jnp.sum(weights, axis=0, keepdims=True)
-        accum = mm(vt_ref[i], weights.astype(bf16))
+        def scores_of(b, place_q):
+            allowed = allowed_keys(place_ref, count, b, place_q, start_q)
+            scores = [mm(kn_ref[h, b], queries[h]) for h in range(heads)]
+            return [jnp.where(allowed, s * SCORE_SCALE_2, masked_score) for s in scores]
+
+        state = []
+        for h, scores in enumerate(scores_of(i, place_q)):
+            top = jnp.max(scores, axis=0, keepdims=True)
+            weights = jnp.exp2(scores - top)
+            total = jnp.sum(weights, axis=0, keepdims=True)
+            state.append((top, total, mm(vt_ref[h, i], weights.astype(bf16))))
 
         def step(b, carry):
-            top, total, accum = carry
-            scores = scores_of(b)
-            new_top = jnp.maximum(top, jnp.max(scores, axis=0, keepdims=True))
-            fade = jnp.exp2(top - new_top)
-            weights = jnp.exp2(scores - new_top)
-            total = total * fade + jnp.sum(weights, axis=0, keepdims=True)
-            accum = accum * fade + mm(vt_ref[b], weights.astype(bf16))
-            return new_top, total, accum
-
-        top, total, accum = lax.fori_loop(starts_ref[i], i, step, (top, total, accum))
-        result = (accum / total).astype(bf16)
-        lse = top + jnp.log2(total)
-        for g in range(QUERY_PER_KV):
-            part = slice(g * BLOCK, (g + 1) * BLOCK)
-            o_ref[0, g, :, columns] = result[:, part]
-            lse_ref[0, g : g + 1, columns] = lse[:, part]
+            result = []
+            for h, scores in enumerate(scores_of(b, None)):
+                top, total, accum = carry[h]
+                new_top = jnp.maximum(top, jnp.max(scores, axis=0, keepdims=True))
+                fade = jnp.exp2(top - new_top)
+                weights = jnp.exp2(scores - new_top)
+                total = total * fade + jnp.sum(weights, axis=0, keepdims=True)
+                accum = accum * fade + mm(vt_ref[h, b], weights.astype(bf16))
+                result.append((new_top, total, accum))
+            return tuple(result)
+
+        state = lax.fori_loop(starts_ref[i], i, step, tuple(state)) if i else state
+        for h, (top, total, accum) in enumerate(state):
+            result = (accum / total).astype(bf16)
+            lse = top + jnp.log2(total)
+            for g in range(QUERY_PER_KV):
+                part = slice(g * BLOCK, (g + 1) * BLOCK)
+                o_ref[h, g, :, columns] = result[:, part]
+                lse_ref[h, g : g + 1, columns] = lse[:, part]
 
 
 def backward_kernel(
-    count, blocks, starts_ref, stripes_ref, place_q_ref, start_q_ref, q_ref, do_ref, o_ref, lse_ref, *rest
+    heads, count, blocks, starts_ref, stripes_ref, place_q_ref, start_q_ref, q_ref, do_ref, o_ref, lse_ref, *rest
 ):
     kv_refs = rest[:count]
     dq_ref = rest[count]
     dkv_refs = rest[count + 1 : 2 * count + 1]
     kn_ref, kt_ref, vn_ref, place_ref, dk_ref, dv_ref = rest[2 * count + 1 :]
-    fill_keys(count, blocks, kv_refs, kn_ref, kt_ref, vn_ref, None)
+    fill_keys(heads, count, blocks, kv_refs, kn_ref, kt_ref, vn_ref, None)
     fill_places(count, stripes_ref, place_ref)
-    dk_ref[...] = jnp.zeros_like(dk_ref)
-    dv_ref[...] = jnp.zeros_like(dv_ref)
     for i in range(blocks):
         columns = slice(i * BLOCK, (i + 1) * BLOCK)
-        query = block_of(q_ref, i)
-        d_out = block_of(do_ref, i)
-        out = block_of(o_ref, i)
-        query_rows = query.T
-        d_out_rows = d_out.T
-        delta = jnp.sum(d_out.astype(f32) * out.astype(f32), axis=0, keepdims=True)
-        lse = jnp.concatenate([lse_ref[0, g : g + 1, columns] for g in range(QUERY_PER_KV)], axis=1)
         place_q = twice(place_q_ref[:, columns])
         start_q = twice(start_q_ref[:, columns])
-
-        def step(b, d_query):
-            scores = mm(kn_ref[b], query)
-            offset = b * (BLOCK * count)
-            place = place_ref[...]
-            allowed = (place >= start_q - offset) & (place <= place_q - offset)
-            probs = jnp.exp2(jnp.where(allowed, scores * SCORE_SCALE_2, masked_score) - lse)
-            d_prob = mm(vn_ref[b], d_out)
-            d_score = (probs * (d_prob - delta)).astype(bf16)
-            dv_ref[b] += mm(probs.astype(bf16), d_out_rows)
-            dk_ref[b] += mm(d_score, query_rows)
-            return d_query + mm(kt_ref[b], d_score)
-
-        d_query = lax.fori_loop(
-            starts_ref[i], i + 1, step, jnp.zeros((HEAD_SIZE, QUERY_PER_KV * BLOCK), f32)
-        )
-        for g in range(QUERY_PER_KV):
-            dq_ref[0, g, :, columns] = d_query[:, g * BLOCK : (g + 1) * BLOCK] * SCORE_SCALE
-    for s in range(count):
-        places = slice(s * BLOCK, (s + 1) * BLOCK)
-        for b in range(blocks):
-            columns = slice(b * BLOCK, (b + 1) * BLOCK)
-            dkv_refs[s][0, 0, :, columns] = (dk_ref[b, places, :] * SCORE_SCALE).T.astype(bf16)
-            dkv_refs[s][0, 1, :, columns] = dv_ref[b, places, :].T.astype(bf16)
-
-
-def head_spec(*dims):
-    return pl.BlockSpec((1, *dims), lambda h, *_: (h,) + (0,) * len(dims))
+        parts = []
+        for h in range(heads):
+            query, d_out, out = (block_of(ref, h, i) for ref in (q_ref, do_ref, o_ref))
+            delta = jnp.sum(d_out.astype(f32) * out.astype(f32), axis=0, keepdims=True)
+            lse = jnp.concatenate(
+                [lse_ref[h, g : g + 1, columns] for g in range(QUERY_PER_KV)], axis=1
+            )
+            parts.append((query, query.T, d_out, d_out.T, delta, lse))
+
+        def terms(b, place_q, first):
+            allowed = allowed_keys(place_ref, count, b, place_q, start_q)
+            d_queries = []
+            for h, (query, query_rows, d_out, d_out_rows, delta, lse) in enumerate(parts):
+                scores = mm(kn_ref[h, b], query)
+                d_prob = mm(vn_ref[h, b], d_out)
+                probs = jnp.exp2(jnp.where(allowed, scores * SCORE_SCALE_2, masked_score) - lse)
+                d_score = (probs * (d_prob - delta)).astype(bf16)
+                d_value = mm(probs.astype(bf16), d_out_rows)
+                d_key = mm(d_score, query_rows)
+                if first:
+                    dv_ref[h, b] = d_value
+                    dk_ref[h, b] = d_key
+                else:
+                    dv_ref[h, b] += d_value
+                    dk_ref[h, b] += d_key
+                d_queries.append(mm(kt_ref[h, b], d_score))
+            return d_queries
+
+        def step(b, carry):
+            return tuple(a + t for a, t in zip(carry, terms(b, None, False)))
+
+        d_queries = tuple(terms(i, place_q, True))
+        if i:
+            d_queries = lax.fori_loop(starts_ref[i], i, step, d_queries)
+        for h in range(heads):
+            for g in range(QUERY_PER_KV):
+                dq_ref[h, g, :, columns] = d_queries[h][:, g * BLOCK : (g + 1) * BLOCK] * SCORE_SCALE
+    for h in range(heads):
+        for s in range(count):
+            places = slice(s * BLOCK, (s + 1) * BLOCK)
+            for b in range(blocks):
+                columns = slice(b * BLOCK, (b + 1) * BLOCK)
+                dkv_refs[s][h, 0, :, columns] = (dk_ref[h, b, places, :] * SCORE_SCALE).T.astype(bf16)
+                dkv_refs[s][h, 1, :, columns] = dv_ref[h, b, places, :].T.astype(bf16)
+
+
+def head_spec(heads, *dims):
+    return pl.BlockSpec((heads, *dims), lambda n, *_: (0,) * (1 + len(dims)))
 
 
 def row_spec(tokens):
-    return pl.BlockSpec((1, tokens), lambda h, *_: (0, 0))
+    return pl.BlockSpec((1, tokens), lambda n, *_: (0, 0))
 
 
 def attention_forward(queries, pieces, starts, stripes, place, start):
     heads, _, _, tokens = queries.shape
     count, blocks = len(pieces), tokens // BLOCK
     keys = count * BLOCK
-    per_query = head_spec(QUERY_PER_KV, HEAD_SIZE, tokens)
-    per_kv = head_spec(2, HEAD_SIZE, tokens)
-    return pl.pallas_call(
-        functools.partial(forward_kernel, count, blocks),
+    per_query = head_spec(heads, QUERY_PER_KV, HEAD_SIZE, tokens)
+    per_kv = head_spec(heads, 2, HEAD_SIZE, tokens)
+    return pl.pallas_call(
+        functools.partial(forward_kernel, heads, count, blocks),
         grid_spec=pltpu.PrefetchScalarGridSpec(
             num_scalar_prefetch=2,
-            grid=(heads,),
+            grid=(1,),
             in_specs=[row_spec(tokens)] * 2 + [per_query] + [per_kv] * count,
-            out_specs=[per_query, head_spec(QUERY_PER_KV, tokens)],
+            out_specs=[per_query, head_spec(heads, QUERY_PER_KV, tokens)],
             scratch_shapes=[
-                pltpu.VMEM((blocks, keys, HEAD_SIZE), bf16),
-                pltpu.VMEM((blocks, HEAD_SIZE, keys), bf16),
+                pltpu.VMEM((heads, blocks, keys, HEAD_SIZE), bf16),
+                pltpu.VMEM((heads, blocks, HEAD_SIZE, keys), bf16),
                 pltpu.VMEM((keys, QUERY_PER_KV * BLOCK), jnp.int32),
             ],
         ),
@@ -193,25 +213,25 @@
     heads, _, _, tokens = queries.shape
     count, blocks = len(pieces), tokens // BLOCK
     keys = count * BLOCK
-    per_query = head_spec(QUERY_PER_KV, HEAD_SIZE, tokens)
-    per_kv = head_spec(2, HEAD_SIZE, tokens)
-    return pl.pallas_call(
-        functools.partial(backward_kernel, count, blocks),
+    per_query = head_spec(heads, QUERY_PER_KV, HEAD_SIZE, tokens)
+    per_kv = head_spec(heads, 2, HEAD_SIZE, tokens)
+    return pl.pallas_call(
+        functools.partial(backward_kernel, heads, count, blocks),
         grid_spec=pltpu.PrefetchScalarGridSpec(
             num_scalar_prefetch=2,
-            grid=(heads,),
+            grid=(1,),
             in_specs=[row_spec(tokens)] * 2
             + [per_query] * 3
-            + [head_spec(QUERY_PER_KV, tokens)]
+            + [head_spec(heads, QUERY_PER_KV, tokens)]
             + [per_kv] * count,
             out_specs=[per_query] + [per_kv] * count,
             scratch_shapes=[
-                pltpu.VMEM((blocks, keys, HEAD_SIZE), bf16),
-                pltpu.VMEM((blocks, HEAD_SIZE, keys), bf16),
-                pltpu.VMEM((blocks, keys, HEAD_SIZE), bf16),
+                pltpu.VMEM((heads, blocks, keys, HEAD_SIZE), bf16),
+                pltpu.VMEM((heads, blocks, HEAD_SIZE, keys), bf16),
+                pltpu.VMEM((heads, blocks, keys, HEAD_SIZE), bf16),
                 pltpu.VMEM((keys, QUERY_PER_KV * BLOCK), jnp.int32),
-                pltpu.VMEM((blocks, keys, HEAD_SIZE), f32),
-                pltpu.VMEM((blocks, keys, HEAD_SIZE), f32),
+                pltpu.VMEM((heads, blocks, keys, HEAD_SIZE), f32),
+                pltpu.VMEM((heads, blocks, keys, HEAD_SIZE), f32),
             ],
         ),
         out_shape=[jax.ShapeDtypeStruct(queries.shape, f32)]
@@ -251,7 +271,7 @@
             out_specs=pl.BlockSpec((rows, width), lambda n, _: (0, 0)),
         ),
         out_shape=jax.ShapeDtypeStruct((rows, width), bf16),
-        compiler_params=pltpu.CompilerParams(vmem_limit_bytes=32 << 20),
+        compiler_params=pltpu.CompilerParams(vmem_limit_bytes=60 << 20),
         cost_estimate=SMALL_COST,
         name="pack",
     )(index[None], feedforward_weight, out_share, out_other)
@@ -686,7 +706,7 @@
         source = (index - 2 * by) % count
         whole = placed(whole, moved, source)
         whole = placed(whole, core_swap(moved), source ^ 1)
-    return whole, all_gains
+    return whole, all_gains, fetched
 
 
 def gradient_kernel(pairs, turned, pieces, place_ref, *refs):
@@ -853,8 +873,9 @@
     out_share = share(output_weight)
     out_other = tp_swap(out_share)
     payload = packed_share(feedforward_weight, out_share, out_other, ctx_index, share)
+    wq, gain_rows, fetched = gathered_rows(query_key_value_weight, gains, payload)
+    payload = lax.optimization_barrier((payload, fetched[0]))[0]
     others = lax.all_gather(payload, ("fsdp", "ctx"), axis=0, tiled=True)
-    wq, gain_rows = gathered_rows(query_key_value_weight, gains, payload)
 
     lengths, stripe_row = doc_lengths[0], stripe[0]
     packed, start = slot_meta(ctx_index, tokens, stripe_row, lengths)
@@ -964,6 +985,11 @@
         gate_part, activated, d_gate, d_up, left_two, others
     )
     right_gate, right_up = (d_gate, other_gate), (d_up, other_up)
+    shares = order(
+        lambda ffn, qkv: [share(ffn[0]), share(ffn[1]), share(qkv)],
+        feedforward_weight,
+        query_key_value_weight,
+    )
     down_arrived, gate_products, down_sum, d_two_sent = order(
         touch, down_arrived, gate_products, down_sum, d_two_sent
     )
@@ -977,7 +1003,6 @@
         gain_rows[1:],
         others,
     )
-    down_scattered = gradient_scatter(order(gradient_chip, left_dy, right_act, down_arrived))
     d_att = d_att.reshape(CHUNKS, chunk, QUERY_PER_KV, HEAD_SIZE, tokens)
 
     def attend_back(query, d_att, attended, lse, pieces, *meta):
@@ -997,7 +1022,9 @@
     d_query_0, d_kv_0 = attention_step(0)
     gate_arrived, up_products = order(touch, gate_arrived, up_products)
     up_arrived = gradient_send(up_products)
-    gate_scattered = gradient_scatter(order(gradient_chip, left_two, right_gate, gate_arrived))
+    down_chip = order(gradient_chip, left_dy, right_act, down_arrived)
+    gate_chip = order(gradient_chip, left_two, right_gate, gate_arrived)
+    two_scattered = gradient_scatter(jnp.concatenate([down_chip, gate_chip], axis=2))
     d_query_1, d_kv_1 = attention_step(1)
 
     def branch_part(d_branch, core, right_att):
@@ -1007,8 +1034,9 @@
         return inner(turned_products, left, right_att), left
 
     out_products, left_branch = order.apart(branch_part, d_branch, core, right_att)
-    out_arrived = gradient_send(out_products)
-    d_kv_0, d_kv_1, down_sent = order(touch, d_kv_0, d_kv_1, down_sent)
+    up_chip = order(gradient_chip, left_two, right_up, up_arrived)
+    d_kv_0, d_kv_1, down_sent, up_chip = order(touch, d_kv_0, d_kv_1, down_sent, up_chip)
+    up_scattered = gradient_scatter(up_chip)
 
     def project_back(d_query, d_kv, wq, *tables):
         inner = Order()
@@ -1020,49 +1048,47 @@
         project_back, [d_query_0, d_query_1], [d_kv_0, d_kv_1], wq, *tables
     )
     d_one_sent = tp_send(d_one_part)
-    up_scattered = gradient_scatter(order(gradient_chip, left_two, right_up, up_arrived))
     right_proj = list(zip(d_proj, other_proj))
-    qkv_arrived = [
-        gradient_send(order(turned_products, left_one, right_proj[c])) for c in range(CHUNKS)
-    ]
-    finish = functools.partial(gradient_chip, turned=True, pieces=True)
-    out_terms = gradient_groups(order(finish, left_branch, right_att, out_arrived))
-    hidden_out = order(lambda m, s: (m + tp_add(s)).astype(bf16), middle, down_sent)
-    qkv_terms = [
-        gradient_groups(order(finish, left_one, right_proj[c], qkv_arrived[c]))
-        for c in range(CHUNKS)
-    ]
-    grad_out = order(gradient_sum, out_terms)
-    grad_qkv = order(
-        lambda *terms: jnp.concatenate([gradient_sum(t) for t in terms], axis=1), *qkv_terms
-    )
+
+    two_scattered = order(touch, two_scattered)[0]
+
+    def tail(left_one, right_proj, left_branch, right_att, out_products, middle, down_sent):
+        inner = Order()
+        out_arrived = gradient_send(out_products)
+        finish = functools.partial(gradient_chip, turned=True, pieces=True)
+        arrived = gradient_send(inner(turned_products, left_one, right_proj[0]))
+        terms = gradient_groups(inner(finish, left_branch, right_att, out_arrived))
+        products = inner(turned_products, left_one, right_proj[1])
+        hidden_out = inner(lambda m, s: (m + tp_add(s)).astype(bf16), middle, down_sent)
+        grad_out = inner(gradient_sum, terms)
+        arrived_1 = gradient_send(lax.optimization_barrier((products, grad_out))[0])
+        terms = gradient_groups(inner(finish, left_one, right_proj[0], arrived))
+        chip = inner(finish, left_one, right_proj[1], arrived_1)
+        return grad_out, hidden_out, inner(gradient_sum, terms), chip
+
+    grad_out, hidden_out, grad_qkv_0, chip = order.apart(
+        tail, left_one, right_proj, left_branch, right_att, out_products, middle, down_sent
+    )
+    terms = gradient_groups(chip)
     own_gains = lax.dynamic_slice_in_dim(
         gains, ctx_index * out_share.shape[0], out_share.shape[0], 1
     ).astype(f32)
 
-    def gain_parts(grad_qkv, grad_gate, grad_up):
-        return jnp.stack(
-            [
-                gain_gradient([share(query_key_value_weight)], [grad_qkv], own_gains[0]),
-                gain_gradient(
-                    [share(feedforward_weight[i]) for i in range(2)],
-                    [grad_gate, grad_up],
-                    own_gains[1],
-                ),
-            ],
-            axis=0,
-        )
-
-    grad_gains = order(gain_parts, grad_qkv, gate_scattered, up_scattered)
-    gains_other = tp_swap(grad_gains)
-    grad_ffn = order(
-        lambda *parts: jnp.stack(parts, axis=0).astype(f32),
-        gate_scattered,
-        up_scattered,
-        down_scattered,
-    )
-    grad_gains = order(lambda a, b: a + b, grad_gains, gains_other)
+    def ffn_gradient(two, up):
+        down, gate = two[:, :units], two[:, units:]
+        gain = gain_gradient(shares[:2], [gate, up], own_gains[1])
+        return jnp.stack([gate, up, down], axis=0).astype(f32), gain
+
+    grad_ffn, gain_two = order(ffn_gradient, two_scattered, up_scattered)
     grad_in = order(input_gradient, d_one_sent, x, d_mid, gain_rows[:1])
+
+    def qkv_gradient(first, terms, gain_two):
+        whole = jnp.concatenate([first, gradient_sum(terms)], axis=1)
+        gain_one = gain_gradient(shares[2:], [whole], own_gains[0])
+        return jnp.stack([gain_one, gain_two], axis=0), whole
+
+    grad_gains, grad_qkv = order(qkv_gradient, grad_qkv_0, terms, gain_two)
+    grad_gains = grad_gains + tp_swap(grad_gains)
     return (hidden_out[None], grad_in[None], grad_qkv, grad_out, grad_ffn, grad_gains)
 
 

time: 562 us -> 513 us (0.913)
  waiting for transfers between devices: 191 us -> 158 us
  starting transfers between devices: 61 us -> 43.5 us
    ppermute x12, waiting for transfers between devices: 52.7 us -> 18.4 us  [group_shift(): lax.ppermute(value, 'fsdp', [(i, (i + by) % size) for i in range(size)])]
    ppermute x12, starting transfers between devices: 34.9 us -> 20.2 us  [group_shift(): lax.ppermute(value, 'fsdp', [(i, (i + by) % size) for i in range(size)])]
    unnamed x98 -> x82, local copies, waits for them, and re-layouts: 16.6 us -> 8.71 us
  transfers between devices with their start and end apart: 54 -> 53, of which waited for: 28 -> 30; matrix products, arithmetic and copies ran while one was open for 7% -> 9% of each run, Pallas kernels for 31% -> 34%
where the time goes in v3:
time: 513 us; the launch traced here: 503 us
  Pallas kernels  226 us (44%)
  waiting for transfers between devices  158 us (31%)
  starting transfers between devices  43.5 us (8%)
  local copies, waits for them, and re-layouts  30.1 us (6%)
  other arithmetic  27.8 us (5%)
  between operations  14.6 us (3%)
    ppermute x11, waiting for transfers between devices, chip_shift(): lax.ppermute(value, 'ctx', [(i, (i + 2 * by) % size) for i in range(size)])  94.2 us
    pallas_call x12, Pallas kernels, gradient_call(): pl.pallas_call(functools.partial(gradient_kernel, len(left), turned, piec...  65.1 us
    pallas_call x1, Pallas kernels, feed_forward(): pl.pallas_call(ffn_kernel, grid=(units // FFN_BLOCK,), in_specs=[whole, w...  34.2 us
    pallas_call x2, Pallas kernels, attention_backward(): pl.pallas_call(functools.partial(backward_kernel, heads, count, blocks),...  32.8 us
    ppermute x20, waiting for transfers between devices, core_swap(): return lax.ppermute(value, 'ctx', [(i, i ^ 1) for i in range(size)])  28.3 us
    pallas_call x2, Pallas kernels, attention_forward(): pl.pallas_call(functools.partial(forward_kernel, heads, count, blocks), g...  25.4 us
    ppermute x12, starting transfers between devices, group_shift(): lax.ppermute(value, 'fsdp', [(i, (i + by) % size) for i in range(size)])  20.2 us
    ppermute x12, waiting for transfers between devices, group_shift(): lax.ppermute(value, 'fsdp', [(i, (i + by) % size) for i in range(size)])  18.4 us
  transfers between devices with their start and end apart: 53, of which 30 were waited for; matrix products, arithmetic and copies ran while one was open for 9% of the time, Pallas kernels for 34%

profile of v3, /device:TPU:0, one launch (start us, length us, event | category | flops | bytes accessed | tf_op | source)
XLA Modules:
  0.0 502.6 jit_solution(1420870692617392977)
XLA Ops:
  38.4 17.0 %collective-permute-done.28 = bf16[112,1536]{1,0:T(8,128)(2,1)} collective-permute-done((bf16[112,1536]{1,0:T(8,128)(2,1)S(1)}, bf16[112,1536]{1,0:T(8,128)(2,1)}, u32[]{:S(2)}, u32[]{:S(2)}) %collective-permute-start.28) | collective-permute-done | bytes 344096 | tf_op jit(solution)/shard_map/ppermute | solution.py:655
  65.1 33.9 %collective-permute-done.32 = bf16[3,96,1536]{2,1,0:T(8,128)(2,1)S(1)} collective-permute-done((bf16[3,96,1536]{2,1,0:T(8,128)(2,1)S(1)}, bf16[3,96,1536]{2,1,0:T(8,128)(2,1)S(1)}, u32[]{:S(2)}, u32[]{:S(2)}) %collective-permute-start.32) | collective-permute-done | bytes 884768 | tf_op jit(solution)/shard_map/ppermute | solution.py:650
  120.7 14.1 %collective-permute-done.34 = bf16[2,2,96,768]{3,2,1,0:T(8,128)(2,1)} collective-permute-done((bf16[2,2,96,768]{3,2,1,0:T(8,128)(2,1)}, bf16[2,2,96,768]{3,2,1,0:T(8,128)(2,1)}, u32[]{:S(2)}, u32[]{:S(2)}) %collective-permute-start.34) | collective-permute-done | bytes 589856 | tf_op jit(solution)/shard_map/ppermute | solution.py:650
  134.8 17.6 %conditional.14 = (bf16[2,2,96,768]{3,2,1,0:T(8,128)(2,1)}, f32[2,2,768]{2,1,0:T(2,128)}, bf16[2,2,96,768]{3,2,1,0:T(8,128)(2,1)}, bf16[384,768]{1,0:T(8,128)(2,1)}) conditional(s32[]{:T(128)} %bitcast.14, () %tuple.182, (bf16[2,2,96,768]{3,2,1,0:T(8,128)(2,1)}, s32[6]{0:T(128)}, s32[4]{0:T(128)}, s32[1,768]{1,0:T(1,128)}, s32[1,768]{1,0:T(1,128)}, ...), branch_computations={%region_8.9_spmd, %region_9.10_spmd} | conditional | flops 1 | bytes 3539017 | solution.py:634
  137.1 12.9 %attention_forward.2 = (bf16[2,2,96,768]{3,2,1,0:T(8,128)(2,1)}, f32[2,2,768]{2,1,0:T(2,128)}) custom-call(s32[6]{0:T(128)} %get-tuple-element.174.starts_ref, s32[4]{0:T(128)} %get-tuple-element.175.stripes_ref, s32[1,768]{1,0:T(1,128)} %get-tuple-element.176.place_q_ref, s32[1,768]{1,0:T(1,128)} %get-tuple-element.177.start_q_ref, ...), custom_call_target="tpu_custom_call" | custom-call | flops 1 | bytes 1 | tf_op jit(solution)/shard_map/cond/branch_1_fun/attention_forward/pallas_call | solution.py:189
  152.4 7.2 %collective-permute-done.35 = bf16[2,2,96,768]{3,2,1,0:T(8,128)(2,1)S(1)} collective-permute-done((bf16[2,2,96,768]{3,2,1,0:T(8,128)(2,1)}, bf16[2,2,96,768]{3,2,1,0:T(8,128)(2,1)S(1)}, u32[]{:S(2)}, u32[]{:S(2)}) %collective-permute-start.35) | collective-permute-done | bytes 589856 | tf_op jit(solution)/shard_map/ppermute | solution.py:650
  161.2 16.2 %conditional.15 = (bf16[2,2,96,768]{3,2,1,0:T(8,128)(2,1)}, f32[2,2,768]{2,1,0:T(2,128)}, bf16[2,2,96,768]{3,2,1,0:T(8,128)(2,1)}, bf16[384,768]{1,0:T(8,128)(2,1)S(1)}) conditional(s32[]{:T(128)} %bitcast.14, () %tuple.185, (bf16[2,2,96,768]{3,2,1,0:T(8,128)(2,1)S(1)}, s32[6]{0:T(128)}, s32[4]{0:T(128)}, s32[1,768]{1,0:T(1,128)}, ...), branch_computations={%region_10.11_spmd, %region_11.12_spmd} | conditional | flops 1 | bytes 3539017 | solution.py:634
  163.8 12.6 %attention_forward.3 = (bf16[2,2,96,768]{3,2,1,0:T(8,128)(2,1)}, f32[2,2,768]{2,1,0:T(2,128)}) custom-call(s32[6]{0:T(128)} %get-tuple-element.184.starts_ref, s32[4]{0:T(128)} %get-tuple-element.185.stripes_ref, s32[1,768]{1,0:T(1,128)} %get-tuple-element.186.place_q_ref, s32[1,768]{1,0:T(1,128)} %get-tuple-element.187.start_q_ref, ...), custom_call_target="tpu_custom_call" | custom-call | flops 1 | bytes 1 | tf_op jit(solution)/shard_map/cond/branch_1_fun/attention_forward/pallas_call | solution.py:189
  178.7 7.2 %conditional.16 = (bf16[768,768]{1,0:T(8,128)(2,1)}, bf16[768,768]{1,0:T(8,128)(2,1)}) conditional(s32[]{:T(128)} %bitcast.14, () %tuple.190, (bf16[384,768]{1,0:T(8,128)(2,1)}, bf16[384,768]{1,0:T(8,128)(2,1)}) %tuple.275), branch_computations={%region_12.13_spmd, %region_13.14_spmd} | conditional | bytes 7077944 | solution.py:634
  185.9 8.0 %collective-permute-done.37.refs_3_ = bf16[384,768]{1,0:T(8,128)(2,1)S(1)} collective-permute-done((bf16[384,768]{1,0:T(8,128)(2,1)}, bf16[384,768]{1,0:T(8,128)(2,1)S(1)}, u32[]{:S(2)}, u32[]{:S(2)}) %collective-permute-start.37) | collective-permute-done | bytes 589856 | tf_op jit(solution)/shard_map/ppermute | solution.py:659
  193.9 9.4 %middle.1 = (f32[768,1536]{1,0:T(8,128)}, bf16[768,1536]{1,0:T(8,128)(2,1)S(1)}) custom-call(s32[1]{0:T(128)} %bitcast.48.tp_ref, bf16[768,1536]{1,0:T(8,128)(2,1)S(1)} %bitcast.114, f32[1,1536]{1,0:T(1,128)S(1)} %get-tuple-element.694.gain_ref, bf16[384,768]{1,0:T(8,128)(2,1)} %get-tuple-element.656.refs_0_, bf16[384,768]{1,0:T(8,128)(2,1)} %copy-done.11, ...), custom_call_target="tpu_custom_call" | custom-call | flops 1 | bytes 1 | tf_op jit(solution)/shard_map/middle/pallas_call | solution.py:378
  203.2 34.2 %feed_forward.1 = (bf16[768,2048]{1,0:T(8,128)(2,1)}, bf16[768,2048]{1,0:T(8,128)(2,1)}, bf16[768,2048]{1,0:T(8,128)(2,1)}, bf16[768,1536]{1,0:T(8,128)(2,1)}) custom-call(bf16[768,1536]{1,0:T(8,128)(2,1)S(1)} %get-tuple-element.668.h_ref, bf16[768,1536]{1,0:T(8,128)(2,1)} %bitcast.116, ...), custom_call_target="tpu_custom_call" | custom-call | flops 1 | bytes 1 | tf_op jit(solution)/shard_map/feed_forward/pallas_call | solution.py:568
  237.9 13.1 %conditional.17 = (bf16[4,96,2048]{2,1,0:T(8,128)(2,1)}, bf16[768,2048]{1,0:T(8,128)(2,1)}, bf16[4,2,96,768]{3,2,1,0:T(8,128)(2,1)}, bf16[4,2,96,768]{3,2,1,0:T(8,128)(2,1)}) conditional(s32[]{:T(128)} %bitcast.14, () %tuple.181, (bf16[768,2048]{1,0:T(8,128)(2,1)}, bf16[768,1536]{1,0:T(8,128)(2,1)S(1)}, s32[]{:T(128)}, ...), branch_computations={%region_14.15_spmd, %region_15.16_spmd} | conditional | flops 37 | bytes 17301968 | solution.py:634
  243.9 7.1 %gradient_send.6 = bf16[4,96,2048]{2,1,0:T(8,128)(2,1)} custom-call(s32[2]{0:T(128)S(1)} %pad_add_fusion.place_ref, bf16[4,2,96,768]{3,2,1,0:T(8,128)(2,1)} %get-tuple-element.204.refs_0_, bf16[768,2048]{1,0:T(8,128)(2,1)} %get-tuple-element.205.refs_1_, bf16[4,2,96,768]{3,2,1,0:T(8,128)(2,1)} %get-tuple-element.206.refs_2_, ...), custom_call_target="tpu_custom_call" | custom-call | flops 1 | bytes 1 | tf_op jit(solution)/shard_map/cond/branch_1_fun/gradient_send/pallas_call | solution.py:771
  252.6 23.9 %conditional.18 = (bf16[4,96,2048]{2,1,0:T(8,128)(2,1)}, bf16[4,96,2048]{2,1,0:T(8,128)(2,1)}, bf16[768,1536]{1,0:T(8,128)(2,1)}, bf16[768,2048]{1,0:T(8,128)(2,1)}, bf16[768,2048]{1,0:T(8,128)(2,1)}) conditional(s32[]{:T(128)} %bitcast.14, () %tuple.197, (bf16[768,2048]{1,0:T(8,128)(2,1)}, bf16[768,2048]{1,0:T(8,128)(2,1)}, ...), branch_computations={%region_16.17_spmd, %region_17.18_spmd} | conditional | flops 38 | bytes 25166296 | solution.py:634
  252.6 8.9 %down_project.1 = bf16[768,1536]{1,0:T(8,128)(2,1)} custom-call(bf16[768,2048]{1,0:T(8,128)(2,1)} %get-tuple-element.214.a_ref, bf16[1536,7680]{1,0:T(8,128)(2,1)} %get-tuple-element.215.w_ref), custom_call_target="tpu_custom_call" | custom-call | flops 1 | bytes 1 | tf_op jit(solution)/shard_map/cond/branch_1_fun/down_project/pallas_call | solution.py:409
  262.1 7.1 %gradient_send.7 = bf16[4,96,2048]{2,1,0:T(8,128)(2,1)} custom-call(s32[2]{0:T(128)S(1)} %pad_add_fusion.1.place_ref, bf16[4,2,96,768]{3,2,1,0:T(8,128)(2,1)} %get-tuple-element.222.refs_0_, bf16[768,2048]{1,0:T(8,128)(2,1)} %get-tuple-element.217.refs_1_, bf16[4,2,96,768]{3,2,1,0:T(8,128)(2,1)} %get-tuple-element.224.refs_2_, ...), custom_call_target="tpu_custom_call" | custom-call | flops 1 | bytes 1 | tf_op jit(solution)/shard_map/cond/branch_1_fun/gradient_send/pallas_call | solution.py:771
  269.2 7.1 %gradient_send.8 = bf16[4,96,2048]{2,1,0:T(8,128)(2,1)} custom-call(s32[2]{0:T(128)S(1)} %pad_add_fusion.1.place_ref, bf16[4,2,96,768]{3,2,1,0:T(8,128)(2,1)} %get-tuple-element.222.refs_0_, bf16[768,2048]{1,0:T(8,128)(2,1)} %get-tuple-element.223.refs_1_, bf16[4,2,96,768]{3,2,1,0:T(8,128)(2,1)} %get-tuple-element.224.refs_2_, ...), custom_call_target="tpu_custom_call" | custom-call | flops 1 | bytes 1 | tf_op jit(solution)/shard_map/cond/branch_1_fun/gradient_send/pallas_call | solution.py:771
  280.6 7.1 %collective-permute-done.38.refs_4_ = bf16[4,96,2048]{2,1,0:T(8,128)(2,1)} collective-permute-done((bf16[4,96,2048]{2,1,0:T(8,128)(2,1)}, bf16[4,96,2048]{2,1,0:T(8,128)(2,1)}, u32[]{:S(2)}, u32[]{:S(2)}) %collective-permute-start.38) | collective-permute-done | bytes 1572896 | tf_op jit(solution)/shard_map/ppermute | solution.py:650
  293.7 9.4 %d_middle.1 = (f32[768,1536]{1,0:T(8,128)}, bf16[768,1536]{1,0:T(8,128)(2,1)}, bf16[768,768]{1,0:T(8,128)(2,1)S(1)}) custom-call(bf16[768,1536]{1,0:T(8,128)(2,1)S(1)} %copy-done.6, bf16[768,1536]{1,0:T(8,128)(2,1)} %collective-permute-done.39.other_ref, f32[768,1536]{1,0:T(8,128)} %get-tuple-element.796.middle_ref, bf16[768,1536]{1,0:T(8,128)(2,1)} %bitcast.117, ...), custom_call_target="tpu_custom_call" | custom-call | flops 1 | bytes 1 | tf_op jit(solution)/shard_map/d_middle/pallas_call | solution.py:446
  304.3 20.2 %conditional.19 = (f32[2,2,96,768]{3,2,1,0:T(8,128)}, bf16[2,2,96,768]{3,2,1,0:T(8,128)(2,1)S(1)}, bf16[2,2,96,768]{3,2,1,0:T(8,128)(2,1)}) conditional(s32[]{:T(128)} %bitcast.14, () %tuple.180, (s32[6]{0:T(128)S(1)}, s32[4]{0:T(128)S(1)}, s32[1,768]{1,0:T(1,128)S(1)}, s32[1,768]{1,0:T(1,128)S(1)}, bf16[2,2,96,768]{3,2,1,0:T(8,128)(2,1)S(1)}, ...), branch_computations={%region_18.19_spmd, %region_19.20_spmd} | conditional | flops 2359297 | bytes 8257641 | solution.py:634
  304.3 15.9 %attention_backward.2 = (f32[2,2,96,768]{3,2,1,0:T(8,128)}, bf16[2,2,96,768]{3,2,1,0:T(8,128)(2,1)S(1)}, bf16[2,2,96,768]{3,2,1,0:T(8,128)(2,1)S(1)}, bf16[2,2,9...) custom-call(s32[6]{0:T(128)S(1)} %get-tuple-element.226.starts_ref, s32[4]{0:T(128)S(1)} %get-tuple-element.227.stripes_ref, ...), custom_call_target="tpu_custom_call" | custom-call | flops 1 | bytes 1 | tf_op jit(solution)/shard_map/cond/branch_1_fun/attention_backward/pallas_call | solution.py:218
  325.6 6.8 %gradient_chip.9 = bf16[4,96,2048]{2,1,0:T(8,128)(2,1)S(1)} custom-call(s32[2]{0:T(128)S(1)} %pad_add_fusion.6.place_ref, bf16[4,2,96,768]{3,2,1,0:T(8,128)(2,1)} %get-tuple-element.720.refs_0_, bf16[768,2048]{1,0:T(8,128)(2,1)} %get-tuple-element.721.refs_1_, bf16[4,2,96,768]{3,2,1,0:T(8,128)(2,1)} %get-tuple-element.722.refs_2_, ...), custom_call_target="tpu_custom_call" | custom-call | flops 1 | bytes 1 | tf_op jit(solution)/shard_map/gradient_chip/pallas_call | solution.py:771
  342.8 20.7 %conditional.20 = (f32[2,2,96,768]{3,2,1,0:T(8,128)}, bf16[2,2,96,768]{3,2,1,0:T(8,128)(2,1)S(1)}, bf16[2,2,96,768]{3,2,1,0:T(8,128)(2,1)}) conditional(s32[]{:T(128)} %bitcast.14, () %tuple.205, (s32[6]{0:T(128)}, s32[4]{0:T(128)}, s32[1,768]{1,0:T(1,128)}, s32[1,768]{1,0:T(1,128)S(1)}, bf16[2,2,96,768]{3,2,1,0:T(8,128)(2,1)}, ...), branch_computations={%region_20.21_spmd, %region_21.22_spmd} | conditional | flops 2359297 | bytes 8257641 | solution.py:634
  342.8 16.9 %attention_backward.3 = (f32[2,2,96,768]{3,2,1,0:T(8,128)}, bf16[2,2,96,768]{3,2,1,0:T(8,128)(2,1)S(1)}, bf16[2,2,96,768]{3,2,1,0:T(8,128)(2,1)S(1)}, bf16[2,2,9...) custom-call(s32[6]{0:T(128)} %get-tuple-element.243.starts_ref, s32[4]{0:T(128)} %get-tuple-element.244.stripes_ref, ...), custom_call_target="tpu_custom_call" | custom-call | flops 1 | bytes 1 | tf_op jit(solution)/shard_map/cond/branch_1_fun/attention_backward/pallas_call | solution.py:218
  365.4 11.6 %conditional.21 = (bf16[4,96,768]{2,1,0:T(8,128)(2,1)S(1)}, bf16[4,2,96,768]{3,2,1,0:T(8,128)(2,1)}, bf16[4,2,96,768]{3,2,1,0:T(8,128)(2,1)}) conditional(s32[]{:T(128)} %bitcast.14, () %tuple.211, (bf16[768,1536]{1,0:T(8,128)(2,1)}, s32[]{:T(128)}, bf16[768,768]{1,0:T(8,128)(2,1)}, bf16[768,768]{1,0:T(8,128)(2,1)}) %tuple.213), branch_computations={%region_22.23_spmd, %region_23.24_spmd} | conditional | flops 37 | bytes 4719009 | solution.py:634
  378.5 6.5 %gradient_chip.11 = bf16[4,96,2048]{2,1,0:T(8,128)(2,1)S(1)} custom-call(s32[2]{0:T(128)S(1)} %pad_add_fusion.6.place_ref, bf16[4,2,96,768]{3,2,1,0:T(8,128)(2,1)} %get-tuple-element.757.refs_0_, bf16[768,2048]{1,0:T(8,128)(2,1)} %get-tuple-element.758.refs_1_, bf16[4,2,96,768]{3,2,1,0:T(8,128)(2,1)} %get-tuple-element.759.refs_2_, ...), custom_call_target="tpu_custom_call" | custom-call | flops 1 | bytes 1 | tf_op jit(solution)/shard_map/gradient_chip/pallas_call | solution.py:771
  391.1 10.9 %collective-permute-done.42 = bf16[2,2,96,768]{3,2,1,0:T(8,128)(2,1)} collective-permute-done((bf16[2,2,96,768]{3,2,1,0:T(8,128)(2,1)}, bf16[2,2,96,768]{3,2,1,0:T(8,128)(2,1)}, u32[]{:S(2)}, u32[]{:S(2)}) %collective-permute-start.42) | collective-permute-done | bytes 589856 | tf_op jit(solution)/shard_map/ppermute | solution.py:650
  402.1 12.9 %conditional.22 = (bf16[768,1536]{1,0:T(8,128)(2,1)}, bf16[768,768]{1,0:T(8,128)(2,1)}, bf16[768,768]{1,0:T(8,128)(2,1)}, bf16[768,768]{1,0:T(8,128)(2,1)}, bf16[768,768]{1,0:T(8,128)(2,1)}) conditional(s32[]{:T(128)} %bitcast.14, () %tuple.179, (f32[2,2,96,768]{3,2,1,0:T(8,128)}, bf16[2,2,96,768]{3,2,1,0:T(8,128)(2,1)S(1)}, ...), branch_computations={%region_24.25_spmd, %region_25.26_spmd} | conditional | flops 3 | bytes 35389648 | solution.py:634
  407.4 7.5 %d_one.1 = bf16[768,1536]{1,0:T(8,128)(2,1)} custom-call(bf16[768,768]{1,0:T(8,128)(2,1)} %turn_back.2.refs_0_, bf16[768,768]{1,0:T(8,128)(2,1)} %turn_back.3.refs_1_, bf16[1536,1536]{1,0:T(8,128)(2,1)S(1)} %copy-done.8), custom_call_target="tpu_custom_call" | custom-call | flops 1 | bytes 1 | tf_op jit(solution)/shard_map/cond/branch_1_fun/d_one/pallas_call | solution.py:514
  417.4 51.5 %conditional.23 = (f32[96,768]{1,0:T(8,128)}, f32[96,768]{1,0:T(8,128)S(1)}, f32[96,768]{1,0:T(8,128)}, bf16[96,768]{1,0:T(8,128)(2,1)}, bf16[96,768]{1,0:T(8,12...) conditional(s32[]{:T(128)} %bitcast.14, () %tuple.165, (bf16[4,96,768]{2,1,0:T(8,128)(2,1)}, ...), branch_computations={%region_27.28_spmd, %region_28.29_spmd} | conditional | flops 6783018 | bytes 43352928 | solution.py:634
  423.8 10.1 %collective-permute-done.18.refs_4_ = bf16[4,96,768]{2,1,0:T(8,128)(2,1)S(1)} collective-permute-done((bf16[4,96,768]{2,1,0:T(8,128)(2,1)}, bf16[4,96,768]{2,1,0:T(8,128)(2,1)S(1)}, u32[]{:S(2)}, u32[]{:S(2)}) %collective-permute-start.18) | collective-permute-done | bytes 589856 | tf_op jit(solution)/shard_map/cond/branch_1_fun/ppermute | solution.py:650
  (286 shorter events, 224.4 us)
Async XLA Ops:
  7.2 186.7 %all-gather.2.cloned.1.call-start = ((), (), s32[]{:S(2)}) async-start(), calls=%async_computation.2 | async-start | bytes 25067520 | tf_op jit(solution)/shard_map/all_gather | solution.py:878
  9.0 13.2 %collective-permute-start.27 = (bf16[112,1536]{1,0:T(8,128)(2,1)S(1)}, bf16[112,1536]{1,0:T(8,128)(2,1)S(1)}, u32[]{:S(2)}, u32[]{:S(2)}) collective-permute-start(bf16[112,1536]{1,0:T(8,128)(2,1)S(1)} %fusion.5), channel_id=1, source_target_pairs={{0,8},{8,16},{16,24},{24,0},{1,9},{9,17},{17,25},{25,1},{2,10},{10... | collective-permute-start | bytes 1032200 | tf_op jit(solution)/shard_map/ppermute | solution.py:655
  22.2 395.3 %reduce-scatter.3.cloned.1.call-start = ((), (), s32[]{:S(2)}) async-start(), calls=%async_computation.3 | async-start | bytes 3932160 | tf_op jit(solution)/shard_map/reduce_scatter | solution.py:809
  22.2 34.2 %collective-permute-start.29 = (bf16[112,1536]{1,0:T(8,128)(2,1)S(1)}, bf16[112,1536]{1,0:T(8,128)(2,1)}, u32[]{:S(2)}, u32[]{:S(2)}) collective-permute-start(bf16[112,1536]{1,0:T(8,128)(2,1)S(1)} %fusion.5), channel_id=1, source_target_pairs={{0,24},{8,0},{16,8},{24,16},{1,25},{9,1},{17,9},{25,17},{2,26},{10... | collective-permute-start | bytes 1032200 | tf_op jit(solution)/shard_map/ppermute | solution.py:655
  24.0 31.4 %collective-permute-start.28 = (bf16[112,1536]{1,0:T(8,128)(2,1)S(1)}, bf16[112,1536]{1,0:T(8,128)(2,1)}, u32[]{:S(2)}, u32[]{:S(2)}) collective-permute-start(bf16[112,1536]{1,0:T(8,128)(2,1)S(1)} %fusion.5), channel_id=1, source_target_pairs={{0,16},{8,24},{16,0},{24,8},{1,17},{9,25},{17,1},{25,9},{2,18},{10... | collective-permute-start | bytes 1032200 | tf_op jit(solution)/shard_map/ppermute | solution.py:655
  57.6 41.4 %collective-permute-start.31 = (bf16[3,96,1536]{2,1,0:T(8,128)(2,1)S(1)}, bf16[3,96,1536]{2,1,0:T(8,128)(2,1)S(1)}, u32[]{:S(2)}, u32[]{:S(2)}) collective-permute-start(bf16[3,96,1536]{2,1,0:T(8,128)(2,1)S(1)} %pad_maximum_fusion.1), channel_id=1, source_target_pairs={{0,2},{2,0},{4,6},{6,4},{1,3},{3,1},{5,7},{7,5},{8,10},{10,8},{12,... | collective-permute-start | bytes 2654216 | tf_op jit(solution)/shard_map/ppermute | solution.py:645
  57.7 41.3 %collective-permute-start.32 = (bf16[3,96,1536]{2,1,0:T(8,128)(2,1)S(1)}, bf16[3,96,1536]{2,1,0:T(8,128)(2,1)S(1)}, u32[]{:S(2)}, u32[]{:S(2)}) collective-permute-start(bf16[3,96,1536]{2,1,0:T(8,128)(2,1)S(1)} %pad_maximum_fusion.1), channel_id=1, source_target_pairs={{0,4},{2,6},{4,0},{6,2},{1,5},{3,7},{5,1},{7,3},{8,12},{10,14},{12... | collective-permute-start | bytes 2654216 | tf_op jit(solution)/shard_map/ppermute | solution.py:650
  105.7 29.1 %collective-permute-start.34 = (bf16[2,2,96,768]{3,2,1,0:T(8,128)(2,1)}, bf16[2,2,96,768]{3,2,1,0:T(8,128)(2,1)}, u32[]{:S(2)}, u32[]{:S(2)}) collective-permute-start(bf16[2,2,96,768]{3,2,1,0:T(8,128)(2,1)} %get-tuple-element.708), channel_id=1, source_target_pairs={{0,4},{2,6},{4,0},{6,2},{1,5},{3,7},{5,1},{7,3},{8,12},{10,14},{12... | collective-permute-start | bytes 1769480 | tf_op jit(solution)/shard_map/ppermute | solution.py:650
  111.2 48.5 %collective-permute-start.35 = (bf16[2,2,96,768]{3,2,1,0:T(8,128)(2,1)}, bf16[2,2,96,768]{3,2,1,0:T(8,128)(2,1)S(1)}, u32[]{:S(2)}, u32[]{:S(2)}) collective-permute-start(bf16[2,2,96,768]{3,2,1,0:T(8,128)(2,1)} %get-tuple-element.738), channel_id=1, source_target_pairs={{0,4},{2,6},{4,0},{6,2},{1,5},{3,7},{5,1},{7,3},{8,12},{10,14},{12... | collective-permute-start | bytes 1769480 | tf_op jit(solution)/shard_map/ppermute | solution.py:650
  159.7 19.0 %collective-permute-start.36 = (bf16[384,768]{1,0:T(8,128)(2,1)}, bf16[384,768]{1,0:T(8,128)(2,1)S(1)}, u32[]{:S(2)}, u32[]{:S(2)}) collective-permute-start(bf16[384,768]{1,0:T(8,128)(2,1)} %get-tuple-element.656.refs_0_), channel_id=1, source_target_pairs={{0,1},{1,0},{2,3},{3,2},{4,5},{5,4},{6,7},{7,6},{8,9},{9,8},{10,11... | collective-permute-start | bytes 1769480 | tf_op jit(solution)/shard_map/ppermute | solution.py:659
  178.3 15.6 %collective-permute-start.37 = (bf16[384,768]{1,0:T(8,128)(2,1)}, bf16[384,768]{1,0:T(8,128)(2,1)S(1)}, u32[]{:S(2)}, u32[]{:S(2)}) collective-permute-start(bf16[384,768]{1,0:T(8,128)(2,1)} %copy-done.11), channel_id=1, source_target_pairs={{0,1},{1,0},{2,3},{3,2},{4,5},{5,4},{6,7},{7,6},{8,9},{9,8},{10,11... | collective-permute-start | bytes 1769480 | tf_op jit(solution)/shard_map/ppermute | solution.py:659
  237.4 52.8 %collective-permute-start.39 = (bf16[768,1536]{1,0:T(8,128)(2,1)}, bf16[768,1536]{1,0:T(8,128)(2,1)}, u32[]{:S(2)}, u32[]{:S(2)}) collective-permute-start(bf16[768,1536]{1,0:T(8,128)(2,1)} %get-tuple-element.690.mine_ref), channel_id=1, source_target_pairs={{0,1},{1,0},{2,3},{3,2},{4,5},{5,4},{6,7},{7,6},{8,9},{9,8},{10,11... | collective-permute-start | bytes 7077896 | tf_op jit(solution)/shard_map/ppermute | solution.py:659
  250.9 36.8 %collective-permute-start.38 = (bf16[4,96,2048]{2,1,0:T(8,128)(2,1)}, bf16[4,96,2048]{2,1,0:T(8,128)(2,1)}, u32[]{:S(2)}, u32[]{:S(2)}) collective-permute-start(bf16[4,96,2048]{2,1,0:T(8,128)(2,1)} %get-tuple-element.672), channel_id=1, source_target_pairs={{0,4},{2,6},{4,0},{6,2},{1,5},{3,7},{5,1},{7,3},{8,12},{10,14},{12... | collective-permute-start | bytes 4718600 | tf_op jit(solution)/shard_map/ppermute | solution.py:650
  290.3 35.3 %collective-permute-start.40 = (bf16[4,96,2048]{2,1,0:T(8,128)(2,1)}, bf16[4,96,2048]{2,1,0:T(8,128)(2,1)}, u32[]{:S(2)}, u32[]{:S(2)}) collective-permute-start(bf16[4,96,2048]{2,1,0:T(8,128)(2,1)} %get-tuple-element.716), channel_id=1, source_target_pairs={{0,4},{2,6},{4,0},{6,2},{1,5},{3,7},{5,1},{7,3},{8,12},{10,14},{12... | collective-permute-start | bytes 4718600 | tf_op jit(solution)/shard_map/ppermute | solution.py:650
  340.6 129.0 %reduce-scatter.5.cloned.1.call-start = ((), (), s32[]{:S(2)}) async-start(), calls=%async_computation.4 | async-start | bytes 1966080 | tf_op jit(solution)/shard_map/reduce_scatter | solution.py:809
  340.7 61.3 %collective-permute-start.43 = (bf16[768,1536]{1,0:T(8,128)(2,1)}, bf16[768,1536]{1,0:T(8,128)(2,1)}, u32[]{:S(2)}, u32[]{:S(2)}) collective-permute-start(bf16[768,1536]{1,0:T(8,128)(2,1)} %get-tuple-element.797), channel_id=1, source_target_pairs={{0,1},{1,0},{2,3},{3,2},{4,5},{5,4},{6,7},{7,6},{8,9},{9,8},{10,11... | collective-permute-start | bytes 7077896 | tf_op jit(solution)/shard_map/ppermute | solution.py:659
  340.8 37.7 %collective-permute-start.44 = (bf16[4,96,2048]{2,1,0:T(8,128)(2,1)}, bf16[4,96,2048]{2,1,0:T(8,128)(2,1)}, u32[]{:S(2)}, u32[]{:S(2)}) collective-permute-start(bf16[4,96,2048]{2,1,0:T(8,128)(2,1)} %get-tuple-element.749), channel_id=1, source_target_pairs={{0,4},{2,6},{4,0},{6,2},{1,5},{3,7},{5,1},{7,3},{8,12},{10,14},{12... | collective-permute-start | bytes 4718600 | tf_op jit(solution)/shard_map/ppermute | solution.py:650
  342.6 48.5 %collective-permute-start.41 = (bf16[2,2,96,768]{3,2,1,0:T(8,128)(2,1)}, bf16[2,2,96,768]{3,2,1,0:T(8,128)(2,1)}, u32[]{:S(2)}, u32[]{:S(2)}) collective-permute-start(bf16[2,2,96,768]{3,2,1,0:T(8,128)(2,1)} %get-tuple-element.744), channel_id=1, source_target_pairs={{0,4},{2,6},{4,0},{6,2},{1,5},{3,7},{5,1},{7,3},{8,12},{10,14},{12... | collective-permute-start | bytes 1769480 | tf_op jit(solution)/shard_map/ppermute | solution.py:650
  363.6 38.4 %collective-permute-start.42 = (bf16[2,2,96,768]{3,2,1,0:T(8,128)(2,1)}, bf16[2,2,96,768]{3,2,1,0:T(8,128)(2,1)}, u32[]{:S(2)}, u32[]{:S(2)}) collective-permute-start(bf16[2,2,96,768]{3,2,1,0:T(8,128)(2,1)} %get-tuple-element.746), channel_id=1, source_target_pairs={{0,4},{2,6},{4,0},{6,2},{1,5},{3,7},{5,1},{7,3},{8,12},{10,14},{12... | collective-permute-start | bytes 1769480 | tf_op jit(solution)/shard_map/ppermute | solution.py:650
  414.9 58.9 %collective-permute-start.45 = (bf16[768,1536]{1,0:T(8,128)(2,1)}, bf16[768,1536]{1,0:T(8,128)(2,1)}, u32[]{:S(2)}, u32[]{:S(2)}) collective-permute-start(bf16[768,1536]{1,0:T(8,128)(2,1)} %get-tuple-element.804.mine_ref), channel_id=1, source_target_pairs={{0,1},{1,0},{2,3},{3,2},{4,5},{5,4},{6,7},{7,6},{8,9},{9,8},{10,11... | collective-permute-start | bytes 7077896 | tf_op jit(solution)/shard_map/ppermute | solution.py:659
  417.4 16.4 %collective-permute-start.18 = (bf16[4,96,768]{2,1,0:T(8,128)(2,1)}, bf16[4,96,768]{2,1,0:T(8,128)(2,1)S(1)}, u32[]{:S(2)}, u32[]{:S(2)}) collective-permute-start(bf16[4,96,768]{2,1,0:T(8,128)(2,1)} %get-tuple-element.298), channel_id=1, source_target_pairs={{0,4},{2,6},{4,0},{6,2},{1,5},{3,7},{5,1},{7,3},{8,12},{10,14},{12... | collective-permute-start | bytes 1769480 | tf_op jit(solution)/shard_map/cond/branch_1_fun/ppermute | solution.py:650
  422.1 29.8 %collective-permute-start.22 = (bf16[4,96,768]{2,1,0:T(8,128)(2,1)S(1)}, bf16[4,96,768]{2,1,0:T(8,128)(2,1)S(1)}, u32[]{:S(2)}, u32[]{:S(2)}) collective-permute-start(bf16[4,96,768]{2,1,0:T(8,128)(2,1)S(1)} %gradient_send.10), channel_id=1, source_target_pairs={{0,4},{2,6},{4,0},{6,2},{1,5},{3,7},{5,1},{7,3},{8,12},{10,14},{12... | collective-permute-start | bytes 1769480 | tf_op jit(solution)/shard_map/cond/branch_1_fun/ppermute | solution.py:650
  438.0 12.6 %collective-permute-start.19 = (bf16[96,768]{1,0:T(8,128)(2,1)S(1)}, bf16[96,768]{1,0:T(8,128)(2,1)S(1)}, u32[]{:S(2)}, u32[]{:S(2)}) collective-permute-start(bf16[96,768]{1,0:T(8,128)(2,1)S(1)} %get-tuple-element.313), channel_id=1, source_target_pairs={{0,8},{8,16},{16,24},{24,0},{1,9},{9,17},{17,25},{25,1},{2,10},{10... | collective-permute-start | bytes 442376 | tf_op jit(solution)/shard_map/cond/branch_1_fun/ppermute | solution.py:655
  438.1 12.5 %collective-permute-start.20 = (bf16[96,768]{1,0:T(8,128)(2,1)S(1)}, bf16[96,768]{1,0:T(8,128)(2,1)S(1)}, u32[]{:S(2)}, u32[]{:S(2)}) collective-permute-start(bf16[96,768]{1,0:T(8,128)(2,1)S(1)} %get-tuple-element.314), channel_id=1, source_target_pairs={{0,16},{8,24},{16,0},{24,8},{1,17},{9,25},{17,1},{25,9},{2,18},{10... | collective-permute-start | bytes 442376 | tf_op jit(solution)/shard_map/cond/branch_1_fun/ppermute | solution.py:655
  438.2 12.5 %collective-permute-start.21 = (bf16[96,768]{1,0:T(8,128)(2,1)S(1)}, bf16[96,768]{1,0:T(8,128)(2,1)S(1)}, u32[]{:S(2)}, u32[]{:S(2)}) collective-permute-start(bf16[96,768]{1,0:T(8,128)(2,1)S(1)} %get-tuple-element.315), channel_id=1, source_target_pairs={{0,24},{8,0},{16,8},{24,16},{1,25},{9,1},{17,9},{25,17},{2,26},{10... | collective-permute-start | bytes 442376 | tf_op jit(solution)/shard_map/cond/branch_1_fun/ppermute | solution.py:655
  451.4 12.8 %collective-permute-start.26 = (bf16[4,96,768]{2,1,0:T(8,128)(2,1)S(1)}, bf16[4,96,768]{2,1,0:T(8,128)(2,1)S(1)}, u32[]{:S(2)}, u32[]{:S(2)}) collective-permute-start(bf16[4,96,768]{2,1,0:T(8,128)(2,1)S(1)} %gradient_send.11), channel_id=1, source_target_pairs={{0,4},{2,6},{4,0},{6,2},{1,5},{3,7},{5,1},{7,3},{8,12},{10,14},{12... | collective-permute-start | bytes 1769480 | tf_op jit(solution)/shard_map/cond/branch_1_fun/ppermute | solution.py:650
  455.8 13.0 %collective-permute-start.23 = (bf16[96,768]{1,0:T(8,128)(2,1)S(1)}, bf16[96,768]{1,0:T(8,128)(2,1)S(1)}, u32[]{:S(2)}, u32[]{:S(2)}) collective-permute-start(bf16[96,768]{1,0:T(8,128)(2,1)S(1)} %get-tuple-element.338), channel_id=1, source_target_pairs={{0,8},{8,16},{16,24},{24,0},{1,9},{9,17},{17,25},{25,1},{2,10},{10... | collective-permute-start | bytes 442376 | tf_op jit(solution)/shard_map/cond/branch_1_fun/ppermute | solution.py:655
  458.2 10.6 %collective-permute-start.24 = (bf16[96,768]{1,0:T(8,128)(2,1)S(1)}, bf16[96,768]{1,0:T(8,128)(2,1)S(1)}, u32[]{:S(2)}, u32[]{:S(2)}) collective-permute-start(bf16[96,768]{1,0:T(8,128)(2,1)S(1)} %get-tuple-element.339), channel_id=1, source_target_pairs={{0,16},{8,24},{16,0},{24,8},{1,17},{9,25},{17,1},{25,9},{2,18},{10... | collective-permute-start | bytes 442376 | tf_op jit(solution)/shard_map/cond/branch_1_fun/ppermute | solution.py:655
  458.2 10.6 %collective-permute-start.25 = (bf16[96,768]{1,0:T(8,128)(2,1)S(1)}, bf16[96,768]{1,0:T(8,128)(2,1)S(1)}, u32[]{:S(2)}, u32[]{:S(2)}) collective-permute-start(bf16[96,768]{1,0:T(8,128)(2,1)S(1)} %get-tuple-element.340), channel_id=1, source_target_pairs={{0,24},{8,0},{16,8},{24,16},{1,25},{9,1},{17,9},{25,17},{2,26},{10... | collective-permute-start | bytes 442376 | tf_op jit(solution)/shard_map/cond/branch_1_fun/ppermute | solution.py:655
  473.9 15.7 %collective-permute-start.46 = (bf16[96,768]{1,0:T(8,128)(2,1)S(1)}, bf16[96,768]{1,0:T(8,128)(2,1)S(1)}, u32[]{:S(2)}, u32[]{:S(2)}) collective-permute-start(bf16[96,768]{1,0:T(8,128)(2,1)S(1)} %copy-done.33), channel_id=1, source_target_pairs={{0,8},{8,16},{16,24},{24,0},{1,9},{9,17},{17,25},{25,1},{2,10},{10... | collective-permute-start | bytes 442376 | tf_op jit(solution)/shard_map/ppermute | solution.py:655
  477.9 11.7 %collective-permute-start.47 = (bf16[96,768]{1,0:T(8,128)(2,1)S(1)}, bf16[96,768]{1,0:T(8,128)(2,1)S(1)}, u32[]{:S(2)}, u32[]{:S(2)}) collective-permute-start(bf16[96,768]{1,0:T(8,128)(2,1)S(1)} %copy-done.34), channel_id=1, source_target_pairs={{0,16},{8,24},{16,0},{24,8},{1,17},{9,25},{17,1},{25,9},{2,18},{10... | collective-permute-start | bytes 442376 | tf_op jit(solution)/shard_map/ppermute | solution.py:655
  478.7 11.0 %collective-permute-start.48 = (bf16[96,768]{1,0:T(8,128)(2,1)S(1)}, bf16[96,768]{1,0:T(8,128)(2,1)S(1)}, u32[]{:S(2)}, u32[]{:S(2)}) collective-permute-start(bf16[96,768]{1,0:T(8,128)(2,1)S(1)} %copy-done.35), channel_id=1, source_target_pairs={{0,24},{8,0},{16,8},{24,16},{1,25},{9,1},{17,9},{25,17},{2,26},{10... | collective-permute-start | bytes 442376 | tf_op jit(solution)/shard_map/ppermute | solution.py:655
  (68 other events, 582.1 us)
Sparse Core Ops, SparseCore 0:
  22.3 164.5 all-gather.1
  340.7 57.7 reduce-scatter.2
  402.2 34.5 reduce-scatter.4

commit v4 on v3

--- a/solution.py
+++ b/solution.py
@@ -12,7 +12,6 @@
 QUERY_PER_KV = 2
 HALF = HEAD_SIZE // 2
 BLOCK = 128
-CHUNKS = 2
 
 norm_eps = 1e-05
 rope_base = 100000.0
@@ -283,7 +282,7 @@
     unit = x * scale
     weighted = (mine_ref[...].astype(f32) + other_ref[...].astype(f32)) * gain_ref[...]
     out_ref[...] = (
-        d_mid_ref[...]
+        d_mid_ref[...].astype(f32)
         + scale * (weighted - unit * jnp.mean(weighted * unit, axis=-1, keepdims=True))
     ).astype(bf16)
 
@@ -422,7 +421,7 @@
 
 
 def d_middle_kernel(
-    mine_ref, other_ref, middle_ref, dy_ref, gain_ref, w_ref, d_mid_ref, branch_ref, d_att_ref
+    mine_ref, other_ref, middle_ref, dy_ref, gain_ref, w_ref, branch_ref, *d_att_refs
 ):
     middle = middle_ref[...]
     scale = lax.rsqrt(jnp.mean(middle * middle, axis=-1, keepdims=True) + norm_eps)
@@ -431,33 +430,35 @@
     d_mid = dy_ref[...].astype(f32) + scale * (
         weighted - unit * jnp.mean(weighted * unit, axis=-1, keepdims=True)
     )
-    d_mid_ref[...] = d_mid
     branch = d_mid.astype(bf16)
     branch_ref[...] = branch
-    d_att_ref[...] = mm(branch, w_ref[...]).astype(bf16).T
-
-
-def d_middle_of(sent, middle, d_out, gain, weight, first, features):
+    d_att = mm(branch, w_ref[...]).astype(bf16).T
+    first = 0
+    for ref in d_att_refs:
+        ref[...] = d_att[first : first + ref.shape[0]]
+        first += ref.shape[0]
+
+
+def d_middle_of(sent, middle, d_out, gain, weight, first, parts):
     mine, other = sent
     tokens, width = middle.shape
+    features = sum(parts)
     block = 256
     here = pl.BlockSpec((block, width), lambda n: (n, 0))
     row = pl.BlockSpec((1, width), lambda n: (0, 0))
-    return pl.pallas_call(
+    branch, *d_att = pl.pallas_call(
         d_middle_kernel,
         grid=(tokens // block,),
         in_specs=[here, here, here, here, row]
         + [pl.BlockSpec((width, features), lambda n: (0, first // features))],
-        out_specs=[here, here, pl.BlockSpec((features, block), lambda n: (0, n))],
-        out_shape=[
-            jax.ShapeDtypeStruct((tokens, width), f32),
-            jax.ShapeDtypeStruct((tokens, width), bf16),
-            jax.ShapeDtypeStruct((features, tokens), bf16),
-        ],
+        out_specs=[here] + [pl.BlockSpec((p, block), lambda n: (0, n)) for p in parts],
+        out_shape=[jax.ShapeDtypeStruct((tokens, width), bf16)]
+        + [jax.ShapeDtypeStruct((p, tokens), bf16) for p in parts],
         compiler_params=pltpu.CompilerParams(vmem_limit_bytes=48 << 20),
         cost_estimate=SMALL_COST,
         name="d_middle",
     )(mine, other, middle, d_out, gain, weight)
+    return branch, d_att
 
 
 def turn_back_kernel(cos_ref, sin_ref, dq_ref, *refs):
@@ -709,7 +710,7 @@
     return whole, all_gains, fetched
 
 
-def gradient_kernel(pairs, turned, pieces, place_ref, *refs):
+def gradient_kernel(pairs, count, turned, pieces, place_ref, *refs):
     total = None
     for i in range(pairs):
         left, right = refs[2 * i], refs[2 * i + 1]
@@ -720,7 +721,7 @@
         total = term if total is None else total + term
     total = total.reshape(groups, rows, total.shape[-1])
     refs = refs[2 * pairs :]
-    arrived = refs[: -1 if not pieces else -1 - groups]
+    arrived = refs[:count]
     for piece in arrived:
         total = total + piece[...].astype(f32)
     if not pieces:
@@ -733,7 +734,7 @@
         out[...] = sum_ref[lax.rem(group + by, groups)].astype(out.dtype)
 
 
-def gradient_call(left, right, which, turned, arrived, pieces):
+def gradient_call(left, right, which, turned, arrived, pieces, inside=None):
     groups, chips, rows, tokens = left[0].shape
     group = lax.axis_index("fsdp")
     columns = right[0].shape[0 if turned else 1]
@@ -766,18 +767,23 @@
         ]
         scratch = [pltpu.VMEM((groups, rows, block), f32)]
     else:
-        out_specs, scratch = sum_spec, []
-        out_shape = jax.ShapeDtypeStruct((groups, rows, columns), bf16)
+        first, total, whole = inside or (0, columns, ())
+        out_specs, scratch = pl.BlockSpec((groups, rows, block), lambda n, _: (0, 0, first // block + n)), []
+        out_shape = jax.ShapeDtypeStruct((groups, rows, total), bf16)
+        operands += whole
     return pl.pallas_call(
-        functools.partial(gradient_kernel, len(left), turned, pieces),
+        functools.partial(gradient_kernel, len(left), len(arrived), turned, pieces),
         grid_spec=pltpu.PrefetchScalarGridSpec(
             num_scalar_prefetch=1,
             grid=(columns // block,),
-            in_specs=[left_spec, right_spec] * len(left) + [sum_spec] * len(arrived),
+            in_specs=[left_spec, right_spec] * len(left)
+            + [sum_spec] * len(arrived)
+            + [pl.BlockSpec(memory_space=pl.ANY)] * (len(operands) - 2 * len(left) - len(arrived)),
             out_specs=out_specs,
             scratch_shapes=scratch,
         ),
         out_shape=out_shape,
+        input_output_aliases={len(operands): 0} if inside and inside[2] else {},
         compiler_params=pltpu.CompilerParams(vmem_limit_bytes=40 << 20),
         cost_estimate=SMALL_COST,
         name="gradient_chip" if arrived else "gradient_send",
@@ -907,11 +913,15 @@
     first_normed, tables, *meta = lax.optimization_barrier(
         (first_normed, (cos_table, sin_table), *meta)
     )
-    chunk = kv_heads // CHUNKS
+    sizes = (kv_heads // 2, kv_heads - kv_heads // 2)
+    chunks = range(len(sizes))
     queries, own, moving, pieces, attended, lse = [], [], [], [], [], []
-    for c in range(CHUNKS):
+    for c in chunks:
         query, kv_own = order(
-            functools.partial(project, first=c * chunk, heads=chunk), first_normed, wq, *tables
+            functools.partial(project, first=sum(sizes[:c]), heads=sizes[c]),
+            first_normed,
+            wq,
+            *tables,
         )
         queries.append(query)
         own.append(kv_own)
@@ -927,7 +937,7 @@
         return attention_forward(query, pieces, *meta), pieces[3::2]
 
     attended_others = []
-    for c in range(CHUNKS):
+    for c in chunks:
         (att, lse_c), swapped = order.apart(
             attend, queries[c], own[c], own_swapped[c], moving[c], *meta
         )
@@ -979,6 +989,8 @@
         gate_products = inner(gradient_products, left_two, (d_gate, other_gate))
         other_up = core_swap(lax.optimization_barrier((d_up, down_sum))[0])
         up_products = inner(gradient_products, left_two, (d_up, other_up))
+        early = units // 4
+        up_products = [[p[:, :, :early] for p in up_products], [p[:, :, early:] for p in up_products]]
         return gate_products, up_products, down_sum, other_gate, other_up
 
     gate_products, up_products, down_sum, other_gate, other_up = order.apart(
@@ -990,20 +1002,23 @@
         feedforward_weight,
         query_key_value_weight,
     )
-    down_arrived, gate_products, down_sum, d_two_sent = order(
-        touch, down_arrived, gate_products, down_sum, d_two_sent
-    )
-    gate_arrived = gradient_send(gate_products)
+    down_arrived, gate_products, up_products, down_sum, d_two_sent = order(
+        touch, down_arrived, gate_products, up_products, down_sum, d_two_sent
+    )
+    gate_arrived, up_first = gradient_send(gate_products), gradient_send(up_products[0])
+    down_scattered = gradient_scatter(order(gradient_chip, left_dy, right_act, down_arrived))
     down_sent = tp_send(down_sum)
-    d_mid, d_branch, d_att = order(
-        functools.partial(d_middle_of, first=3 * units, features=att_columns),
+    d_branch, d_att = order(
+        functools.partial(
+            d_middle_of, first=3 * units, parts=[s * QUERY_PER_KV * HEAD_SIZE for s in sizes]
+        ),
         d_two_sent,
         middle,
         grad_low,
         gain_rows[1:],
         others,
     )
-    d_att = d_att.reshape(CHUNKS, chunk, QUERY_PER_KV, HEAD_SIZE, tokens)
+    d_att = [d.reshape(-1, QUERY_PER_KV, HEAD_SIZE, tokens) for d in d_att]
 
     def attend_back(query, d_att, attended, lse, pieces, *meta):
         d_query, *d_pieces = attention_backward(query, d_att, attended, lse, pieces, *meta)
@@ -1021,10 +1036,10 @@
 
     d_query_0, d_kv_0 = attention_step(0)
     gate_arrived, up_products = order(touch, gate_arrived, up_products)
-    up_arrived = gradient_send(up_products)
-    down_chip = order(gradient_chip, left_dy, right_act, down_arrived)
+    up_second = gradient_send(up_products[1])
     gate_chip = order(gradient_chip, left_two, right_gate, gate_arrived)
-    two_scattered = gradient_scatter(jnp.concatenate([down_chip, gate_chip], axis=2))
+    gate_chip, up_first = order(touch, gate_chip, up_first)
+    gate_scattered = gradient_scatter(gate_chip)
     d_query_1, d_kv_1 = attention_step(1)
 
     def branch_part(d_branch, core, right_att):
@@ -1034,6 +1049,8 @@
         return inner(turned_products, left, right_att), left
 
     out_products, left_branch = order.apart(branch_part, d_branch, core, right_att)
+    up_first, up_second = order(touch, up_first, up_second)
+    up_arrived = [jnp.concatenate(pair, axis=2) for pair in zip(up_first, up_second)]
     up_chip = order(gradient_chip, left_two, right_up, up_arrived)
     d_kv_0, d_kv_1, down_sent, up_chip = order(touch, d_kv_0, d_kv_1, down_sent, up_chip)
     up_scattered = gradient_scatter(up_chip)
@@ -1050,7 +1067,8 @@
     d_one_sent = tp_send(d_one_part)
     right_proj = list(zip(d_proj, other_proj))
 
-    two_scattered = order(touch, two_scattered)[0]
+    grad_down = order(lambda v: v.astype(f32), down_scattered)
+    gate_scattered = order(touch, gate_scattered)[0]
 
     def tail(left_one, right_proj, left_branch, right_att, out_products, middle, down_sent):
         inner = Order()
@@ -1074,13 +1092,12 @@
         gains, ctx_index * out_share.shape[0], out_share.shape[0], 1
     ).astype(f32)
 
-    def ffn_gradient(two, up):
-        down, gate = two[:, :units], two[:, units:]
+    def ffn_gradient(down, gate, up):
         gain = gain_gradient(shares[:2], [gate, up], own_gains[1])
-        return jnp.stack([gate, up, down], axis=0).astype(f32), gain
-
-    grad_ffn, gain_two = order(ffn_gradient, two_scattered, up_scattered)
-    grad_in = order(input_gradient, d_one_sent, x, d_mid, gain_rows[:1])
+        return jnp.stack([gate.astype(f32), up.astype(f32), down], axis=0), gain
+
+    grad_ffn, gain_two = order(ffn_gradient, grad_down, gate_scattered, up_scattered)
+    grad_in = order(input_gradient, d_one_sent, x, d_branch, gain_rows[:1])
 
     def qkv_gradient(first, terms, gain_two):
         whole = jnp.concatenate([first, gradient_sum(terms)], axis=1)

time: 513 us -> 504 us (0.982)
  waiting for transfers between devices: 158 us -> 148 us
    ppermute x11 -> x12, waiting for transfers between devices: 94.2 us -> 83.1 us  [chip_shift(): lax.ppermute(value, 'ctx', [(i, (i + 2 * by) % size) for i in range(size)])]
    ppermute x11 -> x12, starting transfers between devices: 13.3 us -> 15 us  [chip_shift(): lax.ppermute(value, 'ctx', [(i, (i + 2 * by) % size) for i in range(size)])]
  transfers between devices with their start and end apart: 53 -> 55, of which waited for: 30 -> 29; matrix products, arithmetic and copies ran while one was open for 9% -> 9% of each run, Pallas kernels for 34% -> 35%
where the time goes in v4:
time: 504 us; the launch traced here: 494 us
  Pallas kernels  225 us (45%)
  waiting for transfers between devices  148 us (29%)
  starting transfers between devices  44.9 us (9%)
  other arithmetic  30.8 us (6%)
  local copies, waits for them, and re-layouts  29 us (6%)
  between operations  14.8 us (3%)
    ppermute x12, waiting for transfers between devices, chip_shift(): lax.ppermute(value, 'ctx', [(i, (i + 2 * by) % size) for i in range(size)])  83.1 us
    pallas_call x12, Pallas kernels, gradient_call(): pl.pallas_call(functools.partial(gradient_kernel, len(left), len(arrived)...  63.8 us
    pallas_call x1, Pallas kernels, feed_forward(): pl.pallas_call(ffn_kernel, grid=(units // FFN_BLOCK,), in_specs=[whole, w...  34.2 us
    pallas_call x2, Pallas kernels, attention_backward(): pl.pallas_call(functools.partial(backward_kernel, heads, count, blocks),...  32.5 us
    ppermute x20, waiting for transfers between devices, core_swap(): return lax.ppermute(value, 'ctx', [(i, i ^ 1) for i in range(size)])  28.3 us
    pallas_call x2, Pallas kernels, attention_forward(): pl.pallas_call(functools.partial(forward_kernel, heads, count, blocks), g...  25.5 us
    ppermute x12, starting transfers between devices, group_shift(): lax.ppermute(value, 'fsdp', [(i, (i + by) % size) for i in range(size)])  19.8 us
    ppermute x12, waiting for transfers between devices, group_shift(): lax.ppermute(value, 'fsdp', [(i, (i + by) % size) for i in range(size)])  19.2 us
  transfers between devices with their start and end apart: 55, of which 29 were waited for; matrix products, arithmetic and copies ran while one was open for 9% of the time, Pallas kernels for 35%

profile of v4, /device:TPU:0, one launch (start us, length us, event | category | flops | bytes accessed | tf_op | source)
XLA Modules:
  0.0 494.2 jit_solution(8197166583648247955)
XLA Ops:
  38.3 17.1 %collective-permute-done.28 = bf16[112,1536]{1,0:T(8,128)(2,1)} collective-permute-done((bf16[112,1536]{1,0:T(8,128)(2,1)S(1)}, bf16[112,1536]{1,0:T(8,128)(2,1)}, u32[]{:S(2)}, u32[]{:S(2)}) %collective-permute-start.28) | collective-permute-done | bytes 344096 | tf_op jit(solution)/shard_map/ppermute | solution.py:656
  65.1 33.9 %collective-permute-done.32 = bf16[3,96,1536]{2,1,0:T(8,128)(2,1)S(1)} collective-permute-done((bf16[3,96,1536]{2,1,0:T(8,128)(2,1)S(1)}, bf16[3,96,1536]{2,1,0:T(8,128)(2,1)S(1)}, u32[]{:S(2)}, u32[]{:S(2)}) %collective-permute-start.32) | collective-permute-done | bytes 884768 | tf_op jit(solution)/shard_map/ppermute | solution.py:651
  120.7 14.1 %collective-permute-done.34 = bf16[2,2,96,768]{3,2,1,0:T(8,128)(2,1)} collective-permute-done((bf16[2,2,96,768]{3,2,1,0:T(8,128)(2,1)}, bf16[2,2,96,768]{3,2,1,0:T(8,128)(2,1)}, u32[]{:S(2)}, u32[]{:S(2)}) %collective-permute-start.34) | collective-permute-done | bytes 589856 | tf_op jit(solution)/shard_map/ppermute | solution.py:651
  134.8 17.6 %conditional.14 = (bf16[2,2,96,768]{3,2,1,0:T(8,128)(2,1)}, f32[2,2,768]{2,1,0:T(2,128)}, bf16[2,2,96,768]{3,2,1,0:T(8,128)(2,1)}, bf16[384,768]{1,0:T(8,128)(2,1)}) conditional(s32[]{:T(128)} %bitcast.14, () %tuple.188, (bf16[2,2,96,768]{3,2,1,0:T(8,128)(2,1)}, s32[6]{0:T(128)}, s32[4]{0:T(128)}, s32[1,768]{1,0:T(1,128)}, s32[1,768]{1,0:T(1,128)}, ...), branch_computations={%region_8.9_spmd, %region_9.10_spmd} | conditional | flops 1 | bytes 3539017 | solution.py:635
  137.1 12.9 %attention_forward.2 = (bf16[2,2,96,768]{3,2,1,0:T(8,128)(2,1)}, f32[2,2,768]{2,1,0:T(2,128)}) custom-call(s32[6]{0:T(128)} %get-tuple-element.174.starts_ref, s32[4]{0:T(128)} %get-tuple-element.175.stripes_ref, s32[1,768]{1,0:T(1,128)} %get-tuple-element.176.place_q_ref, s32[1,768]{1,0:T(1,128)} %get-tuple-element.177.start_q_ref, ...), custom_call_target="tpu_custom_call" | custom-call | flops 1 | bytes 1 | tf_op jit(solution)/shard_map/cond/branch_1_fun/attention_forward/pallas_call | solution.py:188
  152.4 7.2 %collective-permute-done.35 = bf16[2,2,96,768]{3,2,1,0:T(8,128)(2,1)S(1)} collective-permute-done((bf16[2,2,96,768]{3,2,1,0:T(8,128)(2,1)}, bf16[2,2,96,768]{3,2,1,0:T(8,128)(2,1)S(1)}, u32[]{:S(2)}, u32[]{:S(2)}) %collective-permute-start.35) | collective-permute-done | bytes 589856 | tf_op jit(solution)/shard_map/ppermute | solution.py:651
  161.2 16.3 %conditional.15 = (bf16[2,2,96,768]{3,2,1,0:T(8,128)(2,1)}, f32[2,2,768]{2,1,0:T(2,128)}, bf16[2,2,96,768]{3,2,1,0:T(8,128)(2,1)}, bf16[384,768]{1,0:T(8,128)(2,1)S(1)}) conditional(s32[]{:T(128)} %bitcast.14, () %tuple.191, (bf16[2,2,96,768]{3,2,1,0:T(8,128)(2,1)S(1)}, s32[6]{0:T(128)}, s32[4]{0:T(128)}, s32[1,768]{1,0:T(1,128)}, ...), branch_computations={%region_10.11_spmd, %region_11.12_spmd} | conditional | flops 1 | bytes 3539017 | solution.py:635
  163.8 12.6 %attention_forward.3 = (bf16[2,2,96,768]{3,2,1,0:T(8,128)(2,1)}, f32[2,2,768]{2,1,0:T(2,128)}) custom-call(s32[6]{0:T(128)} %get-tuple-element.184.starts_ref, s32[4]{0:T(128)} %get-tuple-element.185.stripes_ref, s32[1,768]{1,0:T(1,128)} %get-tuple-element.186.place_q_ref, s32[1,768]{1,0:T(1,128)} %get-tuple-element.187.start_q_ref, ...), custom_call_target="tpu_custom_call" | custom-call | flops 1 | bytes 1 | tf_op jit(solution)/shard_map/cond/branch_1_fun/attention_forward/pallas_call | solution.py:188
  178.7 7.2 %conditional.16 = (bf16[768,768]{1,0:T(8,128)(2,1)}, bf16[768,768]{1,0:T(8,128)(2,1)}) conditional(s32[]{:T(128)} %bitcast.14, () %tuple.196, (bf16[384,768]{1,0:T(8,128)(2,1)}, bf16[384,768]{1,0:T(8,128)(2,1)}) %tuple.284), branch_computations={%region_12.13_spmd, %region_13.14_spmd} | conditional | bytes 7077944 | solution.py:635
  185.9 8.0 %collective-permute-done.37.refs_3_ = bf16[384,768]{1,0:T(8,128)(2,1)S(1)} collective-permute-done((bf16[384,768]{1,0:T(8,128)(2,1)}, bf16[384,768]{1,0:T(8,128)(2,1)S(1)}, u32[]{:S(2)}, u32[]{:S(2)}) %collective-permute-start.37) | collective-permute-done | bytes 589856 | tf_op jit(solution)/shard_map/ppermute | solution.py:660
  193.9 9.4 %middle.1 = (f32[768,1536]{1,0:T(8,128)}, bf16[768,1536]{1,0:T(8,128)(2,1)S(1)}) custom-call(s32[1]{0:T(128)} %bitcast.48.tp_ref, bf16[768,1536]{1,0:T(8,128)(2,1)S(1)} %bitcast.115, f32[1,1536]{1,0:T(1,128)S(1)} %get-tuple-element.711.gain_ref, bf16[384,768]{1,0:T(8,128)(2,1)} %get-tuple-element.665.refs_0_, bf16[384,768]{1,0:T(8,128)(2,1)} %copy-done.12, ...), custom_call_target="tpu_custom_call" | custom-call | flops 1 | bytes 1 | tf_op jit(solution)/shard_map/middle/pallas_call | solution.py:377
  203.2 34.2 %feed_forward.1 = (bf16[768,2048]{1,0:T(8,128)(2,1)}, bf16[768,2048]{1,0:T(8,128)(2,1)}, bf16[768,2048]{1,0:T(8,128)(2,1)}, bf16[768,1536]{1,0:T(8,128)(2,1)}) custom-call(bf16[768,1536]{1,0:T(8,128)(2,1)S(1)} %get-tuple-element.677.h_ref, bf16[768,1536]{1,0:T(8,128)(2,1)} %bitcast.117, ...), custom_call_target="tpu_custom_call" | custom-call | flops 1 | bytes 1 | tf_op jit(solution)/shard_map/feed_forward/pallas_call | solution.py:569
  237.8 13.1 %conditional.17 = (bf16[4,96,2048]{2,1,0:T(8,128)(2,1)}, bf16[768,2048]{1,0:T(8,128)(2,1)}, bf16[4,2,96,768]{3,2,1,0:T(8,128)(2,1)}, bf16[4,2,96,768]{3,2,1,0:T(8,128)(2,1)}) conditional(s32[]{:T(128)} %bitcast.14, () %tuple.187, (bf16[768,2048]{1,0:T(8,128)(2,1)}, bf16[768,1536]{1,0:T(8,128)(2,1)S(1)}, s32[]{:T(128)}, ...), branch_computations={%region_14.15_spmd, %region_15.16_spmd} | conditional | flops 37 | bytes 17301968 | solution.py:635
  243.9 7.1 %gradient_send.6 = bf16[4,96,2048]{2,1,0:T(8,128)(2,1)} custom-call(s32[2]{0:T(128)S(1)} %pad_add_fusion.place_ref, bf16[4,2,96,768]{3,2,1,0:T(8,128)(2,1)} %get-tuple-element.204.refs_0_, bf16[768,2048]{1,0:T(8,128)(2,1)} %get-tuple-element.205.refs_1_, bf16[4,2,96,768]{3,2,1,0:T(8,128)(2,1)} %get-tuple-element.206.refs_2_, ...), custom_call_target="tpu_custom_call" | custom-call | flops 1 | bytes 1 | tf_op jit(solution)/shard_map/cond/branch_1_fun/gradient_send/pallas_call | solution.py:774
  252.7 24.1 %conditional.18 = (bf16[4,96,2048]{2,1,0:T(8,128)(2,1)}, bf16[4,96,512]{2,1,0:T(8,128)(2,1)}, bf16[4,96,1536]{2,1,0:T(8,128)(2,1)S(1)}, bf16[768,1536]{1,0:T(8,1...) conditional(s32[]{:T(128)} %bitcast.14, () %tuple.203, (bf16[768,2048]{1,0:T(8,128)(2,1)}, ...), branch_computations={%region_16.17_spmd, %region_17.18_spmd} | conditional | flops 38 | bytes 28312032 | solution.py:635
  252.7 9.1 %down_project.1 = bf16[768,1536]{1,0:T(8,128)(2,1)} custom-call(bf16[768,2048]{1,0:T(8,128)(2,1)} %get-tuple-element.214.a_ref, bf16[1536,7680]{1,0:T(8,128)(2,1)} %get-tuple-element.215.w_ref), custom_call_target="tpu_custom_call" | custom-call | flops 1 | bytes 1 | tf_op jit(solution)/shard_map/cond/branch_1_fun/down_project/pallas_call | solution.py:408
  262.3 7.1 %gradient_send.7 = bf16[4,96,2048]{2,1,0:T(8,128)(2,1)} custom-call(s32[2]{0:T(128)S(1)} %pad_add_fusion.1.place_ref, bf16[4,2,96,768]{3,2,1,0:T(8,128)(2,1)} %get-tuple-element.222.refs_0_, bf16[768,2048]{1,0:T(8,128)(2,1)} %get-tuple-element.217.refs_1_, bf16[4,2,96,768]{3,2,1,0:T(8,128)(2,1)} %get-tuple-element.224.refs_2_, ...), custom_call_target="tpu_custom_call" | custom-call | flops 1 | bytes 1 | tf_op jit(solution)/shard_map/cond/branch_1_fun/gradient_send/pallas_call | solution.py:774
  269.4 6.2 %gradient_send.8 = bf16[4,96,2048]{2,1,0:T(8,128)(2,1)S(1)} custom-call(s32[2]{0:T(128)S(1)} %pad_add_fusion.1.place_ref, bf16[4,2,96,768]{3,2,1,0:T(8,128)(2,1)} %get-tuple-element.222.refs_0_, bf16[768,2048]{1,0:T(8,128)(2,1)} %get-tuple-element.223.refs_1_, bf16[4,2,96,768]{3,2,1,0:T(8,128)(2,1)} %get-tuple-element.224.refs_2_, ...), custom_call_target="tpu_custom_call" | custom-call | flops 1 | bytes 1 | tf_op jit(solution)/shard_map/cond/branch_1_fun/gradient_send/pallas_call | solution.py:774
  281.8 5.8 %collective-permute-done.38.refs_4_ = bf16[4,96,2048]{2,1,0:T(8,128)(2,1)} collective-permute-done((bf16[4,96,2048]{2,1,0:T(8,128)(2,1)}, bf16[4,96,2048]{2,1,0:T(8,128)(2,1)}, u32[]{:S(2)}, u32[]{:S(2)}) %collective-permute-start.38) | collective-permute-done | bytes 1572896 | tf_op jit(solution)/shard_map/ppermute | solution.py:651
  290.3 6.4 %gradient_chip.9 = bf16[4,96,2048]{2,1,0:T(8,128)(2,1)S(1)} custom-call(s32[2]{0:T(128)S(1)} %pad_add_fusion.6.place_ref, bf16[4,2,96,768]{3,2,1,0:T(8,128)(2,1)S(1)} %copy-done.13, bf16[768,2048]{1,0:T(8,128)(2,1)} %get-tuple-element.703.refs_1_, bf16[4,2,96,768]{3,2,1,0:T(8,128)(2,1)} %get-tuple-element.704.refs_2_, ...), custom_call_target="tpu_custom_call" | custom-call | flops 1 | bytes 1 | tf_op jit(solution)/shard_map/gradient_chip/pallas_call | solution.py:774
  301.7 9.0 %d_middle.1 = (bf16[768,1536]{1,0:T(8,128)(2,1)}, bf16[384,768]{1,0:T(8,128)(2,1)S(1)}, bf16[384,768]{1,0:T(8,128)(2,1)}) custom-call(bf16[768,1536]{1,0:T(8,128)(2,1)S(1)} %copy-done.7, bf16[768,1536]{1,0:T(8,128)(2,1)} %collective-permute-done.39.other_ref, f32[768,1536]{1,0:T(8,128)} %get-tuple-element.813.middle_ref, bf16[768,1536]{1,0:T(8,128)(2,1)} %bitcast.118, ...), custom_call_target="tpu_custom_call" | custom-call | flops 1 | bytes 1 | tf_op jit(solution)/shard_map/d_middle/pallas_call | solution.py:449
  310.8 19.4 %conditional.19 = (f32[2,2,96,768]{3,2,1,0:T(8,128)}, bf16[2,2,96,768]{3,2,1,0:T(8,128)(2,1)S(1)}, bf16[2,2,96,768]{3,2,1,0:T(8,128)(2,1)S(1)}) conditional(s32[]{:T(128)} %bitcast.14, () %tuple.186, (s32[6]{0:T(128)S(1)}, s32[4]{0:T(128)S(1)}, s32[1,768]{1,0:T(1,128)S(1)}, s32[1,768]{1,0:T(1,128)S(1)}, bf16[2,2,96,768]{3,2,1,0:T(8,128)(2,1)S(1)}, ...), branch_computations={%region_18.19_spmd, %region_19.20_spmd} | conditional | flops 2359297 | bytes 8257641 | solution.py:635
  310.8 15.9 %attention_backward.2 = (f32[2,2,96,768]{3,2,1,0:T(8,128)}, bf16[2,2,96,768]{3,2,1,0:T(8,128)(2,1)S(1)}, bf16[2,2,96,768]{3,2,1,0:T(8,128)(2,1)S(1)}, bf16[2,2,9...) custom-call(s32[6]{0:T(128)S(1)} %get-tuple-element.226.starts_ref, s32[4]{0:T(128)S(1)} %get-tuple-element.227.stripes_ref, ...), custom_call_target="tpu_custom_call" | custom-call | flops 1 | bytes 1 | tf_op jit(solution)/shard_map/cond/branch_1_fun/attention_backward/pallas_call | solution.py:217
  335.6 6.5 %gradient_chip.10 = bf16[4,96,2048]{2,1,0:T(8,128)(2,1)S(1)} custom-call(s32[2]{0:T(128)S(1)} %pad_add_fusion.6.place_ref, bf16[4,2,96,768]{3,2,1,0:T(8,128)(2,1)} %get-tuple-element.773.refs_0_, bf16[768,2048]{1,0:T(8,128)(2,1)} %get-tuple-element.739.refs_1_, bf16[4,2,96,768]{3,2,1,0:T(8,128)(2,1)} %get-tuple-element.775.refs_2_, ...), custom_call_target="tpu_custom_call" | custom-call | flops 1 | bytes 1 | tf_op jit(solution)/shard_map/gradient_chip/pallas_call | solution.py:774
  345.8 20.4 %conditional.20 = (f32[2,2,96,768]{3,2,1,0:T(8,128)}, bf16[2,2,96,768]{3,2,1,0:T(8,128)(2,1)S(1)}, bf16[2,2,96,768]{3,2,1,0:T(8,128)(2,1)}) conditional(s32[]{:T(128)} %bitcast.14, () %tuple.212, (s32[6]{0:T(128)}, s32[4]{0:T(128)}, s32[1,768]{1,0:T(1,128)}, s32[1,768]{1,0:T(1,128)S(1)}, bf16[2,2,96,768]{3,2,1,0:T(8,128)(2,1)}, ...), branch_computations={%region_20.21_spmd, %region_21.22_spmd} | conditional | flops 2359297 | bytes 8257641 | solution.py:635
  345.8 16.6 %attention_backward.3 = (f32[2,2,96,768]{3,2,1,0:T(8,128)}, bf16[2,2,96,768]{3,2,1,0:T(8,128)(2,1)S(1)}, bf16[2,2,96,768]{3,2,1,0:T(8,128)(2,1)S(1)}, bf16[2,2,9...) custom-call(s32[6]{0:T(128)} %get-tuple-element.243.starts_ref, s32[4]{0:T(128)} %get-tuple-element.244.stripes_ref, ...), custom_call_target="tpu_custom_call" | custom-call | flops 1 | bytes 1 | tf_op jit(solution)/shard_map/cond/branch_1_fun/attention_backward/pallas_call | solution.py:217
  368.0 11.4 %conditional.21 = (bf16[4,96,768]{2,1,0:T(8,128)(2,1)S(1)}, bf16[4,2,96,768]{3,2,1,0:T(8,128)(2,1)}, bf16[4,2,96,768]{3,2,1,0:T(8,128)(2,1)}) conditional(s32[]{:T(128)} %bitcast.14, () %tuple.218, (bf16[768,1536]{1,0:T(8,128)(2,1)}, s32[]{:T(128)}, bf16[768,768]{1,0:T(8,128)(2,1)}, bf16[768,768]{1,0:T(8,128)(2,1)}) %tuple.220), branch_computations={%region_22.23_spmd, %region_23.24_spmd} | conditional | flops 37 | bytes 4719009 | solution.py:635
  381.3 6.3 %gradient_chip.11 = bf16[4,96,2048]{2,1,0:T(8,128)(2,1)S(1)} custom-call(s32[2]{0:T(128)S(1)} %pad_add_fusion.6.place_ref, bf16[4,2,96,768]{3,2,1,0:T(8,128)(2,1)} %get-tuple-element.773.refs_0_, bf16[768,2048]{1,0:T(8,128)(2,1)} %get-tuple-element.774.refs_1_, bf16[4,2,96,768]{3,2,1,0:T(8,128)(2,1)} %get-tuple-element.775.refs_2_, ...), custom_call_target="tpu_custom_call" | custom-call | flops 1 | bytes 1 | tf_op jit(solution)/shard_map/gradient_chip/pallas_call | solution.py:774
  393.2 12.9 %conditional.22 = (bf16[768,1536]{1,0:T(8,128)(2,1)}, bf16[768,768]{1,0:T(8,128)(2,1)}, bf16[768,768]{1,0:T(8,128)(2,1)}, bf16[768,768]{1,0:T(8,128)(2,1)}, bf16[768,768]{1,0:T(8,128)(2,1)}) conditional(s32[]{:T(128)} %bitcast.14, () %tuple.185, (f32[2,2,96,768]{3,2,1,0:T(8,128)}, bf16[2,2,96,768]{3,2,1,0:T(8,128)(2,1)S(1)}, ...), branch_computations={%region_24.25_spmd, %region_25.26_spmd} | conditional | flops 3 | bytes 35389648 | solution.py:635
  398.6 7.5 %d_one.1 = bf16[768,1536]{1,0:T(8,128)(2,1)} custom-call(bf16[768,768]{1,0:T(8,128)(2,1)} %turn_back.2.refs_0_, bf16[768,768]{1,0:T(8,128)(2,1)} %turn_back.3.refs_1_, bf16[1536,1536]{1,0:T(8,128)(2,1)S(1)} %copy-done.9), custom_call_target="tpu_custom_call" | custom-call | flops 1 | bytes 1 | tf_op jit(solution)/shard_map/cond/branch_1_fun/d_one/pallas_call | solution.py:515
  410.6 52.3 %conditional.23 = (f32[96,768]{1,0:T(8,128)}, f32[96,768]{1,0:T(8,128)S(1)}, f32[96,768]{1,0:T(8,128)}, bf16[96,768]{1,0:T(8,128)(2,1)}, bf16[96,768]{1,0:T(8,12...) conditional(s32[]{:T(128)} %bitcast.14, () %tuple.171, (bf16[4,96,768]{2,1,0:T(8,128)(2,1)}, ...), branch_computations={%region_28.29_spmd, %region_29.30_spmd} | conditional | flops 6783018 | bytes 43352928 | solution.py:635
  417.0 10.0 %collective-permute-done.18.refs_4_ = bf16[4,96,768]{2,1,0:T(8,128)(2,1)S(1)} collective-permute-done((bf16[4,96,768]{2,1,0:T(8,128)(2,1)}, bf16[4,96,768]{2,1,0:T(8,128)(2,1)S(1)}, u32[]{:S(2)}, u32[]{:S(2)}) %collective-permute-start.18) | collective-permute-done | bytes 589856 | tf_op jit(solution)/shard_map/cond/branch_1_fun/ppermute | solution.py:651
  (300 shorter events, 223.5 us)
Async XLA Ops:
  7.2 186.7 %all-gather.2.cloned.1.call-start = ((), (), s32[]{:S(2)}) async-start(), calls=%async_computation.3 | async-start | bytes 25067520 | tf_op jit(solution)/shard_map/all_gather | solution.py:884
  9.0 13.2 %collective-permute-start.27 = (bf16[112,1536]{1,0:T(8,128)(2,1)S(1)}, bf16[112,1536]{1,0:T(8,128)(2,1)S(1)}, u32[]{:S(2)}, u32[]{:S(2)}) collective-permute-start(bf16[112,1536]{1,0:T(8,128)(2,1)S(1)} %fusion.6), channel_id=1, source_target_pairs={{0,8},{8,16},{16,24},{24,0},{1,9},{9,17},{17,25},{25,1},{2,10},{10... | collective-permute-start | bytes 1032200 | tf_op jit(solution)/shard_map/ppermute | solution.py:656
  22.2 386.4 %reduce-scatter.6.cloned.1.call-start = ((), (), s32[]{:S(2)}) async-start(), calls=%async_computation.5 | async-start | bytes 1966080 | tf_op jit(solution)/shard_map/reduce_scatter | solution.py:815
  22.2 34.2 %collective-permute-start.29 = (bf16[112,1536]{1,0:T(8,128)(2,1)S(1)}, bf16[112,1536]{1,0:T(8,128)(2,1)}, u32[]{:S(2)}, u32[]{:S(2)}) collective-permute-start(bf16[112,1536]{1,0:T(8,128)(2,1)S(1)} %fusion.6), channel_id=1, source_target_pairs={{0,24},{8,0},{16,8},{24,16},{1,25},{9,1},{17,9},{25,17},{2,26},{10... | collective-permute-start | bytes 1032200 | tf_op jit(solution)/shard_map/ppermute | solution.py:656
  24.0 31.4 %collective-permute-start.28 = (bf16[112,1536]{1,0:T(8,128)(2,1)S(1)}, bf16[112,1536]{1,0:T(8,128)(2,1)}, u32[]{:S(2)}, u32[]{:S(2)}) collective-permute-start(bf16[112,1536]{1,0:T(8,128)(2,1)S(1)} %fusion.6), channel_id=1, source_target_pairs={{0,16},{8,24},{16,0},{24,8},{1,17},{9,25},{17,1},{25,9},{2,18},{10... | collective-permute-start | bytes 1032200 | tf_op jit(solution)/shard_map/ppermute | solution.py:656
  57.6 41.4 %collective-permute-start.31 = (bf16[3,96,1536]{2,1,0:T(8,128)(2,1)S(1)}, bf16[3,96,1536]{2,1,0:T(8,128)(2,1)S(1)}, u32[]{:S(2)}, u32[]{:S(2)}) collective-permute-start(bf16[3,96,1536]{2,1,0:T(8,128)(2,1)S(1)} %pad_maximum_fusion.2), channel_id=1, source_target_pairs={{0,2},{2,0},{4,6},{6,4},{1,3},{3,1},{5,7},{7,5},{8,10},{10,8},{12,... | collective-permute-start | bytes 2654216 | tf_op jit(solution)/shard_map/ppermute | solution.py:646
  57.7 41.3 %collective-permute-start.32 = (bf16[3,96,1536]{2,1,0:T(8,128)(2,1)S(1)}, bf16[3,96,1536]{2,1,0:T(8,128)(2,1)S(1)}, u32[]{:S(2)}, u32[]{:S(2)}) collective-permute-start(bf16[3,96,1536]{2,1,0:T(8,128)(2,1)S(1)} %pad_maximum_fusion.2), channel_id=1, source_target_pairs={{0,4},{2,6},{4,0},{6,2},{1,5},{3,7},{5,1},{7,3},{8,12},{10,14},{12... | collective-permute-start | bytes 2654216 | tf_op jit(solution)/shard_map/ppermute | solution.py:651
  105.7 29.1 %collective-permute-start.34 = (bf16[2,2,96,768]{3,2,1,0:T(8,128)(2,1)}, bf16[2,2,96,768]{3,2,1,0:T(8,128)(2,1)}, u32[]{:S(2)}, u32[]{:S(2)}) collective-permute-start(bf16[2,2,96,768]{3,2,1,0:T(8,128)(2,1)} %get-tuple-element.725), channel_id=1, source_target_pairs={{0,4},{2,6},{4,0},{6,2},{1,5},{3,7},{5,1},{7,3},{8,12},{10,14},{12... | collective-permute-start | bytes 1769480 | tf_op jit(solution)/shard_map/ppermute | solution.py:651
  111.2 48.5 %collective-permute-start.35 = (bf16[2,2,96,768]{3,2,1,0:T(8,128)(2,1)}, bf16[2,2,96,768]{3,2,1,0:T(8,128)(2,1)S(1)}, u32[]{:S(2)}, u32[]{:S(2)}) collective-permute-start(bf16[2,2,96,768]{3,2,1,0:T(8,128)(2,1)} %get-tuple-element.752), channel_id=1, source_target_pairs={{0,4},{2,6},{4,0},{6,2},{1,5},{3,7},{5,1},{7,3},{8,12},{10,14},{12... | collective-permute-start | bytes 1769480 | tf_op jit(solution)/shard_map/ppermute | solution.py:651
  159.7 19.0 %collective-permute-start.36 = (bf16[384,768]{1,0:T(8,128)(2,1)}, bf16[384,768]{1,0:T(8,128)(2,1)S(1)}, u32[]{:S(2)}, u32[]{:S(2)}) collective-permute-start(bf16[384,768]{1,0:T(8,128)(2,1)} %get-tuple-element.665.refs_0_), channel_id=1, source_target_pairs={{0,1},{1,0},{2,3},{3,2},{4,5},{5,4},{6,7},{7,6},{8,9},{9,8},{10,11... | collective-permute-start | bytes 1769480 | tf_op jit(solution)/shard_map/ppermute | solution.py:660
  178.3 15.6 %collective-permute-start.37 = (bf16[384,768]{1,0:T(8,128)(2,1)}, bf16[384,768]{1,0:T(8,128)(2,1)S(1)}, u32[]{:S(2)}, u32[]{:S(2)}) collective-permute-start(bf16[384,768]{1,0:T(8,128)(2,1)} %copy-done.12), channel_id=1, source_target_pairs={{0,1},{1,0},{2,3},{3,2},{4,5},{5,4},{6,7},{7,6},{8,9},{9,8},{10,11... | collective-permute-start | bytes 1769480 | tf_op jit(solution)/shard_map/ppermute | solution.py:660
  237.4 52.8 %collective-permute-start.39 = (bf16[768,1536]{1,0:T(8,128)(2,1)}, bf16[768,1536]{1,0:T(8,128)(2,1)}, u32[]{:S(2)}, u32[]{:S(2)}) collective-permute-start(bf16[768,1536]{1,0:T(8,128)(2,1)} %get-tuple-element.707.mine_ref), channel_id=1, source_target_pairs={{0,1},{1,0},{2,3},{3,2},{4,5},{5,4},{6,7},{7,6},{8,9},{9,8},{10,11... | collective-permute-start | bytes 7077896 | tf_op jit(solution)/shard_map/ppermute | solution.py:660
  250.9 36.8 %collective-permute-start.38 = (bf16[4,96,2048]{2,1,0:T(8,128)(2,1)}, bf16[4,96,2048]{2,1,0:T(8,128)(2,1)}, u32[]{:S(2)}, u32[]{:S(2)}) collective-permute-start(bf16[4,96,2048]{2,1,0:T(8,128)(2,1)} %get-tuple-element.681), channel_id=1, source_target_pairs={{0,4},{2,6},{4,0},{6,2},{1,5},{3,7},{5,1},{7,3},{8,12},{10,14},{12... | collective-permute-start | bytes 4718600 | tf_op jit(solution)/shard_map/ppermute | solution.py:651
  297.8 112.7 %reduce-scatter.4.cloned.1.call-start = ((), (), s32[]{:S(2)}) async-start(), calls=%async_computation.4 | async-start | bytes 1966080 | tf_op jit(solution)/shard_map/reduce_scatter | solution.py:815
  297.9 37.7 %collective-permute-start.40 = (bf16[4,96,2048]{2,1,0:T(8,128)(2,1)}, bf16[4,96,2048]{2,1,0:T(8,128)(2,1)}, u32[]{:S(2)}, u32[]{:S(2)}) collective-permute-start(bf16[4,96,2048]{2,1,0:T(8,128)(2,1)} %get-tuple-element.734), channel_id=1, source_target_pairs={{0,4},{2,6},{4,0},{6,2},{1,5},{3,7},{5,1},{7,3},{8,12},{10,14},{12... | collective-permute-start | bytes 4718600 | tf_op jit(solution)/shard_map/ppermute | solution.py:651
  299.6 43.7 %collective-permute-start.41 = (bf16[4,96,512]{2,1,0:T(8,128)(2,1)}, bf16[4,96,512]{2,1,0:T(8,128)(2,1)}, u32[]{:S(2)}, u32[]{:S(2)}) collective-permute-start(bf16[4,96,512]{2,1,0:T(8,128)(2,1)} %get-tuple-element.735), channel_id=1, source_target_pairs={{0,4},{2,6},{4,0},{6,2},{1,5},{3,7},{5,1},{7,3},{8,12},{10,14},{12... | collective-permute-start | bytes 1179656 | tf_op jit(solution)/shard_map/ppermute | solution.py:651
  343.3 125.6 %reduce-scatter.8.cloned.1.call-start = ((), (), s32[]{:S(2)}) async-start(), calls=%async_computation.6 | async-start | bytes 1966080 | tf_op jit(solution)/shard_map/reduce_scatter | solution.py:815
  343.4 49.8 %collective-permute-start.44 = (bf16[768,1536]{1,0:T(8,128)(2,1)}, bf16[768,1536]{1,0:T(8,128)(2,1)}, u32[]{:S(2)}, u32[]{:S(2)}) collective-permute-start(bf16[768,1536]{1,0:T(8,128)(2,1)} %get-tuple-element.814), channel_id=1, source_target_pairs={{0,1},{1,0},{2,3},{3,2},{4,5},{5,4},{6,7},{7,6},{8,9},{9,8},{10,11... | collective-permute-start | bytes 7077896 | tf_op jit(solution)/shard_map/ppermute | solution.py:660
  343.8 35.7 %collective-permute-start.45 = (bf16[4,96,1536]{2,1,0:T(8,128)(2,1)}, bf16[4,96,1536]{2,1,0:T(8,128)(2,1)}, u32[]{:S(2)}, u32[]{:S(2)}) collective-permute-start(bf16[4,96,1536]{2,1,0:T(8,128)(2,1)} %copy-done.31), channel_id=1, source_target_pairs={{0,4},{2,6},{4,0},{6,2},{1,5},{3,7},{5,1},{7,3},{8,12},{10,14},{12... | collective-permute-start | bytes 3538952 | tf_op jit(solution)/shard_map/ppermute | solution.py:651
  345.5 43.2 %collective-permute-start.42 = (bf16[2,2,96,768]{3,2,1,0:T(8,128)(2,1)}, bf16[2,2,96,768]{3,2,1,0:T(8,128)(2,1)}, u32[]{:S(2)}, u32[]{:S(2)}) collective-permute-start(bf16[2,2,96,768]{3,2,1,0:T(8,128)(2,1)} %copy-done.35), channel_id=1, source_target_pairs={{0,4},{2,6},{4,0},{6,2},{1,5},{3,7},{5,1},{7,3},{8,12},{10,14},{12... | collective-permute-start | bytes 1769480 | tf_op jit(solution)/shard_map/ppermute | solution.py:651
  366.2 27.0 %collective-permute-start.43 = (bf16[2,2,96,768]{3,2,1,0:T(8,128)(2,1)}, bf16[2,2,96,768]{3,2,1,0:T(8,128)(2,1)}, u32[]{:S(2)}, u32[]{:S(2)}) collective-permute-start(bf16[2,2,96,768]{3,2,1,0:T(8,128)(2,1)} %get-tuple-element.760), channel_id=1, source_target_pairs={{0,4},{2,6},{4,0},{6,2},{1,5},{3,7},{5,1},{7,3},{8,12},{10,14},{12... | collective-permute-start | bytes 1769480 | tf_op jit(solution)/shard_map/ppermute | solution.py:651
  406.1 67.9 %collective-permute-start.46 = (bf16[768,1536]{1,0:T(8,128)(2,1)}, bf16[768,1536]{1,0:T(8,128)(2,1)}, u32[]{:S(2)}, u32[]{:S(2)}) collective-permute-start(bf16[768,1536]{1,0:T(8,128)(2,1)} %get-tuple-element.822.mine_ref), channel_id=1, source_target_pairs={{0,1},{1,0},{2,3},{3,2},{4,5},{5,4},{6,7},{7,6},{8,9},{9,8},{10,11... | collective-permute-start | bytes 7077896 | tf_op jit(solution)/shard_map/ppermute | solution.py:660
  410.6 16.4 %collective-permute-start.18 = (bf16[4,96,768]{2,1,0:T(8,128)(2,1)}, bf16[4,96,768]{2,1,0:T(8,128)(2,1)S(1)}, u32[]{:S(2)}, u32[]{:S(2)}) collective-permute-start(bf16[4,96,768]{2,1,0:T(8,128)(2,1)} %get-tuple-element.298), channel_id=1, source_target_pairs={{0,4},{2,6},{4,0},{6,2},{1,5},{3,7},{5,1},{7,3},{8,12},{10,14},{12... | collective-permute-start | bytes 1769480 | tf_op jit(solution)/shard_map/cond/branch_1_fun/ppermute | solution.py:651
  416.5 29.7 %collective-permute-start.22 = (bf16[4,96,768]{2,1,0:T(8,128)(2,1)S(1)}, bf16[4,96,768]{2,1,0:T(8,128)(2,1)S(1)}, u32[]{:S(2)}, u32[]{:S(2)}) collective-permute-start(bf16[4,96,768]{2,1,0:T(8,128)(2,1)S(1)} %gradient_send.10), channel_id=1, source_target_pairs={{0,4},{2,6},{4,0},{6,2},{1,5},{3,7},{5,1},{7,3},{8,12},{10,14},{12... | collective-permute-start | bytes 1769480 | tf_op jit(solution)/shard_map/cond/branch_1_fun/ppermute | solution.py:651
  431.1 12.6 %collective-permute-start.19 = (bf16[96,768]{1,0:T(8,128)(2,1)S(1)}, bf16[96,768]{1,0:T(8,128)(2,1)S(1)}, u32[]{:S(2)}, u32[]{:S(2)}) collective-permute-start(bf16[96,768]{1,0:T(8,128)(2,1)S(1)} %get-tuple-element.313), channel_id=1, source_target_pairs={{0,8},{8,16},{16,24},{24,0},{1,9},{9,17},{17,25},{25,1},{2,10},{10... | collective-permute-start | bytes 442376 | tf_op jit(solution)/shard_map/cond/branch_1_fun/ppermute | solution.py:656
  431.2 12.5 %collective-permute-start.20 = (bf16[96,768]{1,0:T(8,128)(2,1)S(1)}, bf16[96,768]{1,0:T(8,128)(2,1)S(1)}, u32[]{:S(2)}, u32[]{:S(2)}) collective-permute-start(bf16[96,768]{1,0:T(8,128)(2,1)S(1)} %get-tuple-element.314), channel_id=1, source_target_pairs={{0,16},{8,24},{16,0},{24,8},{1,17},{9,25},{17,1},{25,9},{2,18},{10... | collective-permute-start | bytes 442376 | tf_op jit(solution)/shard_map/cond/branch_1_fun/ppermute | solution.py:656
  432.9 10.8 %collective-permute-start.21 = (bf16[96,768]{1,0:T(8,128)(2,1)S(1)}, bf16[96,768]{1,0:T(8,128)(2,1)S(1)}, u32[]{:S(2)}, u32[]{:S(2)}) collective-permute-start(bf16[96,768]{1,0:T(8,128)(2,1)S(1)} %get-tuple-element.315), channel_id=1, source_target_pairs={{0,24},{8,0},{16,8},{24,16},{1,25},{9,1},{17,9},{25,17},{2,26},{10... | collective-permute-start | bytes 442376 | tf_op jit(solution)/shard_map/cond/branch_1_fun/ppermute | solution.py:656
  444.5 12.9 %collective-permute-start.26 = (bf16[4,96,768]{2,1,0:T(8,128)(2,1)S(1)}, bf16[4,96,768]{2,1,0:T(8,128)(2,1)S(1)}, u32[]{:S(2)}, u32[]{:S(2)}) collective-permute-start(bf16[4,96,768]{2,1,0:T(8,128)(2,1)S(1)} %gradient_send.11), channel_id=1, source_target_pairs={{0,4},{2,6},{4,0},{6,2},{1,5},{3,7},{5,1},{7,3},{8,12},{10,14},{12... | collective-permute-start | bytes 1769480 | tf_op jit(solution)/shard_map/cond/branch_1_fun/ppermute | solution.py:651
  450.2 11.8 %collective-permute-start.23 = (bf16[96,768]{1,0:T(8,128)(2,1)S(1)}, bf16[96,768]{1,0:T(8,128)(2,1)S(1)}, u32[]{:S(2)}, u32[]{:S(2)}) collective-permute-start(bf16[96,768]{1,0:T(8,128)(2,1)S(1)} %get-tuple-element.338), channel_id=1, source_target_pairs={{0,8},{8,16},{16,24},{24,0},{1,9},{9,17},{17,25},{25,1},{2,10},{10... | collective-permute-start | bytes 442376 | tf_op jit(solution)/shard_map/cond/branch_1_fun/ppermute | solution.py:656
  462.9 18.3 %collective-permute-start.47 = (bf16[96,768]{1,0:T(8,128)(2,1)}, bf16[96,768]{1,0:T(8,128)(2,1)S(1)}, u32[]{:S(2)}, u32[]{:S(2)}) collective-permute-start(bf16[96,768]{1,0:T(8,128)(2,1)} %get-tuple-element.829), channel_id=1, source_target_pairs={{0,8},{8,16},{16,24},{24,0},{1,9},{9,17},{17,25},{25,1},{2,10},{10... | collective-permute-start | bytes 442376 | tf_op jit(solution)/shard_map/ppermute | solution.py:656
  466.5 14.7 %collective-permute-start.48 = (bf16[96,768]{1,0:T(8,128)(2,1)}, bf16[96,768]{1,0:T(8,128)(2,1)S(1)}, u32[]{:S(2)}, u32[]{:S(2)}) collective-permute-start(bf16[96,768]{1,0:T(8,128)(2,1)} %get-tuple-element.830), channel_id=1, source_target_pairs={{0,16},{8,24},{16,0},{24,8},{1,17},{9,25},{17,1},{25,9},{2,18},{10... | collective-permute-start | bytes 442376 | tf_op jit(solution)/shard_map/ppermute | solution.py:656
  468.2 12.9 %collective-permute-start.49 = (bf16[96,768]{1,0:T(8,128)(2,1)}, bf16[96,768]{1,0:T(8,128)(2,1)S(1)}, u32[]{:S(2)}, u32[]{:S(2)}) collective-permute-start(bf16[96,768]{1,0:T(8,128)(2,1)} %get-tuple-element.831), channel_id=1, source_target_pairs={{0,24},{8,0},{16,8},{24,16},{1,25},{9,1},{17,9},{25,17},{2,26},{10... | collective-permute-start | bytes 442376 | tf_op jit(solution)/shard_map/ppermute | solution.py:656
  (73 other events, 639.9 us)
Sparse Core Ops, SparseCore 0:
  22.3 164.5 all-gather.1
  297.9 32.8 reduce-scatter.5
  343.4 32.8 reduce-scatter.3
  393.3 33.8 reduce-scatter.7

commit v5 on v4

--- a/solution.py
+++ b/solution.py
@@ -1055,27 +1055,29 @@
     d_kv_0, d_kv_1, down_sent, up_chip = order(touch, d_kv_0, d_kv_1, down_sent, up_chip)
     up_scattered = gradient_scatter(up_chip)
 
-    def project_back(d_query, d_kv, wq, *tables):
+    def project_back(out_products, d_query, d_kv, wq, *tables):
         inner = Order()
+        out_arrived = gradient_send(out_products)
         parts = [inner(turned_back, q, kv, *tables) for q, kv in zip(d_query, d_kv)]
-        others = [core_swap(p) for p in parts]
-        return inner(d_one_of, parts, wq), parts, others
-
-    d_one_part, d_proj, other_proj = order.apart(
-        project_back, [d_query_0, d_query_1], [d_kv_0, d_kv_1], wq, *tables
+        return inner(d_one_of, parts, wq), parts, out_arrived
+
+    d_one_part, d_proj, out_arrived = order.apart(
+        project_back, out_products, [d_query_0, d_query_1], [d_kv_0, d_kv_1], wq, *tables
     )
     d_one_sent = tp_send(d_one_part)
-    right_proj = list(zip(d_proj, other_proj))
 
     grad_down = order(lambda v: v.astype(f32), down_scattered)
     gate_scattered = order(touch, gate_scattered)[0]
 
-    def tail(left_one, right_proj, left_branch, right_att, out_products, middle, down_sent):
+    def tail(left_one, d_proj, left_branch, right_att, out_arrived, middle, down_sent):
         inner = Order()
-        out_arrived = gradient_send(out_products)
         finish = functools.partial(gradient_chip, turned=True, pieces=True)
-        arrived = gradient_send(inner(turned_products, left_one, right_proj[0]))
-        terms = gradient_groups(inner(finish, left_branch, right_att, out_arrived))
+        other_proj = [core_swap(p) for p in d_proj]
+        chip = inner(finish, left_branch, right_att, out_arrived)
+        right_proj = list(zip(d_proj, inner(touch, *other_proj)))
+        products = inner(turned_products, left_one, right_proj[0])
+        arrived = gradient_send(products)
+        terms = gradient_groups(lax.optimization_barrier((chip, products))[0])
         products = inner(turned_products, left_one, right_proj[1])
         hidden_out = inner(lambda m, s: (m + tp_add(s)).astype(bf16), middle, down_sent)
         grad_out = inner(gradient_sum, terms)
@@ -1085,7 +1087,7 @@
         return grad_out, hidden_out, inner(gradient_sum, terms), chip
 
     grad_out, hidden_out, grad_qkv_0, chip = order.apart(
-        tail, left_one, right_proj, left_branch, right_att, out_products, middle, down_sent
+        tail, left_one, d_proj, left_branch, right_att, out_arrived, middle, down_sent
     )
     terms = gradient_groups(chip)
     own_gains = lax.dynamic_slice_in_dim(

time: 504 us -> 501 us (level)
  waiting for transfers between devices: 148 us -> 139 us
    ppermute x12, waiting for transfers between devices: 83.1 us -> 75.6 us  [chip_shift(): lax.ppermute(value, 'ctx', [(i, (i + 2 * by) % size) for i in range(size)])]
  transfers between devices with their start and end apart: 55 -> 55, of which waited for: 29 -> 28; matrix products, arithmetic and copies ran while one was open for 9% -> 10% of each run, Pallas kernels for 35% -> 36%
where the time goes in v5:
time: 501 us; the launch traced here: 491 us
  Pallas kernels  225 us (45%)
  waiting for transfers between devices  139 us (28%)
  starting transfers between devices  49.5 us (10%)
  other arithmetic  32 us (6%)
  local copies, waits for them, and re-layouts  28.9 us (6%)
  between operations  14.8 us (3%)
    ppermute x12, waiting for transfers between devices, chip_shift(): lax.ppermute(value, 'ctx', [(i, (i + 2 * by) % size) for i in range(size)])  75.6 us
    pallas_call x12, Pallas kernels, gradient_call(): pl.pallas_call(functools.partial(gradient_kernel, len(left), len(arrived)...  64.2 us
    pallas_call x1, Pallas kernels, feed_forward(): pl.pallas_call(ffn_kernel, grid=(units // FFN_BLOCK,), in_specs=[whole, w...  34.2 us
    pallas_call x2, Pallas kernels, attention_backward(): pl.pallas_call(functools.partial(backward_kernel, heads, count, blocks),...  32.5 us
    ppermute x20, waiting for transfers between devices, core_swap(): return lax.ppermute(value, 'ctx', [(i, i ^ 1) for i in range(size)])  27.8 us
    pallas_call x2, Pallas kernels, attention_forward(): pl.pallas_call(functools.partial(forward_kernel, heads, count, blocks), g...  25.4 us
    ppermute x12, starting transfers between devices, group_shift(): lax.ppermute(value, 'fsdp', [(i, (i + by) % size) for i in range(size)])  21 us
    ppermute x12, waiting for transfers between devices, group_shift(): lax.ppermute(value, 'fsdp', [(i, (i + by) % size) for i in range(size)])  20.5 us
  transfers between devices with their start and end apart: 55, of which 28 were waited for; matrix products, arithmetic and copies ran while one was open for 10% of the time, Pallas kernels for 36%

profile of v5, /device:TPU:0, one launch (start us, length us, event | category | flops | bytes accessed | tf_op | source)
XLA Modules:
  0.0 491.0 jit_solution(11422211062307242714)
XLA Ops:
  38.6 16.8 %collective-permute-done.28 = bf16[112,1536]{1,0:T(8,128)(2,1)} collective-permute-done((bf16[112,1536]{1,0:T(8,128)(2,1)S(1)}, bf16[112,1536]{1,0:T(8,128)(2,1)}, u32[]{:S(2)}, u32[]{:S(2)}) %collective-permute-start.28) | collective-permute-done | bytes 344096 | tf_op jit(solution)/shard_map/ppermute | solution.py:656
  65.1 33.9 %collective-permute-done.32 = bf16[3,96,1536]{2,1,0:T(8,128)(2,1)S(1)} collective-permute-done((bf16[3,96,1536]{2,1,0:T(8,128)(2,1)S(1)}, bf16[3,96,1536]{2,1,0:T(8,128)(2,1)S(1)}, u32[]{:S(2)}, u32[]{:S(2)}) %collective-permute-start.32) | collective-permute-done | bytes 884768 | tf_op jit(solution)/shard_map/ppermute | solution.py:651
  120.6 14.1 %collective-permute-done.34 = bf16[2,2,96,768]{3,2,1,0:T(8,128)(2,1)} collective-permute-done((bf16[2,2,96,768]{3,2,1,0:T(8,128)(2,1)}, bf16[2,2,96,768]{3,2,1,0:T(8,128)(2,1)}, u32[]{:S(2)}, u32[]{:S(2)}) %collective-permute-start.34) | collective-permute-done | bytes 589856 | tf_op jit(solution)/shard_map/ppermute | solution.py:651
  134.7 17.6 %conditional.14 = (bf16[2,2,96,768]{3,2,1,0:T(8,128)(2,1)}, f32[2,2,768]{2,1,0:T(2,128)}, bf16[2,2,96,768]{3,2,1,0:T(8,128)(2,1)}, bf16[384,768]{1,0:T(8,128)(2,1)}) conditional(s32[]{:T(128)} %bitcast.14, () %tuple.190, (bf16[2,2,96,768]{3,2,1,0:T(8,128)(2,1)}, s32[6]{0:T(128)}, s32[4]{0:T(128)}, s32[1,768]{1,0:T(1,128)}, s32[1,768]{1,0:T(1,128)}, ...), branch_computations={%region_8.9_spmd, %region_9.10_spmd} | conditional | flops 1 | bytes 3539017 | solution.py:635
  137.1 12.8 %attention_forward.2 = (bf16[2,2,96,768]{3,2,1,0:T(8,128)(2,1)}, f32[2,2,768]{2,1,0:T(2,128)}) custom-call(s32[6]{0:T(128)} %get-tuple-element.172.starts_ref, s32[4]{0:T(128)} %get-tuple-element.173.stripes_ref, s32[1,768]{1,0:T(1,128)} %get-tuple-element.174.place_q_ref, s32[1,768]{1,0:T(1,128)} %get-tuple-element.175.start_q_ref, ...), custom_call_target="tpu_custom_call" | custom-call | flops 1 | bytes 1 | tf_op jit(solution)/shard_map/cond/branch_1_fun/attention_forward/pallas_call | solution.py:188
  152.3 7.3 %collective-permute-done.35 = bf16[2,2,96,768]{3,2,1,0:T(8,128)(2,1)S(1)} collective-permute-done((bf16[2,2,96,768]{3,2,1,0:T(8,128)(2,1)}, bf16[2,2,96,768]{3,2,1,0:T(8,128)(2,1)S(1)}, u32[]{:S(2)}, u32[]{:S(2)}) %collective-permute-start.35) | collective-permute-done | bytes 589856 | tf_op jit(solution)/shard_map/ppermute | solution.py:651
  161.1 15.8 %conditional.15 = (bf16[2,2,96,768]{3,2,1,0:T(8,128)(2,1)}, f32[2,2,768]{2,1,0:T(2,128)}, bf16[2,2,96,768]{3,2,1,0:T(8,128)(2,1)}, bf16[384,768]{1,0:T(8,128)(2,1)S(1)}) conditional(s32[]{:T(128)} %bitcast.14, () %tuple.193, (bf16[2,2,96,768]{3,2,1,0:T(8,128)(2,1)S(1)}, s32[6]{0:T(128)}, s32[4]{0:T(128)}, s32[1,768]{1,0:T(1,128)}, ...), branch_computations={%region_10.11_spmd, %region_11.12_spmd} | conditional | flops 1 | bytes 3539017 | solution.py:635
  163.3 12.6 %attention_forward.3 = (bf16[2,2,96,768]{3,2,1,0:T(8,128)(2,1)}, f32[2,2,768]{2,1,0:T(2,128)}) custom-call(s32[6]{0:T(128)} %get-tuple-element.182.starts_ref, s32[4]{0:T(128)} %get-tuple-element.183.stripes_ref, s32[1,768]{1,0:T(1,128)} %get-tuple-element.184.place_q_ref, s32[1,768]{1,0:T(1,128)} %get-tuple-element.185.start_q_ref, ...), custom_call_target="tpu_custom_call" | custom-call | flops 1 | bytes 1 | tf_op jit(solution)/shard_map/cond/branch_1_fun/attention_forward/pallas_call | solution.py:188
  178.6 7.2 %conditional.16 = (bf16[768,768]{1,0:T(8,128)(2,1)}, bf16[768,768]{1,0:T(8,128)(2,1)}) conditional(s32[]{:T(128)} %bitcast.14, () %tuple.198, (bf16[384,768]{1,0:T(8,128)(2,1)}, bf16[384,768]{1,0:T(8,128)(2,1)}) %tuple.286), branch_computations={%region_12.13_spmd, %region_13.14_spmd} | conditional | bytes 7077944 | solution.py:635
  185.8 7.5 %collective-permute-done.37.refs_3_ = bf16[384,768]{1,0:T(8,128)(2,1)S(1)} collective-permute-done((bf16[384,768]{1,0:T(8,128)(2,1)}, bf16[384,768]{1,0:T(8,128)(2,1)S(1)}, u32[]{:S(2)}, u32[]{:S(2)}) %collective-permute-start.37) | collective-permute-done | bytes 589856 | tf_op jit(solution)/shard_map/ppermute | solution.py:660
  193.3 9.4 %middle.1 = (f32[768,1536]{1,0:T(8,128)}, bf16[768,1536]{1,0:T(8,128)(2,1)S(1)}) custom-call(s32[1]{0:T(128)} %bitcast.48.tp_ref, bf16[768,1536]{1,0:T(8,128)(2,1)S(1)} %bitcast.115, f32[1,1536]{1,0:T(1,128)S(1)} %get-tuple-element.712.gain_ref, bf16[384,768]{1,0:T(8,128)(2,1)} %get-tuple-element.666.refs_0_, bf16[384,768]{1,0:T(8,128)(2,1)} %copy-done.13, ...), custom_call_target="tpu_custom_call" | custom-call | flops 1 | bytes 1 | tf_op jit(solution)/shard_map/middle/pallas_call | solution.py:377
  202.7 34.2 %feed_forward.1 = (bf16[768,2048]{1,0:T(8,128)(2,1)}, bf16[768,2048]{1,0:T(8,128)(2,1)}, bf16[768,2048]{1,0:T(8,128)(2,1)}, bf16[768,1536]{1,0:T(8,128)(2,1)}) custom-call(bf16[768,1536]{1,0:T(8,128)(2,1)S(1)} %get-tuple-element.678.h_ref, bf16[768,1536]{1,0:T(8,128)(2,1)} %bitcast.117, ...), custom_call_target="tpu_custom_call" | custom-call | flops 1 | bytes 1 | tf_op jit(solution)/shard_map/feed_forward/pallas_call | solution.py:569
  237.8 13.1 %conditional.17 = (bf16[4,96,2048]{2,1,0:T(8,128)(2,1)}, bf16[768,2048]{1,0:T(8,128)(2,1)}, bf16[4,2,96,768]{3,2,1,0:T(8,128)(2,1)}, bf16[4,2,96,768]{3,2,1,0:T(8,128)(2,1)}) conditional(s32[]{:T(128)} %bitcast.14, () %tuple.189, (bf16[768,2048]{1,0:T(8,128)(2,1)}, bf16[768,1536]{1,0:T(8,128)(2,1)S(1)}, s32[]{:T(128)}, ...), branch_computations={%region_14.15_spmd, %region_15.16_spmd} | conditional | flops 37 | bytes 17301968 | solution.py:635
  243.8 7.1 %gradient_send.6 = bf16[4,96,2048]{2,1,0:T(8,128)(2,1)} custom-call(s32[2]{0:T(128)S(1)} %pad_add_fusion.place_ref, bf16[4,2,96,768]{3,2,1,0:T(8,128)(2,1)} %get-tuple-element.202.refs_0_, bf16[768,2048]{1,0:T(8,128)(2,1)} %get-tuple-element.203.refs_1_, bf16[4,2,96,768]{3,2,1,0:T(8,128)(2,1)} %get-tuple-element.204.refs_2_, ...), custom_call_target="tpu_custom_call" | custom-call | flops 1 | bytes 1 | tf_op jit(solution)/shard_map/cond/branch_1_fun/gradient_send/pallas_call | solution.py:774
  252.8 24.0 %conditional.18 = (bf16[4,96,2048]{2,1,0:T(8,128)(2,1)}, bf16[4,96,512]{2,1,0:T(8,128)(2,1)}, bf16[4,96,1536]{2,1,0:T(8,128)(2,1)S(1)}, bf16[768,1536]{1,0:T(8,1...) conditional(s32[]{:T(128)} %bitcast.14, () %tuple.205, (bf16[768,2048]{1,0:T(8,128)(2,1)}, ...), branch_computations={%region_16.17_spmd, %region_17.18_spmd} | conditional | flops 38 | bytes 28312032 | solution.py:635
  252.8 9.0 %down_project.1 = bf16[768,1536]{1,0:T(8,128)(2,1)} custom-call(bf16[768,2048]{1,0:T(8,128)(2,1)} %get-tuple-element.212.a_ref, bf16[1536,7680]{1,0:T(8,128)(2,1)} %get-tuple-element.213.w_ref), custom_call_target="tpu_custom_call" | custom-call | flops 1 | bytes 1 | tf_op jit(solution)/shard_map/cond/branch_1_fun/down_project/pallas_call | solution.py:408
  262.4 7.1 %gradient_send.7 = bf16[4,96,2048]{2,1,0:T(8,128)(2,1)} custom-call(s32[2]{0:T(128)S(1)} %pad_add_fusion.1.place_ref, bf16[4,2,96,768]{3,2,1,0:T(8,128)(2,1)} %get-tuple-element.220.refs_0_, bf16[768,2048]{1,0:T(8,128)(2,1)} %get-tuple-element.215.refs_1_, bf16[4,2,96,768]{3,2,1,0:T(8,128)(2,1)} %get-tuple-element.222.refs_2_, ...), custom_call_target="tpu_custom_call" | custom-call | flops 1 | bytes 1 | tf_op jit(solution)/shard_map/cond/branch_1_fun/gradient_send/pallas_call | solution.py:774
  269.4 6.2 %gradient_send.8 = bf16[4,96,2048]{2,1,0:T(8,128)(2,1)S(1)} custom-call(s32[2]{0:T(128)S(1)} %pad_add_fusion.1.place_ref, bf16[4,2,96,768]{3,2,1,0:T(8,128)(2,1)} %get-tuple-element.220.refs_0_, bf16[768,2048]{1,0:T(8,128)(2,1)} %get-tuple-element.221.refs_1_, bf16[4,2,96,768]{3,2,1,0:T(8,128)(2,1)} %get-tuple-element.222.refs_2_, ...), custom_call_target="tpu_custom_call" | custom-call | flops 1 | bytes 1 | tf_op jit(solution)/shard_map/cond/branch_1_fun/gradient_send/pallas_call | solution.py:774
  281.8 5.9 %collective-permute-done.38.refs_4_ = bf16[4,96,2048]{2,1,0:T(8,128)(2,1)} collective-permute-done((bf16[4,96,2048]{2,1,0:T(8,128)(2,1)}, bf16[4,96,2048]{2,1,0:T(8,128)(2,1)}, u32[]{:S(2)}, u32[]{:S(2)}) %collective-permute-start.38) | collective-permute-done | bytes 1572896 | tf_op jit(solution)/shard_map/ppermute | solution.py:651
  289.7 6.4 %gradient_chip.9 = bf16[4,96,2048]{2,1,0:T(8,128)(2,1)S(1)} custom-call(s32[2]{0:T(128)S(1)} %pad_add_fusion.6.place_ref, bf16[4,2,96,768]{3,2,1,0:T(8,128)(2,1)S(1)} %copy-done.14, bf16[768,2048]{1,0:T(8,128)(2,1)} %get-tuple-element.704.refs_1_, bf16[4,2,96,768]{3,2,1,0:T(8,128)(2,1)} %get-tuple-element.705.refs_2_, ...), custom_call_target="tpu_custom_call" | custom-call | flops 1 | bytes 1 | tf_op jit(solution)/shard_map/gradient_chip/pallas_call | solution.py:774
  301.6 9.0 %d_middle.1 = (bf16[768,1536]{1,0:T(8,128)(2,1)}, bf16[384,768]{1,0:T(8,128)(2,1)S(1)}, bf16[384,768]{1,0:T(8,128)(2,1)}) custom-call(bf16[768,1536]{1,0:T(8,128)(2,1)S(1)} %copy-done.7, bf16[768,1536]{1,0:T(8,128)(2,1)} %collective-permute-done.39.other_ref, f32[768,1536]{1,0:T(8,128)} %get-tuple-element.812.middle_ref, bf16[768,1536]{1,0:T(8,128)(2,1)} %bitcast.118, ...), custom_call_target="tpu_custom_call" | custom-call | flops 1 | bytes 1 | tf_op jit(solution)/shard_map/d_middle/pallas_call | solution.py:449
  310.6 19.4 %conditional.19 = (f32[2,2,96,768]{3,2,1,0:T(8,128)}, bf16[2,2,96,768]{3,2,1,0:T(8,128)(2,1)S(1)}, bf16[2,2,96,768]{3,2,1,0:T(8,128)(2,1)S(1)}) conditional(s32[]{:T(128)} %bitcast.14, () %tuple.213, (s32[6]{0:T(128)S(1)}, s32[4]{0:T(128)S(1)}, s32[1,768]{1,0:T(1,128)S(1)}, s32[1,768]{1,0:T(1,128)S(1)}, bf16[2,2,96,768]{3,2,1,0:T(8,128)(2,1)S(1)}, ...), branch_computations={%region_18.19_spmd, %region_19.20_spmd} | conditional | flops 2359297 | bytes 8257641 | solution.py:635
  310.7 16.0 %attention_backward.2 = (f32[2,2,96,768]{3,2,1,0:T(8,128)}, bf16[2,2,96,768]{3,2,1,0:T(8,128)(2,1)S(1)}, bf16[2,2,96,768]{3,2,1,0:T(8,128)(2,1)S(1)}, bf16[2,2,9...) custom-call(s32[6]{0:T(128)S(1)} %get-tuple-element.224.starts_ref, s32[4]{0:T(128)S(1)} %get-tuple-element.225.stripes_ref, ...), custom_call_target="tpu_custom_call" | custom-call | flops 1 | bytes 1 | tf_op jit(solution)/shard_map/cond/branch_1_fun/attention_backward/pallas_call | solution.py:217
  335.4 6.5 %gradient_chip.10 = bf16[4,96,2048]{2,1,0:T(8,128)(2,1)S(1)} custom-call(s32[2]{0:T(128)S(1)} %pad_add_fusion.6.place_ref, bf16[4,2,96,768]{3,2,1,0:T(8,128)(2,1)} %get-tuple-element.774.refs_0_, bf16[768,2048]{1,0:T(8,128)(2,1)} %get-tuple-element.741.refs_1_, bf16[4,2,96,768]{3,2,1,0:T(8,128)(2,1)} %get-tuple-element.776.refs_2_, ...), custom_call_target="tpu_custom_call" | custom-call | flops 1 | bytes 1 | tf_op jit(solution)/shard_map/gradient_chip/pallas_call | solution.py:774
  345.8 20.4 %conditional.20 = (f32[2,2,96,768]{3,2,1,0:T(8,128)}, bf16[2,2,96,768]{3,2,1,0:T(8,128)(2,1)S(1)}, bf16[2,2,96,768]{3,2,1,0:T(8,128)(2,1)}) conditional(s32[]{:T(128)} %bitcast.14, () %tuple.212, (s32[6]{0:T(128)}, s32[4]{0:T(128)}, s32[1,768]{1,0:T(1,128)}, s32[1,768]{1,0:T(1,128)S(1)}, bf16[2,2,96,768]{3,2,1,0:T(8,128)(2,1)}, ...), branch_computations={%region_20.21_spmd, %region_21.22_spmd} | conditional | flops 2359297 | bytes 8257641 | solution.py:635
  345.8 16.6 %attention_backward.3 = (f32[2,2,96,768]{3,2,1,0:T(8,128)}, bf16[2,2,96,768]{3,2,1,0:T(8,128)(2,1)S(1)}, bf16[2,2,96,768]{3,2,1,0:T(8,128)(2,1)S(1)}, bf16[2,2,9...) custom-call(s32[6]{0:T(128)} %get-tuple-element.241.starts_ref, s32[4]{0:T(128)} %get-tuple-element.242.stripes_ref, ...), custom_call_target="tpu_custom_call" | custom-call | flops 1 | bytes 1 | tf_op jit(solution)/shard_map/cond/branch_1_fun/attention_backward/pallas_call | solution.py:217
  368.0 11.4 %conditional.21 = (bf16[4,96,768]{2,1,0:T(8,128)(2,1)S(1)}, bf16[4,2,96,768]{3,2,1,0:T(8,128)(2,1)}, bf16[4,2,96,768]{3,2,1,0:T(8,128)(2,1)}) conditional(s32[]{:T(128)} %bitcast.14, () %tuple.188, (bf16[768,1536]{1,0:T(8,128)(2,1)}, s32[]{:T(128)}, bf16[768,768]{1,0:T(8,128)(2,1)}, bf16[768,768]{1,0:T(8,128)(2,1)}) %tuple.222), branch_computations={%region_22.23_spmd, %region_23.24_spmd} | conditional | flops 37 | bytes 4719009 | solution.py:635
  381.3 6.3 %gradient_chip.11 = bf16[4,96,2048]{2,1,0:T(8,128)(2,1)S(1)} custom-call(s32[2]{0:T(128)S(1)} %pad_add_fusion.6.place_ref, bf16[4,2,96,768]{3,2,1,0:T(8,128)(2,1)} %get-tuple-element.774.refs_0_, bf16[768,2048]{1,0:T(8,128)(2,1)} %get-tuple-element.775.refs_1_, bf16[4,2,96,768]{3,2,1,0:T(8,128)(2,1)} %get-tuple-element.776.refs_2_, ...), custom_call_target="tpu_custom_call" | custom-call | flops 1 | bytes 1 | tf_op jit(solution)/shard_map/gradient_chip/pallas_call | solution.py:774
  388.8 5.9 %collective-permute-done.43 = bf16[2,2,96,768]{3,2,1,0:T(8,128)(2,1)} collective-permute-done((bf16[2,2,96,768]{3,2,1,0:T(8,128)(2,1)}, bf16[2,2,96,768]{3,2,1,0:T(8,128)(2,1)}, u32[]{:S(2)}, u32[]{:S(2)}) %collective-permute-start.43) | collective-permute-done | bytes 589856 | tf_op jit(solution)/shard_map/ppermute | solution.py:651
  394.7 14.4 %conditional.22 = (bf16[768,1536]{1,0:T(8,128)(2,1)}, bf16[768,768]{1,0:T(8,128)(2,1)}, bf16[768,768]{1,0:T(8,128)(2,1)}, bf16[4,96,768]{2,1,0:T(8,128)(2,1)}) conditional(s32[]{:T(128)} %bitcast.14, () %tuple.187, (f32[2,2,96,768]{3,2,1,0:T(8,128)}, bf16[2,2,96,768]{3,2,1,0:T(8,128)(2,1)S(1)}, bf16[2,2,96,768]{3,2,1,0:T(8,128)(2,1)}, ...), branch_computations={%region_24.25_spmd, %region_25.26_spmd} | conditional | flops 3 | bytes 28311712 | solution.py:635
  401.6 7.5 %d_one.1 = bf16[768,1536]{1,0:T(8,128)(2,1)} custom-call(bf16[768,768]{1,0:T(8,128)(2,1)} %turn_back.2.refs_0_, bf16[768,768]{1,0:T(8,128)(2,1)} %turn_back.3.refs_1_, bf16[1536,1536]{1,0:T(8,128)(2,1)S(1)} %copy-done.9), custom_call_target="tpu_custom_call" | custom-call | flops 1 | bytes 1 | tf_op jit(solution)/shard_map/cond/branch_1_fun/d_one/pallas_call | solution.py:515
  413.8 44.6 %conditional.23 = (f32[96,768]{1,0:T(8,128)}, f32[96,768]{1,0:T(8,128)S(1)}, f32[96,768]{1,0:T(8,128)}, bf16[96,768]{1,0:T(8,128)(2,1)}, bf16[96,768]{1,0:T(8,12...) conditional(s32[]{:T(128)} %bitcast.14, () %tuple.173, (bf16[4,2,96,768]{3,2,1,0:T(8,128)(2,1)}, ...), branch_computations={%region_28.29_spmd, %region_29.30_spmd} | conditional | flops 6783018 | bytes 55149428 | solution.py:635
  (295 shorter events, 225.3 us)
Async XLA Ops:
  7.2 186.1 %all-gather.2.cloned.1.call-start = ((), (), s32[]{:S(2)}) async-start(), calls=%async_computation.3 | async-start | bytes 25067520 | tf_op jit(solution)/shard_map/all_gather | solution.py:884
  9.0 13.3 %collective-permute-start.27 = (bf16[112,1536]{1,0:T(8,128)(2,1)S(1)}, bf16[112,1536]{1,0:T(8,128)(2,1)}, u32[]{:S(2)}, u32[]{:S(2)}) collective-permute-start(bf16[112,1536]{1,0:T(8,128)(2,1)S(1)} %fusion.6), channel_id=1, source_target_pairs={{0,8},{8,16},{16,24},{24,0},{1,9},{9,17},{17,25},{25,1},{2,10},{10... | collective-permute-start | bytes 1032200 | tf_op jit(solution)/shard_map/ppermute | solution.py:656
  22.3 389.5 %reduce-scatter.6.cloned.1.call-start = ((), (), s32[]{:S(2)}) async-start(), calls=%async_computation.5 | async-start | bytes 1966080 | tf_op jit(solution)/shard_map/reduce_scatter | solution.py:815
  22.3 34.1 %collective-permute-start.29 = (bf16[112,1536]{1,0:T(8,128)(2,1)S(1)}, bf16[112,1536]{1,0:T(8,128)(2,1)}, u32[]{:S(2)}, u32[]{:S(2)}) collective-permute-start(bf16[112,1536]{1,0:T(8,128)(2,1)S(1)} %fusion.6), channel_id=1, source_target_pairs={{0,24},{8,0},{16,8},{24,16},{1,25},{9,1},{17,9},{25,17},{2,26},{10... | collective-permute-start | bytes 1032200 | tf_op jit(solution)/shard_map/ppermute | solution.py:656
  24.1 31.2 %collective-permute-start.28 = (bf16[112,1536]{1,0:T(8,128)(2,1)S(1)}, bf16[112,1536]{1,0:T(8,128)(2,1)}, u32[]{:S(2)}, u32[]{:S(2)}) collective-permute-start(bf16[112,1536]{1,0:T(8,128)(2,1)S(1)} %fusion.6), channel_id=1, source_target_pairs={{0,16},{8,24},{16,0},{24,8},{1,17},{9,25},{17,1},{25,9},{2,18},{10... | collective-permute-start | bytes 1032200 | tf_op jit(solution)/shard_map/ppermute | solution.py:656
  57.5 41.4 %collective-permute-start.31 = (bf16[3,96,1536]{2,1,0:T(8,128)(2,1)S(1)}, bf16[3,96,1536]{2,1,0:T(8,128)(2,1)S(1)}, u32[]{:S(2)}, u32[]{:S(2)}) collective-permute-start(bf16[3,96,1536]{2,1,0:T(8,128)(2,1)S(1)} %pad_maximum_fusion.2), channel_id=1, source_target_pairs={{0,2},{2,0},{4,6},{6,4},{1,3},{3,1},{5,7},{7,5},{8,10},{10,8},{12,... | collective-permute-start | bytes 2654216 | tf_op jit(solution)/shard_map/ppermute | solution.py:646
  57.6 41.3 %collective-permute-start.32 = (bf16[3,96,1536]{2,1,0:T(8,128)(2,1)S(1)}, bf16[3,96,1536]{2,1,0:T(8,128)(2,1)S(1)}, u32[]{:S(2)}, u32[]{:S(2)}) collective-permute-start(bf16[3,96,1536]{2,1,0:T(8,128)(2,1)S(1)} %pad_maximum_fusion.2), channel_id=1, source_target_pairs={{0,4},{2,6},{4,0},{6,2},{1,5},{3,7},{5,1},{7,3},{8,12},{10,14},{12... | collective-permute-start | bytes 2654216 | tf_op jit(solution)/shard_map/ppermute | solution.py:651
  105.6 29.1 %collective-permute-start.34 = (bf16[2,2,96,768]{3,2,1,0:T(8,128)(2,1)}, bf16[2,2,96,768]{3,2,1,0:T(8,128)(2,1)}, u32[]{:S(2)}, u32[]{:S(2)}) collective-permute-start(bf16[2,2,96,768]{3,2,1,0:T(8,128)(2,1)} %get-tuple-element.734), channel_id=1, source_target_pairs={{0,4},{2,6},{4,0},{6,2},{1,5},{3,7},{5,1},{7,3},{8,12},{10,14},{12... | collective-permute-start | bytes 1769480 | tf_op jit(solution)/shard_map/ppermute | solution.py:651
  111.3 48.3 %collective-permute-start.35 = (bf16[2,2,96,768]{3,2,1,0:T(8,128)(2,1)}, bf16[2,2,96,768]{3,2,1,0:T(8,128)(2,1)S(1)}, u32[]{:S(2)}, u32[]{:S(2)}) collective-permute-start(bf16[2,2,96,768]{3,2,1,0:T(8,128)(2,1)} %get-tuple-element.754), channel_id=1, source_target_pairs={{0,4},{2,6},{4,0},{6,2},{1,5},{3,7},{5,1},{7,3},{8,12},{10,14},{12... | collective-permute-start | bytes 1769480 | tf_op jit(solution)/shard_map/ppermute | solution.py:651
  159.6 19.0 %collective-permute-start.36 = (bf16[384,768]{1,0:T(8,128)(2,1)}, bf16[384,768]{1,0:T(8,128)(2,1)S(1)}, u32[]{:S(2)}, u32[]{:S(2)}) collective-permute-start(bf16[384,768]{1,0:T(8,128)(2,1)} %get-tuple-element.666.refs_0_), channel_id=1, source_target_pairs={{0,1},{1,0},{2,3},{3,2},{4,5},{5,4},{6,7},{7,6},{8,9},{9,8},{10,11... | collective-permute-start | bytes 1769480 | tf_op jit(solution)/shard_map/ppermute | solution.py:660
  177.8 15.6 %collective-permute-start.37 = (bf16[384,768]{1,0:T(8,128)(2,1)}, bf16[384,768]{1,0:T(8,128)(2,1)S(1)}, u32[]{:S(2)}, u32[]{:S(2)}) collective-permute-start(bf16[384,768]{1,0:T(8,128)(2,1)} %copy-done.13), channel_id=1, source_target_pairs={{0,1},{1,0},{2,3},{3,2},{4,5},{5,4},{6,7},{7,6},{8,9},{9,8},{10,11... | collective-permute-start | bytes 1769480 | tf_op jit(solution)/shard_map/ppermute | solution.py:660
  236.9 52.8 %collective-permute-start.39 = (bf16[768,1536]{1,0:T(8,128)(2,1)}, bf16[768,1536]{1,0:T(8,128)(2,1)}, u32[]{:S(2)}, u32[]{:S(2)}) collective-permute-start(bf16[768,1536]{1,0:T(8,128)(2,1)} %get-tuple-element.708.mine_ref), channel_id=1, source_target_pairs={{0,1},{1,0},{2,3},{3,2},{4,5},{5,4},{6,7},{7,6},{8,9},{9,8},{10,11... | collective-permute-start | bytes 7077896 | tf_op jit(solution)/shard_map/ppermute | solution.py:660
  250.9 36.8 %collective-permute-start.38 = (bf16[4,96,2048]{2,1,0:T(8,128)(2,1)}, bf16[4,96,2048]{2,1,0:T(8,128)(2,1)}, u32[]{:S(2)}, u32[]{:S(2)}) collective-permute-start(bf16[4,96,2048]{2,1,0:T(8,128)(2,1)} %get-tuple-element.682), channel_id=1, source_target_pairs={{0,4},{2,6},{4,0},{6,2},{1,5},{3,7},{5,1},{7,3},{8,12},{10,14},{12... | collective-permute-start | bytes 4718600 | tf_op jit(solution)/shard_map/ppermute | solution.py:651
  297.3 116.4 %reduce-scatter.4.cloned.1.call-start = ((), (), s32[]{:S(2)}) async-start(), calls=%async_computation.4 | async-start | bytes 1966080 | tf_op jit(solution)/shard_map/reduce_scatter | solution.py:815
  297.4 38.0 %collective-permute-start.40 = (bf16[4,96,2048]{2,1,0:T(8,128)(2,1)}, bf16[4,96,2048]{2,1,0:T(8,128)(2,1)}, u32[]{:S(2)}, u32[]{:S(2)}) collective-permute-start(bf16[4,96,2048]{2,1,0:T(8,128)(2,1)} %get-tuple-element.720), channel_id=1, source_target_pairs={{0,4},{2,6},{4,0},{6,2},{1,5},{3,7},{5,1},{7,3},{8,12},{10,14},{12... | collective-permute-start | bytes 4718600 | tf_op jit(solution)/shard_map/ppermute | solution.py:651
  299.8 43.3 %collective-permute-start.41 = (bf16[4,96,512]{2,1,0:T(8,128)(2,1)}, bf16[4,96,512]{2,1,0:T(8,128)(2,1)}, u32[]{:S(2)}, u32[]{:S(2)}) collective-permute-start(bf16[4,96,512]{2,1,0:T(8,128)(2,1)} %get-tuple-element.721), channel_id=1, source_target_pairs={{0,4},{2,6},{4,0},{6,2},{1,5},{3,7},{5,1},{7,3},{8,12},{10,14},{12... | collective-permute-start | bytes 1179656 | tf_op jit(solution)/shard_map/ppermute | solution.py:651
  343.1 121.5 %reduce-scatter.8.cloned.1.call-start = ((), (), s32[]{:S(2)}) async-start(), calls=%async_computation.6 | async-start | bytes 1966080 | tf_op jit(solution)/shard_map/reduce_scatter | solution.py:815
  343.2 51.5 %collective-permute-start.44 = (bf16[768,1536]{1,0:T(8,128)(2,1)}, bf16[768,1536]{1,0:T(8,128)(2,1)}, u32[]{:S(2)}, u32[]{:S(2)}) collective-permute-start(bf16[768,1536]{1,0:T(8,128)(2,1)} %get-tuple-element.813), channel_id=1, source_target_pairs={{0,1},{1,0},{2,3},{3,2},{4,5},{5,4},{6,7},{7,6},{8,9},{9,8},{10,11... | collective-permute-start | bytes 7077896 | tf_op jit(solution)/shard_map/ppermute | solution.py:660
  343.8 35.7 %collective-permute-start.45 = (bf16[4,96,1536]{2,1,0:T(8,128)(2,1)}, bf16[4,96,1536]{2,1,0:T(8,128)(2,1)}, u32[]{:S(2)}, u32[]{:S(2)}) collective-permute-start(bf16[4,96,1536]{2,1,0:T(8,128)(2,1)} %copy-done.32), channel_id=1, source_target_pairs={{0,4},{2,6},{4,0},{6,2},{1,5},{3,7},{5,1},{7,3},{8,12},{10,14},{12... | collective-permute-start | bytes 3538952 | tf_op jit(solution)/shard_map/ppermute | solution.py:651
  345.6 43.1 %collective-permute-start.42 = (bf16[2,2,96,768]{3,2,1,0:T(8,128)(2,1)}, bf16[2,2,96,768]{3,2,1,0:T(8,128)(2,1)}, u32[]{:S(2)}, u32[]{:S(2)}) collective-permute-start(bf16[2,2,96,768]{3,2,1,0:T(8,128)(2,1)} %copy-done.36), channel_id=1, source_target_pairs={{0,4},{2,6},{4,0},{6,2},{1,5},{3,7},{5,1},{7,3},{8,12},{10,14},{12... | collective-permute-start | bytes 1769480 | tf_op jit(solution)/shard_map/ppermute | solution.py:651
  366.2 28.5 %collective-permute-start.43 = (bf16[2,2,96,768]{3,2,1,0:T(8,128)(2,1)}, bf16[2,2,96,768]{3,2,1,0:T(8,128)(2,1)}, u32[]{:S(2)}, u32[]{:S(2)}) collective-permute-start(bf16[2,2,96,768]{3,2,1,0:T(8,128)(2,1)} %get-tuple-element.767), channel_id=1, source_target_pairs={{0,4},{2,6},{4,0},{6,2},{1,5},{3,7},{5,1},{7,3},{8,12},{10,14},{12... | collective-permute-start | bytes 1769480 | tf_op jit(solution)/shard_map/ppermute | solution.py:651
  394.8 14.4 %collective-permute-start.6 = (bf16[4,96,768]{2,1,0:T(8,128)(2,1)}, bf16[4,96,768]{2,1,0:T(8,128)(2,1)}, u32[]{:S(2)}, u32[]{:S(2)}) collective-permute-start(bf16[4,96,768]{2,1,0:T(8,128)(2,1)} %get-tuple-element.292), channel_id=1, source_target_pairs={{0,4},{2,6},{4,0},{6,2},{1,5},{3,7},{5,1},{7,3},{8,12},{10,14},{12... | collective-permute-start | bytes 1769480 | tf_op jit(solution)/shard_map/cond/branch_1_fun/ppermute | solution.py:651
  409.2 60.6 %collective-permute-start.46 = (bf16[768,1536]{1,0:T(8,128)(2,1)}, bf16[768,1536]{1,0:T(8,128)(2,1)}, u32[]{:S(2)}, u32[]{:S(2)}) collective-permute-start(bf16[768,1536]{1,0:T(8,128)(2,1)} %get-tuple-element.821.mine_ref), channel_id=1, source_target_pairs={{0,1},{1,0},{2,3},{3,2},{4,5},{5,4},{6,7},{7,6},{8,9},{9,8},{10,11... | collective-permute-start | bytes 7077896 | tf_op jit(solution)/shard_map/ppermute | solution.py:660
  423.1 17.4 %collective-permute-start.22 = (bf16[4,96,768]{2,1,0:T(8,128)(2,1)S(1)}, bf16[4,96,768]{2,1,0:T(8,128)(2,1)S(1)}, u32[]{:S(2)}, u32[]{:S(2)}) collective-permute-start(bf16[4,96,768]{2,1,0:T(8,128)(2,1)S(1)} %gradient_send.10), channel_id=1, source_target_pairs={{0,4},{2,6},{4,0},{6,2},{1,5},{3,7},{5,1},{7,3},{8,12},{10,14},{12... | collective-permute-start | bytes 1769480 | tf_op jit(solution)/shard_map/cond/branch_1_fun/ppermute | solution.py:651
  423.3 12.5 %collective-permute-start.19 = (bf16[96,768]{1,0:T(8,128)(2,1)}, bf16[96,768]{1,0:T(8,128)(2,1)S(1)}, u32[]{:S(2)}, u32[]{:S(2)}) collective-permute-start(bf16[96,768]{1,0:T(8,128)(2,1)} %get-tuple-element.317), channel_id=1, source_target_pairs={{0,8},{8,16},{16,24},{24,0},{1,9},{9,17},{17,25},{25,1},{2,10},{10... | collective-permute-start | bytes 442376 | tf_op jit(solution)/shard_map/cond/branch_1_fun/ppermute | solution.py:656
  423.3 14.8 %collective-permute-start.20 = (bf16[96,768]{1,0:T(8,128)(2,1)S(1)}, bf16[96,768]{1,0:T(8,128)(2,1)S(1)}, u32[]{:S(2)}, u32[]{:S(2)}) collective-permute-start(bf16[96,768]{1,0:T(8,128)(2,1)S(1)} %get-tuple-element.318), channel_id=1, source_target_pairs={{0,16},{8,24},{16,0},{24,8},{1,17},{9,25},{17,1},{25,9},{2,18},{10... | collective-permute-start | bytes 442376 | tf_op jit(solution)/shard_map/cond/branch_1_fun/ppermute | solution.py:656
  423.3 14.8 %collective-permute-start.21 = (bf16[96,768]{1,0:T(8,128)(2,1)S(1)}, bf16[96,768]{1,0:T(8,128)(2,1)S(1)}, u32[]{:S(2)}, u32[]{:S(2)}) collective-permute-start(bf16[96,768]{1,0:T(8,128)(2,1)S(1)} %get-tuple-element.319), channel_id=1, source_target_pairs={{0,24},{8,0},{16,8},{24,16},{1,25},{9,1},{17,9},{25,17},{2,26},{10... | collective-permute-start | bytes 442376 | tf_op jit(solution)/shard_map/cond/branch_1_fun/ppermute | solution.py:656
  438.9 14.8 %collective-permute-start.26 = (bf16[4,96,768]{2,1,0:T(8,128)(2,1)S(1)}, bf16[4,96,768]{2,1,0:T(8,128)(2,1)S(1)}, u32[]{:S(2)}, u32[]{:S(2)}) collective-permute-start(bf16[4,96,768]{2,1,0:T(8,128)(2,1)S(1)} %gradient_send.11), channel_id=1, source_target_pairs={{0,4},{2,6},{4,0},{6,2},{1,5},{3,7},{5,1},{7,3},{8,12},{10,14},{12... | collective-permute-start | bytes 1769480 | tf_op jit(solution)/shard_map/cond/branch_1_fun/ppermute | solution.py:651
  444.4 13.8 %collective-permute-start.23 = (bf16[96,768]{1,0:T(8,128)(2,1)S(1)}, bf16[96,768]{1,0:T(8,128)(2,1)S(1)}, u32[]{:S(2)}, u32[]{:S(2)}) collective-permute-start(bf16[96,768]{1,0:T(8,128)(2,1)S(1)} %get-tuple-element.341), channel_id=1, source_target_pairs={{0,8},{8,16},{16,24},{24,0},{1,9},{9,17},{17,25},{25,1},{2,10},{10... | collective-permute-start | bytes 442376 | tf_op jit(solution)/shard_map/cond/branch_1_fun/ppermute | solution.py:656
  458.3 18.6 %collective-permute-start.47 = (bf16[96,768]{1,0:T(8,128)(2,1)}, bf16[96,768]{1,0:T(8,128)(2,1)}, u32[]{:S(2)}, u32[]{:S(2)}) collective-permute-start(bf16[96,768]{1,0:T(8,128)(2,1)} %get-tuple-element.828), channel_id=1, source_target_pairs={{0,8},{8,16},{16,24},{24,0},{1,9},{9,17},{17,25},{25,1},{2,10},{10... | collective-permute-start | bytes 442376 | tf_op jit(solution)/shard_map/ppermute | solution.py:656
  462.2 14.7 %collective-permute-start.48 = (bf16[96,768]{1,0:T(8,128)(2,1)}, bf16[96,768]{1,0:T(8,128)(2,1)}, u32[]{:S(2)}, u32[]{:S(2)}) collective-permute-start(bf16[96,768]{1,0:T(8,128)(2,1)} %get-tuple-element.829), channel_id=1, source_target_pairs={{0,16},{8,24},{16,0},{24,8},{1,17},{9,25},{17,1},{25,9},{2,18},{10... | collective-permute-start | bytes 442376 | tf_op jit(solution)/shard_map/ppermute | solution.py:656
  464.3 12.6 %collective-permute-start.49 = (bf16[96,768]{1,0:T(8,128)(2,1)}, bf16[96,768]{1,0:T(8,128)(2,1)}, u32[]{:S(2)}, u32[]{:S(2)}) collective-permute-start(bf16[96,768]{1,0:T(8,128)(2,1)} %get-tuple-element.830), channel_id=1, source_target_pairs={{0,24},{8,0},{16,8},{24,16},{1,25},{9,1},{17,9},{25,17},{2,26},{10... | collective-permute-start | bytes 442376 | tf_op jit(solution)/shard_map/ppermute | solution.py:656
  (71 other events, 596.3 us)
Sparse Core Ops, SparseCore 0:
  22.4 164.5 all-gather.1
  297.5 33.3 reduce-scatter.5
  343.3 33.0 reduce-scatter.3
  394.8 34.5 reduce-scatter.7

commit v6 on v5

--- a/solution.py
+++ b/solution.py
@@ -738,7 +738,7 @@
     groups, chips, rows, tokens = left[0].shape
     group = lax.axis_index("fsdp")
     columns = right[0].shape[0 if turned else 1]
-    block = next((b for b in (512, 384) if columns % b == 0), columns)
+    block = next((b for b in (768, 512, 384) if columns % b == 0), columns)
     if rows % 16 or columns % block:
         total = None
         for a, b in zip(left, right):
@@ -989,7 +989,7 @@
         gate_products = inner(gradient_products, left_two, (d_gate, other_gate))
         other_up = core_swap(lax.optimization_barrier((d_up, down_sum))[0])
         up_products = inner(gradient_products, left_two, (d_up, other_up))
-        early = units // 4
+        early = units // 16 * 5
         up_products = [[p[:, :, :early] for p in up_products], [p[:, :, early:] for p in up_products]]
         return gate_products, up_products, down_sum, other_gate, other_up
 

time: 501 us -> 500 us (level)
  transfers between devices with their start and end apart: 55 -> 55, of which waited for: 28 -> 31; matrix products, arithmetic and copies ran while one was open for 10% -> 10% of each run, Pallas kernels for 36% -> 35%
where the time goes in v6:
time: 500 us; the launch traced here: 490 us
  Pallas kernels  223 us (45%)
  waiting for transfers between devices  142 us (28%)
  starting transfers between devices  46.9 us (9%)
  other arithmetic  32 us (6%)
  local copies, waits for them, and re-layouts  29 us (6%)
  between operations  14.8 us (3%)
    ppermute x12, waiting for transfers between devices, chip_shift(): lax.ppermute(value, 'ctx', [(i, (i + 2 * by) % size) for i in range(size)])  75.9 us
    pallas_call x12, Pallas kernels, gradient_call(): pl.pallas_call(functools.partial(gradient_kernel, len(left), len(arrived)...  62.9 us
    pallas_call x1, Pallas kernels, feed_forward(): pl.pallas_call(ffn_kernel, grid=(units // FFN_BLOCK,), in_specs=[whole, w...  34.2 us
    pallas_call x2, Pallas kernels, attention_backward(): pl.pallas_call(functools.partial(backward_kernel, heads, count, blocks),...  32.6 us
    ppermute x20, waiting for transfers between devices, core_swap(): return lax.ppermute(value, 'ctx', [(i, i ^ 1) for i in range(size)])  27.8 us
    pallas_call x2, Pallas kernels, attention_forward(): pl.pallas_call(functools.partial(forward_kernel, heads, count, blocks), g...  25.5 us
    ppermute x12, waiting for transfers between devices, group_shift(): lax.ppermute(value, 'fsdp', [(i, (i + by) % size) for i in range(size)])  21.1 us
    ppermute x12, starting transfers between devices, group_shift(): lax.ppermute(value, 'fsdp', [(i, (i + by) % size) for i in range(size)])  20.7 us
  transfers between devices with their start and end apart: 55, of which 31 were waited for; matrix products, arithmetic and copies ran while one was open for 10% of the time, Pallas kernels for 35%

profile of v6, /device:TPU:0, one launch (start us, length us, event | category | flops | bytes accessed | tf_op | source)
XLA Modules:
  0.0 490.2 jit_solution(3051695337571003335)
XLA Ops:
  38.5 16.9 %collective-permute-done.28 = bf16[112,1536]{1,0:T(8,128)(2,1)} collective-permute-done((bf16[112,1536]{1,0:T(8,128)(2,1)S(1)}, bf16[112,1536]{1,0:T(8,128)(2,1)}, u32[]{:S(2)}, u32[]{:S(2)}) %collective-permute-start.28) | collective-permute-done | bytes 344096 | tf_op jit(solution)/shard_map/ppermute | solution.py:656
  65.1 33.9 %collective-permute-done.32 = bf16[3,96,1536]{2,1,0:T(8,128)(2,1)S(1)} collective-permute-done((bf16[3,96,1536]{2,1,0:T(8,128)(2,1)S(1)}, bf16[3,96,1536]{2,1,0:T(8,128)(2,1)S(1)}, u32[]{:S(2)}, u32[]{:S(2)}) %collective-permute-start.32) | collective-permute-done | bytes 884768 | tf_op jit(solution)/shard_map/ppermute | solution.py:651
  120.6 14.1 %collective-permute-done.34 = bf16[2,2,96,768]{3,2,1,0:T(8,128)(2,1)} collective-permute-done((bf16[2,2,96,768]{3,2,1,0:T(8,128)(2,1)}, bf16[2,2,96,768]{3,2,1,0:T(8,128)(2,1)}, u32[]{:S(2)}, u32[]{:S(2)}) %collective-permute-start.34) | collective-permute-done | bytes 589856 | tf_op jit(solution)/shard_map/ppermute | solution.py:651
  134.7 17.6 %conditional.14 = (bf16[2,2,96,768]{3,2,1,0:T(8,128)(2,1)}, f32[2,2,768]{2,1,0:T(2,128)}, bf16[2,2,96,768]{3,2,1,0:T(8,128)(2,1)}, bf16[384,768]{1,0:T(8,128)(2,1)}) conditional(s32[]{:T(128)} %bitcast.14, () %tuple.190, (bf16[2,2,96,768]{3,2,1,0:T(8,128)(2,1)}, s32[6]{0:T(128)}, s32[4]{0:T(128)}, s32[1,768]{1,0:T(1,128)}, s32[1,768]{1,0:T(1,128)}, ...), branch_computations={%region_8.9_spmd, %region_9.10_spmd} | conditional | flops 1 | bytes 3539017 | solution.py:635
  137.1 12.9 %attention_forward.2 = (bf16[2,2,96,768]{3,2,1,0:T(8,128)(2,1)}, f32[2,2,768]{2,1,0:T(2,128)}) custom-call(s32[6]{0:T(128)} %get-tuple-element.172.starts_ref, s32[4]{0:T(128)} %get-tuple-element.173.stripes_ref, s32[1,768]{1,0:T(1,128)} %get-tuple-element.174.place_q_ref, s32[1,768]{1,0:T(1,128)} %get-tuple-element.175.start_q_ref, ...), custom_call_target="tpu_custom_call" | custom-call | flops 1 | bytes 1 | tf_op jit(solution)/shard_map/cond/branch_1_fun/attention_forward/pallas_call | solution.py:188
  152.4 7.2 %collective-permute-done.35 = bf16[2,2,96,768]{3,2,1,0:T(8,128)(2,1)S(1)} collective-permute-done((bf16[2,2,96,768]{3,2,1,0:T(8,128)(2,1)}, bf16[2,2,96,768]{3,2,1,0:T(8,128)(2,1)S(1)}, u32[]{:S(2)}, u32[]{:S(2)}) %collective-permute-start.35) | collective-permute-done | bytes 589856 | tf_op jit(solution)/shard_map/ppermute | solution.py:651
  161.1 15.8 %conditional.15 = (bf16[2,2,96,768]{3,2,1,0:T(8,128)(2,1)}, f32[2,2,768]{2,1,0:T(2,128)}, bf16[2,2,96,768]{3,2,1,0:T(8,128)(2,1)}, bf16[384,768]{1,0:T(8,128)(2,1)S(1)}) conditional(s32[]{:T(128)} %bitcast.14, () %tuple.193, (bf16[2,2,96,768]{3,2,1,0:T(8,128)(2,1)S(1)}, s32[6]{0:T(128)}, s32[4]{0:T(128)}, s32[1,768]{1,0:T(1,128)}, ...), branch_computations={%region_10.11_spmd, %region_11.12_spmd} | conditional | flops 1 | bytes 3539017 | solution.py:635
  163.3 12.6 %attention_forward.3 = (bf16[2,2,96,768]{3,2,1,0:T(8,128)(2,1)}, f32[2,2,768]{2,1,0:T(2,128)}) custom-call(s32[6]{0:T(128)} %get-tuple-element.182.starts_ref, s32[4]{0:T(128)} %get-tuple-element.183.stripes_ref, s32[1,768]{1,0:T(1,128)} %get-tuple-element.184.place_q_ref, s32[1,768]{1,0:T(1,128)} %get-tuple-element.185.start_q_ref, ...), custom_call_target="tpu_custom_call" | custom-call | flops 1 | bytes 1 | tf_op jit(solution)/shard_map/cond/branch_1_fun/attention_forward/pallas_call | solution.py:188
  178.7 7.2 %conditional.16 = (bf16[768,768]{1,0:T(8,128)(2,1)}, bf16[768,768]{1,0:T(8,128)(2,1)}) conditional(s32[]{:T(128)} %bitcast.14, () %tuple.198, (bf16[384,768]{1,0:T(8,128)(2,1)}, bf16[384,768]{1,0:T(8,128)(2,1)}) %tuple.286), branch_computations={%region_12.13_spmd, %region_13.14_spmd} | conditional | bytes 7077944 | solution.py:635
  185.9 7.5 %collective-permute-done.37.refs_3_ = bf16[384,768]{1,0:T(8,128)(2,1)S(1)} collective-permute-done((bf16[384,768]{1,0:T(8,128)(2,1)}, bf16[384,768]{1,0:T(8,128)(2,1)S(1)}, u32[]{:S(2)}, u32[]{:S(2)}) %collective-permute-start.37) | collective-permute-done | bytes 589856 | tf_op jit(solution)/shard_map/ppermute | solution.py:660
  193.4 9.4 %middle.1 = (f32[768,1536]{1,0:T(8,128)}, bf16[768,1536]{1,0:T(8,128)(2,1)S(1)}) custom-call(s32[1]{0:T(128)} %bitcast.48.tp_ref, bf16[768,1536]{1,0:T(8,128)(2,1)S(1)} %bitcast.115, f32[1,1536]{1,0:T(1,128)S(1)} %get-tuple-element.712.gain_ref, bf16[384,768]{1,0:T(8,128)(2,1)} %get-tuple-element.666.refs_0_, bf16[384,768]{1,0:T(8,128)(2,1)} %copy-done.13, ...), custom_call_target="tpu_custom_call" | custom-call | flops 1 | bytes 1 | tf_op jit(solution)/shard_map/middle/pallas_call | solution.py:377
  202.7 34.2 %feed_forward.1 = (bf16[768,2048]{1,0:T(8,128)(2,1)}, bf16[768,2048]{1,0:T(8,128)(2,1)}, bf16[768,2048]{1,0:T(8,128)(2,1)}, bf16[768,1536]{1,0:T(8,128)(2,1)}) custom-call(bf16[768,1536]{1,0:T(8,128)(2,1)S(1)} %get-tuple-element.678.h_ref, bf16[768,1536]{1,0:T(8,128)(2,1)} %bitcast.117, ...), custom_call_target="tpu_custom_call" | custom-call | flops 1 | bytes 1 | tf_op jit(solution)/shard_map/feed_forward/pallas_call | solution.py:569
  237.8 13.1 %conditional.17 = (bf16[4,96,2048]{2,1,0:T(8,128)(2,1)}, bf16[768,2048]{1,0:T(8,128)(2,1)}, bf16[4,2,96,768]{3,2,1,0:T(8,128)(2,1)}, bf16[4,2,96,768]{3,2,1,0:T(8,128)(2,1)}) conditional(s32[]{:T(128)} %bitcast.14, () %tuple.189, (bf16[768,2048]{1,0:T(8,128)(2,1)}, bf16[768,1536]{1,0:T(8,128)(2,1)S(1)}, s32[]{:T(128)}, ...), branch_computations={%region_14.15_spmd, %region_15.16_spmd} | conditional | flops 37 | bytes 17301968 | solution.py:635
  243.8 7.1 %gradient_send.6 = bf16[4,96,2048]{2,1,0:T(8,128)(2,1)} custom-call(s32[2]{0:T(128)S(1)} %pad_add_fusion.place_ref, bf16[4,2,96,768]{3,2,1,0:T(8,128)(2,1)} %get-tuple-element.202.refs_0_, bf16[768,2048]{1,0:T(8,128)(2,1)} %get-tuple-element.203.refs_1_, bf16[4,2,96,768]{3,2,1,0:T(8,128)(2,1)} %get-tuple-element.204.refs_2_, ...), custom_call_target="tpu_custom_call" | custom-call | flops 1 | bytes 1 | tf_op jit(solution)/shard_map/cond/branch_1_fun/gradient_send/pallas_call | solution.py:774
  252.8 24.1 %conditional.18 = (bf16[4,96,2048]{2,1,0:T(8,128)(2,1)}, bf16[4,96,640]{2,1,0:T(8,128)(2,1)}, bf16[4,96,1408]{2,1,0:T(8,128)(2,1)S(1)}, bf16[768,1536]{1,0:T(8,1...) conditional(s32[]{:T(128)} %bitcast.14, () %tuple.205, (bf16[768,2048]{1,0:T(8,128)(2,1)}, ...), branch_computations={%region_16.17_spmd, %region_17.18_spmd} | conditional | flops 38 | bytes 28312032 | solution.py:635
  253.1 9.0 %down_project.1 = bf16[768,1536]{1,0:T(8,128)(2,1)} custom-call(bf16[768,2048]{1,0:T(8,128)(2,1)} %get-tuple-element.212.a_ref, bf16[1536,7680]{1,0:T(8,128)(2,1)} %get-tuple-element.213.w_ref), custom_call_target="tpu_custom_call" | custom-call | flops 1 | bytes 1 | tf_op jit(solution)/shard_map/cond/branch_1_fun/down_project/pallas_call | solution.py:408
  262.6 7.1 %gradient_send.7 = bf16[4,96,2048]{2,1,0:T(8,128)(2,1)} custom-call(s32[2]{0:T(128)S(1)} %pad_add_fusion.1.place_ref, bf16[4,2,96,768]{3,2,1,0:T(8,128)(2,1)} %get-tuple-element.220.refs_0_, bf16[768,2048]{1,0:T(8,128)(2,1)} %get-tuple-element.215.refs_1_, bf16[4,2,96,768]{3,2,1,0:T(8,128)(2,1)} %get-tuple-element.222.refs_2_, ...), custom_call_target="tpu_custom_call" | custom-call | flops 1 | bytes 1 | tf_op jit(solution)/shard_map/cond/branch_1_fun/gradient_send/pallas_call | solution.py:774
  269.7 6.2 %gradient_send.8 = bf16[4,96,2048]{2,1,0:T(8,128)(2,1)S(1)} custom-call(s32[2]{0:T(128)S(1)} %pad_add_fusion.1.place_ref, bf16[4,2,96,768]{3,2,1,0:T(8,128)(2,1)} %get-tuple-element.220.refs_0_, bf16[768,2048]{1,0:T(8,128)(2,1)} %get-tuple-element.221.refs_1_, bf16[4,2,96,768]{3,2,1,0:T(8,128)(2,1)} %get-tuple-element.222.refs_2_, ...), custom_call_target="tpu_custom_call" | custom-call | flops 1 | bytes 1 | tf_op jit(solution)/shard_map/cond/branch_1_fun/gradient_send/pallas_call | solution.py:774
  281.9 5.8 %collective-permute-done.38.refs_4_ = bf16[4,96,2048]{2,1,0:T(8,128)(2,1)} collective-permute-done((bf16[4,96,2048]{2,1,0:T(8,128)(2,1)}, bf16[4,96,2048]{2,1,0:T(8,128)(2,1)}, u32[]{:S(2)}, u32[]{:S(2)}) %collective-permute-start.38) | collective-permute-done | bytes 1572896 | tf_op jit(solution)/shard_map/ppermute | solution.py:651
  289.8 6.4 %gradient_chip.9 = bf16[4,96,2048]{2,1,0:T(8,128)(2,1)S(1)} custom-call(s32[2]{0:T(128)S(1)} %pad_add_fusion.6.place_ref, bf16[4,2,96,768]{3,2,1,0:T(8,128)(2,1)S(1)} %copy-done.14, bf16[768,2048]{1,0:T(8,128)(2,1)} %get-tuple-element.704.refs_1_, bf16[4,2,96,768]{3,2,1,0:T(8,128)(2,1)} %get-tuple-element.705.refs_2_, ...), custom_call_target="tpu_custom_call" | custom-call | flops 1 | bytes 1 | tf_op jit(solution)/shard_map/gradient_chip/pallas_call | solution.py:774
  301.7 9.0 %d_middle.1 = (bf16[768,1536]{1,0:T(8,128)(2,1)}, bf16[384,768]{1,0:T(8,128)(2,1)S(1)}, bf16[384,768]{1,0:T(8,128)(2,1)}) custom-call(bf16[768,1536]{1,0:T(8,128)(2,1)S(1)} %copy-done.7, bf16[768,1536]{1,0:T(8,128)(2,1)} %collective-permute-done.39.other_ref, f32[768,1536]{1,0:T(8,128)} %get-tuple-element.812.middle_ref, bf16[768,1536]{1,0:T(8,128)(2,1)} %bitcast.118, ...), custom_call_target="tpu_custom_call" | custom-call | flops 1 | bytes 1 | tf_op jit(solution)/shard_map/d_middle/pallas_call | solution.py:449
  310.7 19.4 %conditional.19 = (f32[2,2,96,768]{3,2,1,0:T(8,128)}, bf16[2,2,96,768]{3,2,1,0:T(8,128)(2,1)S(1)}, bf16[2,2,96,768]{3,2,1,0:T(8,128)(2,1)S(1)}) conditional(s32[]{:T(128)} %bitcast.14, () %tuple.213, (s32[6]{0:T(128)S(1)}, s32[4]{0:T(128)S(1)}, s32[1,768]{1,0:T(1,128)S(1)}, s32[1,768]{1,0:T(1,128)S(1)}, bf16[2,2,96,768]{3,2,1,0:T(8,128)(2,1)S(1)}, ...), branch_computations={%region_18.19_spmd, %region_19.20_spmd} | conditional | flops 2359297 | bytes 8257641 | solution.py:635
  310.7 15.9 %attention_backward.2 = (f32[2,2,96,768]{3,2,1,0:T(8,128)}, bf16[2,2,96,768]{3,2,1,0:T(8,128)(2,1)S(1)}, bf16[2,2,96,768]{3,2,1,0:T(8,128)(2,1)S(1)}, bf16[2,2,9...) custom-call(s32[6]{0:T(128)S(1)} %get-tuple-element.224.starts_ref, s32[4]{0:T(128)S(1)} %get-tuple-element.225.stripes_ref, ...), custom_call_target="tpu_custom_call" | custom-call | flops 1 | bytes 1 | tf_op jit(solution)/shard_map/cond/branch_1_fun/attention_backward/pallas_call | solution.py:217
  335.5 6.5 %gradient_chip.10 = bf16[4,96,2048]{2,1,0:T(8,128)(2,1)S(1)} custom-call(s32[2]{0:T(128)S(1)} %pad_add_fusion.6.place_ref, bf16[4,2,96,768]{3,2,1,0:T(8,128)(2,1)} %get-tuple-element.774.refs_0_, bf16[768,2048]{1,0:T(8,128)(2,1)} %get-tuple-element.741.refs_1_, bf16[4,2,96,768]{3,2,1,0:T(8,128)(2,1)} %get-tuple-element.776.refs_2_, ...), custom_call_target="tpu_custom_call" | custom-call | flops 1 | bytes 1 | tf_op jit(solution)/shard_map/gradient_chip/pallas_call | solution.py:774
  346.4 20.5 %conditional.20 = (f32[2,2,96,768]{3,2,1,0:T(8,128)}, bf16[2,2,96,768]{3,2,1,0:T(8,128)(2,1)S(1)}, bf16[2,2,96,768]{3,2,1,0:T(8,128)(2,1)}) conditional(s32[]{:T(128)} %bitcast.14, () %tuple.212, (s32[6]{0:T(128)}, s32[4]{0:T(128)}, s32[1,768]{1,0:T(1,128)}, s32[1,768]{1,0:T(1,128)S(1)}, bf16[2,2,96,768]{3,2,1,0:T(8,128)(2,1)}, ...), branch_computations={%region_20.21_spmd, %region_21.22_spmd} | conditional | flops 2359297 | bytes 8257641 | solution.py:635
  346.4 16.6 %attention_backward.3 = (f32[2,2,96,768]{3,2,1,0:T(8,128)}, bf16[2,2,96,768]{3,2,1,0:T(8,128)(2,1)S(1)}, bf16[2,2,96,768]{3,2,1,0:T(8,128)(2,1)S(1)}, bf16[2,2,9...) custom-call(s32[6]{0:T(128)} %get-tuple-element.241.starts_ref, s32[4]{0:T(128)} %get-tuple-element.242.stripes_ref, ...), custom_call_target="tpu_custom_call" | custom-call | flops 1 | bytes 1 | tf_op jit(solution)/shard_map/cond/branch_1_fun/attention_backward/pallas_call | solution.py:217
  368.7 11.3 %conditional.21 = (bf16[4,96,768]{2,1,0:T(8,128)(2,1)S(1)}, bf16[4,2,96,768]{3,2,1,0:T(8,128)(2,1)}, bf16[4,2,96,768]{3,2,1,0:T(8,128)(2,1)}) conditional(s32[]{:T(128)} %bitcast.14, () %tuple.188, (bf16[768,1536]{1,0:T(8,128)(2,1)}, s32[]{:T(128)}, bf16[768,768]{1,0:T(8,128)(2,1)}, bf16[768,768]{1,0:T(8,128)(2,1)}) %tuple.222), branch_computations={%region_22.23_spmd, %region_23.24_spmd} | conditional | flops 37 | bytes 4719009 | solution.py:635
  381.8 6.3 %gradient_chip.11 = bf16[4,96,2048]{2,1,0:T(8,128)(2,1)S(1)} custom-call(s32[2]{0:T(128)S(1)} %pad_add_fusion.6.place_ref, bf16[4,2,96,768]{3,2,1,0:T(8,128)(2,1)} %get-tuple-element.774.refs_0_, bf16[768,2048]{1,0:T(8,128)(2,1)} %get-tuple-element.775.refs_1_, bf16[4,2,96,768]{3,2,1,0:T(8,128)(2,1)} %get-tuple-element.776.refs_2_, ...), custom_call_target="tpu_custom_call" | custom-call | flops 1 | bytes 1 | tf_op jit(solution)/shard_map/gradient_chip/pallas_call | solution.py:774
  396.1 13.9 %conditional.22 = (bf16[768,1536]{1,0:T(8,128)(2,1)}, bf16[768,768]{1,0:T(8,128)(2,1)}, bf16[768,768]{1,0:T(8,128)(2,1)}, bf16[4,96,768]{2,1,0:T(8,128)(2,1)}) conditional(s32[]{:T(128)} %bitcast.14, () %tuple.187, (f32[2,2,96,768]{3,2,1,0:T(8,128)}, bf16[2,2,96,768]{3,2,1,0:T(8,128)(2,1)S(1)}, bf16[2,2,96,768]{3,2,1,0:T(8,128)(2,1)}, ...), branch_computations={%region_24.25_spmd, %region_25.26_spmd} | conditional | flops 3 | bytes 28311712 | solution.py:635
  402.5 7.5 %d_one.1 = bf16[768,1536]{1,0:T(8,128)(2,1)} custom-call(bf16[768,768]{1,0:T(8,128)(2,1)} %turn_back.2.refs_0_, bf16[768,768]{1,0:T(8,128)(2,1)} %turn_back.3.refs_1_, bf16[1536,1536]{1,0:T(8,128)(2,1)S(1)} %copy-done.9), custom_call_target="tpu_custom_call" | custom-call | flops 1 | bytes 1 | tf_op jit(solution)/shard_map/cond/branch_1_fun/d_one/pallas_call | solution.py:515
  413.0 44.8 %conditional.23 = (f32[96,768]{1,0:T(8,128)}, f32[96,768]{1,0:T(8,128)S(1)}, f32[96,768]{1,0:T(8,128)}, bf16[96,768]{1,0:T(8,128)(2,1)}, bf16[96,768]{1,0:T(8,12...) conditional(s32[]{:T(128)} %bitcast.14, () %tuple.173, (bf16[4,2,96,768]{3,2,1,0:T(8,128)(2,1)}, ...), branch_computations={%region_28.29_spmd, %region_29.30_spmd} | conditional | flops 6783018 | bytes 55149428 | solution.py:635
  470.4 5.7 %input_gradient.1 = bf16[768,1536]{1,0:T(8,128)(2,1)} custom-call(bf16[768,1536]{1,0:T(8,128)(2,1)} %get-tuple-element.821.mine_ref, bf16[768,1536]{1,0:T(8,128)(2,1)} %collective-permute-done.46.other_ref, bf16[768,1536]{1,0:T(8,128)(2,1)S(1)} %bitcast.116, bf16[768,1536]{1,0:T(8,128)(2,1)S(1)} %copy-done.12, f32[1,1536]{1,0:T(1,128)S(1)} %get-tuple-element.825.gain_ref), custom_call_target="tpu_custom_call" | custom-call | flops 1 | bytes 1 | tf_op jit(solution)/shard_map/input_gradient/pallas_call | solution.py:294
  (295 shorter events, 224.7 us)
Async XLA Ops:
  7.2 186.2 %all-gather.2.cloned.1.call-start = ((), (), s32[]{:S(2)}) async-start(), calls=%async_computation.3 | async-start | bytes 25067520 | tf_op jit(solution)/shard_map/all_gather | solution.py:884
  9.0 13.3 %collective-permute-start.27 = (bf16[112,1536]{1,0:T(8,128)(2,1)S(1)}, bf16[112,1536]{1,0:T(8,128)(2,1)}, u32[]{:S(2)}, u32[]{:S(2)}) collective-permute-start(bf16[112,1536]{1,0:T(8,128)(2,1)S(1)} %fusion.6), channel_id=1, source_target_pairs={{0,8},{8,16},{16,24},{24,0},{1,9},{9,17},{17,25},{25,1},{2,10},{10... | collective-permute-start | bytes 1032200 | tf_op jit(solution)/shard_map/ppermute | solution.py:656
  22.3 388.7 %reduce-scatter.6.cloned.1.call-start = ((), (), s32[]{:S(2)}) async-start(), calls=%async_computation.5 | async-start | bytes 1966080 | tf_op jit(solution)/shard_map/reduce_scatter | solution.py:815
  22.3 34.1 %collective-permute-start.29 = (bf16[112,1536]{1,0:T(8,128)(2,1)S(1)}, bf16[112,1536]{1,0:T(8,128)(2,1)}, u32[]{:S(2)}, u32[]{:S(2)}) collective-permute-start(bf16[112,1536]{1,0:T(8,128)(2,1)S(1)} %fusion.6), channel_id=1, source_target_pairs={{0,24},{8,0},{16,8},{24,16},{1,25},{9,1},{17,9},{25,17},{2,26},{10... | collective-permute-start | bytes 1032200 | tf_op jit(solution)/shard_map/ppermute | solution.py:656
  24.1 31.2 %collective-permute-start.28 = (bf16[112,1536]{1,0:T(8,128)(2,1)S(1)}, bf16[112,1536]{1,0:T(8,128)(2,1)}, u32[]{:S(2)}, u32[]{:S(2)}) collective-permute-start(bf16[112,1536]{1,0:T(8,128)(2,1)S(1)} %fusion.6), channel_id=1, source_target_pairs={{0,16},{8,24},{16,0},{24,8},{1,17},{9,25},{17,1},{25,9},{2,18},{10... | collective-permute-start | bytes 1032200 | tf_op jit(solution)/shard_map/ppermute | solution.py:656
  57.5 41.4 %collective-permute-start.31 = (bf16[3,96,1536]{2,1,0:T(8,128)(2,1)S(1)}, bf16[3,96,1536]{2,1,0:T(8,128)(2,1)S(1)}, u32[]{:S(2)}, u32[]{:S(2)}) collective-permute-start(bf16[3,96,1536]{2,1,0:T(8,128)(2,1)S(1)} %pad_maximum_fusion.2), channel_id=1, source_target_pairs={{0,2},{2,0},{4,6},{6,4},{1,3},{3,1},{5,7},{7,5},{8,10},{10,8},{12,... | collective-permute-start | bytes 2654216 | tf_op jit(solution)/shard_map/ppermute | solution.py:646
  57.6 41.3 %collective-permute-start.32 = (bf16[3,96,1536]{2,1,0:T(8,128)(2,1)S(1)}, bf16[3,96,1536]{2,1,0:T(8,128)(2,1)S(1)}, u32[]{:S(2)}, u32[]{:S(2)}) collective-permute-start(bf16[3,96,1536]{2,1,0:T(8,128)(2,1)S(1)} %pad_maximum_fusion.2), channel_id=1, source_target_pairs={{0,4},{2,6},{4,0},{6,2},{1,5},{3,7},{5,1},{7,3},{8,12},{10,14},{12... | collective-permute-start | bytes 2654216 | tf_op jit(solution)/shard_map/ppermute | solution.py:651
  105.6 29.1 %collective-permute-start.34 = (bf16[2,2,96,768]{3,2,1,0:T(8,128)(2,1)}, bf16[2,2,96,768]{3,2,1,0:T(8,128)(2,1)}, u32[]{:S(2)}, u32[]{:S(2)}) collective-permute-start(bf16[2,2,96,768]{3,2,1,0:T(8,128)(2,1)} %get-tuple-element.734), channel_id=1, source_target_pairs={{0,4},{2,6},{4,0},{6,2},{1,5},{3,7},{5,1},{7,3},{8,12},{10,14},{12... | collective-permute-start | bytes 1769480 | tf_op jit(solution)/shard_map/ppermute | solution.py:651
  111.3 48.3 %collective-permute-start.35 = (bf16[2,2,96,768]{3,2,1,0:T(8,128)(2,1)}, bf16[2,2,96,768]{3,2,1,0:T(8,128)(2,1)S(1)}, u32[]{:S(2)}, u32[]{:S(2)}) collective-permute-start(bf16[2,2,96,768]{3,2,1,0:T(8,128)(2,1)} %get-tuple-element.754), channel_id=1, source_target_pairs={{0,4},{2,6},{4,0},{6,2},{1,5},{3,7},{5,1},{7,3},{8,12},{10,14},{12... | collective-permute-start | bytes 1769480 | tf_op jit(solution)/shard_map/ppermute | solution.py:651
  159.6 19.1 %collective-permute-start.36 = (bf16[384,768]{1,0:T(8,128)(2,1)}, bf16[384,768]{1,0:T(8,128)(2,1)S(1)}, u32[]{:S(2)}, u32[]{:S(2)}) collective-permute-start(bf16[384,768]{1,0:T(8,128)(2,1)} %get-tuple-element.666.refs_0_), channel_id=1, source_target_pairs={{0,1},{1,0},{2,3},{3,2},{4,5},{5,4},{6,7},{7,6},{8,9},{9,8},{10,11... | collective-permute-start | bytes 1769480 | tf_op jit(solution)/shard_map/ppermute | solution.py:660
  177.8 15.6 %collective-permute-start.37 = (bf16[384,768]{1,0:T(8,128)(2,1)}, bf16[384,768]{1,0:T(8,128)(2,1)S(1)}, u32[]{:S(2)}, u32[]{:S(2)}) collective-permute-start(bf16[384,768]{1,0:T(8,128)(2,1)} %copy-done.13), channel_id=1, source_target_pairs={{0,1},{1,0},{2,3},{3,2},{4,5},{5,4},{6,7},{7,6},{8,9},{9,8},{10,11... | collective-permute-start | bytes 1769480 | tf_op jit(solution)/shard_map/ppermute | solution.py:660
  236.9 52.8 %collective-permute-start.39 = (bf16[768,1536]{1,0:T(8,128)(2,1)}, bf16[768,1536]{1,0:T(8,128)(2,1)}, u32[]{:S(2)}, u32[]{:S(2)}) collective-permute-start(bf16[768,1536]{1,0:T(8,128)(2,1)} %get-tuple-element.708.mine_ref), channel_id=1, source_target_pairs={{0,1},{1,0},{2,3},{3,2},{4,5},{5,4},{6,7},{7,6},{8,9},{9,8},{10,11... | collective-permute-start | bytes 7077896 | tf_op jit(solution)/shard_map/ppermute | solution.py:660
  250.9 36.8 %collective-permute-start.38 = (bf16[4,96,2048]{2,1,0:T(8,128)(2,1)}, bf16[4,96,2048]{2,1,0:T(8,128)(2,1)}, u32[]{:S(2)}, u32[]{:S(2)}) collective-permute-start(bf16[4,96,2048]{2,1,0:T(8,128)(2,1)} %get-tuple-element.682), channel_id=1, source_target_pairs={{0,4},{2,6},{4,0},{6,2},{1,5},{3,7},{5,1},{7,3},{8,12},{10,14},{12... | collective-permute-start | bytes 4718600 | tf_op jit(solution)/shard_map/ppermute | solution.py:651
  297.4 115.6 %reduce-scatter.4.cloned.1.call-start = ((), (), s32[]{:S(2)}) async-start(), calls=%async_computation.4 | async-start | bytes 1966080 | tf_op jit(solution)/shard_map/reduce_scatter | solution.py:815
  297.4 38.1 %collective-permute-start.40 = (bf16[4,96,2048]{2,1,0:T(8,128)(2,1)}, bf16[4,96,2048]{2,1,0:T(8,128)(2,1)}, u32[]{:S(2)}, u32[]{:S(2)}) collective-permute-start(bf16[4,96,2048]{2,1,0:T(8,128)(2,1)} %get-tuple-element.720), channel_id=1, source_target_pairs={{0,4},{2,6},{4,0},{6,2},{1,5},{3,7},{5,1},{7,3},{8,12},{10,14},{12... | collective-permute-start | bytes 4718600 | tf_op jit(solution)/shard_map/ppermute | solution.py:651
  299.9 44.3 %collective-permute-start.41 = (bf16[4,96,640]{2,1,0:T(8,128)(2,1)}, bf16[4,96,640]{2,1,0:T(8,128)(2,1)}, u32[]{:S(2)}, u32[]{:S(2)}) collective-permute-start(bf16[4,96,640]{2,1,0:T(8,128)(2,1)} %get-tuple-element.721), channel_id=1, source_target_pairs={{0,4},{2,6},{4,0},{6,2},{1,5},{3,7},{5,1},{7,3},{8,12},{10,14},{12... | collective-permute-start | bytes 1474568 | tf_op jit(solution)/shard_map/ppermute | solution.py:651
  344.2 119.7 %reduce-scatter.8.cloned.1.call-start = ((), (), s32[]{:S(2)}) async-start(), calls=%async_computation.6 | async-start | bytes 1966080 | tf_op jit(solution)/shard_map/reduce_scatter | solution.py:815
  344.3 51.8 %collective-permute-start.44 = (bf16[768,1536]{1,0:T(8,128)(2,1)}, bf16[768,1536]{1,0:T(8,128)(2,1)}, u32[]{:S(2)}, u32[]{:S(2)}) collective-permute-start(bf16[768,1536]{1,0:T(8,128)(2,1)} %get-tuple-element.813), channel_id=1, source_target_pairs={{0,1},{1,0},{2,3},{3,2},{4,5},{5,4},{6,7},{7,6},{8,9},{9,8},{10,11... | collective-permute-start | bytes 7077896 | tf_op jit(solution)/shard_map/ppermute | solution.py:660
  344.3 35.6 %collective-permute-start.45 = (bf16[4,96,1408]{2,1,0:T(8,128)(2,1)}, bf16[4,96,1408]{2,1,0:T(8,128)(2,1)}, u32[]{:S(2)}, u32[]{:S(2)}) collective-permute-start(bf16[4,96,1408]{2,1,0:T(8,128)(2,1)} %copy-done.33), channel_id=1, source_target_pairs={{0,4},{2,6},{4,0},{6,2},{1,5},{3,7},{5,1},{7,3},{8,12},{10,14},{12... | collective-permute-start | bytes 3244040 | tf_op jit(solution)/shard_map/ppermute | solution.py:651
  346.1 43.1 %collective-permute-start.42 = (bf16[2,2,96,768]{3,2,1,0:T(8,128)(2,1)}, bf16[2,2,96,768]{3,2,1,0:T(8,128)(2,1)}, u32[]{:S(2)}, u32[]{:S(2)}) collective-permute-start(bf16[2,2,96,768]{3,2,1,0:T(8,128)(2,1)} %copy-done.36), channel_id=1, source_target_pairs={{0,4},{2,6},{4,0},{6,2},{1,5},{3,7},{5,1},{7,3},{8,12},{10,14},{12... | collective-permute-start | bytes 1769480 | tf_op jit(solution)/shard_map/ppermute | solution.py:651
  366.9 27.1 %collective-permute-start.43 = (bf16[2,2,96,768]{3,2,1,0:T(8,128)(2,1)}, bf16[2,2,96,768]{3,2,1,0:T(8,128)(2,1)}, u32[]{:S(2)}, u32[]{:S(2)}) collective-permute-start(bf16[2,2,96,768]{3,2,1,0:T(8,128)(2,1)} %get-tuple-element.767), channel_id=1, source_target_pairs={{0,4},{2,6},{4,0},{6,2},{1,5},{3,7},{5,1},{7,3},{8,12},{10,14},{12... | collective-permute-start | bytes 1769480 | tf_op jit(solution)/shard_map/ppermute | solution.py:651
  396.2 13.8 %collective-permute-start.6 = (bf16[4,96,768]{2,1,0:T(8,128)(2,1)}, bf16[4,96,768]{2,1,0:T(8,128)(2,1)}, u32[]{:S(2)}, u32[]{:S(2)}) collective-permute-start(bf16[4,96,768]{2,1,0:T(8,128)(2,1)} %get-tuple-element.292), channel_id=1, source_target_pairs={{0,4},{2,6},{4,0},{6,2},{1,5},{3,7},{5,1},{7,3},{8,12},{10,14},{12... | collective-permute-start | bytes 1769480 | tf_op jit(solution)/shard_map/cond/branch_1_fun/ppermute | solution.py:651
  410.0 59.0 %collective-permute-start.46 = (bf16[768,1536]{1,0:T(8,128)(2,1)}, bf16[768,1536]{1,0:T(8,128)(2,1)}, u32[]{:S(2)}, u32[]{:S(2)}) collective-permute-start(bf16[768,1536]{1,0:T(8,128)(2,1)} %get-tuple-element.821.mine_ref), channel_id=1, source_target_pairs={{0,1},{1,0},{2,3},{3,2},{4,5},{5,4},{6,7},{7,6},{8,9},{9,8},{10,11... | collective-permute-start | bytes 7077896 | tf_op jit(solution)/shard_map/ppermute | solution.py:660
  421.9 17.9 %collective-permute-start.22 = (bf16[4,96,768]{2,1,0:T(8,128)(2,1)S(1)}, bf16[4,96,768]{2,1,0:T(8,128)(2,1)S(1)}, u32[]{:S(2)}, u32[]{:S(2)}) collective-permute-start(bf16[4,96,768]{2,1,0:T(8,128)(2,1)S(1)} %gradient_send.10), channel_id=1, source_target_pairs={{0,4},{2,6},{4,0},{6,2},{1,5},{3,7},{5,1},{7,3},{8,12},{10,14},{12... | collective-permute-start | bytes 1769480 | tf_op jit(solution)/shard_map/cond/branch_1_fun/ppermute | solution.py:651
  422.6 12.3 %collective-permute-start.19 = (bf16[96,768]{1,0:T(8,128)(2,1)}, bf16[96,768]{1,0:T(8,128)(2,1)S(1)}, u32[]{:S(2)}, u32[]{:S(2)}) collective-permute-start(bf16[96,768]{1,0:T(8,128)(2,1)} %get-tuple-element.317), channel_id=1, source_target_pairs={{0,8},{8,16},{16,24},{24,0},{1,9},{9,17},{17,25},{25,1},{2,10},{10... | collective-permute-start | bytes 442376 | tf_op jit(solution)/shard_map/cond/branch_1_fun/ppermute | solution.py:656
  422.6 14.9 %collective-permute-start.20 = (bf16[96,768]{1,0:T(8,128)(2,1)S(1)}, bf16[96,768]{1,0:T(8,128)(2,1)S(1)}, u32[]{:S(2)}, u32[]{:S(2)}) collective-permute-start(bf16[96,768]{1,0:T(8,128)(2,1)S(1)} %get-tuple-element.318), channel_id=1, source_target_pairs={{0,16},{8,24},{16,0},{24,8},{1,17},{9,25},{17,1},{25,9},{2,18},{10... | collective-permute-start | bytes 442376 | tf_op jit(solution)/shard_map/cond/branch_1_fun/ppermute | solution.py:656
  425.1 12.3 %collective-permute-start.21 = (bf16[96,768]{1,0:T(8,128)(2,1)S(1)}, bf16[96,768]{1,0:T(8,128)(2,1)S(1)}, u32[]{:S(2)}, u32[]{:S(2)}) collective-permute-start(bf16[96,768]{1,0:T(8,128)(2,1)S(1)} %get-tuple-element.319), channel_id=1, source_target_pairs={{0,24},{8,0},{16,8},{24,16},{1,25},{9,1},{17,9},{25,17},{2,26},{10... | collective-permute-start | bytes 442376 | tf_op jit(solution)/shard_map/cond/branch_1_fun/ppermute | solution.py:656
  438.3 14.7 %collective-permute-start.26 = (bf16[4,96,768]{2,1,0:T(8,128)(2,1)S(1)}, bf16[4,96,768]{2,1,0:T(8,128)(2,1)S(1)}, u32[]{:S(2)}, u32[]{:S(2)}) collective-permute-start(bf16[4,96,768]{2,1,0:T(8,128)(2,1)S(1)} %gradient_send.11), channel_id=1, source_target_pairs={{0,4},{2,6},{4,0},{6,2},{1,5},{3,7},{5,1},{7,3},{8,12},{10,14},{12... | collective-permute-start | bytes 1769480 | tf_op jit(solution)/shard_map/cond/branch_1_fun/ppermute | solution.py:651
  443.3 14.1 %collective-permute-start.23 = (bf16[96,768]{1,0:T(8,128)(2,1)S(1)}, bf16[96,768]{1,0:T(8,128)(2,1)S(1)}, u32[]{:S(2)}, u32[]{:S(2)}) collective-permute-start(bf16[96,768]{1,0:T(8,128)(2,1)S(1)} %get-tuple-element.341), channel_id=1, source_target_pairs={{0,8},{8,16},{16,24},{24,0},{1,9},{9,17},{17,25},{25,1},{2,10},{10... | collective-permute-start | bytes 442376 | tf_op jit(solution)/shard_map/cond/branch_1_fun/ppermute | solution.py:656
  457.8 18.4 %collective-permute-start.47 = (bf16[96,768]{1,0:T(8,128)(2,1)}, bf16[96,768]{1,0:T(8,128)(2,1)}, u32[]{:S(2)}, u32[]{:S(2)}) collective-permute-start(bf16[96,768]{1,0:T(8,128)(2,1)} %get-tuple-element.828), channel_id=1, source_target_pairs={{0,8},{8,16},{16,24},{24,0},{1,9},{9,17},{17,25},{25,1},{2,10},{10... | collective-permute-start | bytes 442376 | tf_op jit(solution)/shard_map/ppermute | solution.py:656
  461.5 14.7 %collective-permute-start.48 = (bf16[96,768]{1,0:T(8,128)(2,1)}, bf16[96,768]{1,0:T(8,128)(2,1)}, u32[]{:S(2)}, u32[]{:S(2)}) collective-permute-start(bf16[96,768]{1,0:T(8,128)(2,1)} %get-tuple-element.829), channel_id=1, source_target_pairs={{0,16},{8,24},{16,0},{24,8},{1,17},{9,25},{17,1},{25,9},{2,18},{10... | collective-permute-start | bytes 442376 | tf_op jit(solution)/shard_map/ppermute | solution.py:656
  463.0 13.2 %collective-permute-start.49 = (bf16[96,768]{1,0:T(8,128)(2,1)}, bf16[96,768]{1,0:T(8,128)(2,1)}, u32[]{:S(2)}, u32[]{:S(2)}) collective-permute-start(bf16[96,768]{1,0:T(8,128)(2,1)} %get-tuple-element.830), channel_id=1, source_target_pairs={{0,24},{8,0},{16,8},{24,16},{1,25},{9,1},{17,9},{25,17},{2,26},{10... | collective-permute-start | bytes 442376 | tf_op jit(solution)/shard_map/ppermute | solution.py:656
  (71 other events, 599.0 us)
Sparse Core Ops, SparseCore 0:
  22.4 164.5 all-gather.1
  297.5 33.4 reduce-scatter.5
  344.3 32.8 reduce-scatter.3
  396.2 32.9 reduce-scatter.7
